TPU v7x, 32 devices: a whole 2x2x4 slice. The times are simulated.
32 devices in a mesh: row: 8 (over z, x), col: 4 (over y, core).
Axes of the slice: x: 2, y: 2, z: 4, core: 2. Of those that a mesh axis runs over, the one named last changes fastest.
Arguments:
- features: bfloat16 [96, 128, 1024], P(None, 'row', 'col'), may hold values from -6 to 6
- teacher: bfloat16 [1536, 128, 1024], P(None, 'row', 'col'), may hold values from -6 to 6
- conv_in: bfloat16 [9, 96, 96], replicated, may hold values from -0.21875 to 0.21875
- conv_out: bfloat16 [9, 96, 96], replicated, may hold values from -0.21875 to 0.21875
- projector: bfloat16 [96, 1536], replicated, may hold values from -0.625 to 0.625
Outputs:
- grad_conv_in: float32 [9, 96, 96], replicated
- grad_conv_out: float32 [9, 96, 96], replicated
- grad_projector: float32 [96, 1536], replicated
All inputs are finite; a program needn't handle non-finite values.
Results may differ from a plain program's by a relative error of at most 0.0003.
Values may be sent and summed in bfloat16 or wider, within the bound.
No kernel may reach another device: no remote copies, remote signals or barrier semaphores. Data moves between devices by JAX's collectives and lax.ppermute only.
A program may use at most 128 MiB of HBM per device.

v0:
```python
import jax
import jax.numpy as jnp
from jax import lax
from jax.sharding import PartitionSpec as P


def padded_2(cells, sides, width):
    for axis, dim in sides:
        count = lax.axis_size(axis)
        ends = count - 1
        head = lax.slice_in_dim(cells, 0, width, axis=dim)
        tail = lax.slice_in_dim(cells, cells.shape[dim] - width, cells.shape[dim], axis=dim)
        cells = jnp.concatenate(
            [
                lax.ppermute(tail, axis, [(i, (i + 1) % count) for i in range(ends)]),
                cells,
                lax.ppermute(head, axis, [((i + 1) % count, i) for i in range(ends)]),
            ],
            axis=dim,
        )
    return cells


def gelu_grad(value):
    cdf = 0.5 * (1.0 + jax.scipy.special.erf(value * 0.7071067811865476))
    dens = jnp.exp(-0.5 * value * value) * 0.3989422804014327
    return cdf + value * dens


def tap_stack(padded, height, width):
    return jnp.concatenate(
        [padded[:, tap // 3 : tap // 3 + height, tap % 3 : tap % 3 + width] for tap in range(9)], 0
    )


def flip_stack(padded, height, width):
    return jnp.concatenate(
        [
            padded[:, 2 - tap // 3 : 2 - tap // 3 + height, 2 - tap % 3 : 2 - tap % 3 + width]
            for tap in range(9)
        ],
        0,
    )


def shards(features, teacher, conv_in, conv_out, projector):
    chans, height, width = features.shape
    flat_in = conv_in.reshape(9 * chans, chans)
    flat_out = conv_out.reshape(9 * chans, chans)
    xpad = padded_2(features, (("row", 1), ("col", 2)), 1)
    x_taps = tap_stack(xpad, height, width)
    pre = jnp.einsum("ko,khw->ohw", flat_in, x_taps, preferred_element_type=jnp.float32)
    hidden = jax.nn.gelu(pre, approximate=False).astype(jnp.bfloat16)
    gpad = padded_2(hidden, (("row", 1), ("col", 2)), 1)
    g_taps = tap_stack(gpad, height, width)
    branch = jnp.einsum("ko,khw->ohw", flat_out, g_taps, preferred_element_type=jnp.float32)
    student = (features.astype(jnp.float32) + branch).astype(jnp.bfloat16)
    pred = jnp.einsum("ce,chw->ehw", projector, student, preferred_element_type=jnp.float32)
    npix = height * width * lax.axis_size("row") * lax.axis_size("col")
    dpred = ((pred - teacher.astype(jnp.float32)) / npix).astype(jnp.bfloat16)
    grad_proj = jnp.einsum("chw,ehw->ce", student, dpred, preferred_element_type=jnp.float32)
    dstudent = jnp.einsum(
        "ce,ehw->chw", projector, dpred, preferred_element_type=jnp.float32
    ).astype(jnp.bfloat16)
    spad = padded_2(dstudent, (("row", 1), ("col", 2)), 1)
    back_matrix = jnp.transpose(conv_out, (0, 2, 1)).reshape(9 * chans, chans)
    dhidden = jnp.einsum(
        "kc,khw->chw",
        back_matrix,
        flip_stack(spad, height, width),
        preferred_element_type=jnp.float32,
    )
    dpre = (dhidden * gelu_grad(pre)).astype(jnp.bfloat16)
    grad_out = jnp.einsum(
        "khw,ohw->ko", g_taps, dstudent, preferred_element_type=jnp.float32
    ).reshape(9, chans, chans)
    grad_in = jnp.einsum("khw,ohw->ko", x_taps, dpre, preferred_element_type=jnp.float32).reshape(
        9, chans, chans
    )
    result = lax.psum((grad_in, grad_out, grad_proj), ("row", "col"))
    return (result[0], result[1], result[2])


def solution(mesh):
    in_specs = (P(None, "row", "col"), P(None, "row", "col"), P(), P(), P())
    out_specs = (P(), P(), P())
    return jax.shard_map(shards, mesh=mesh, in_specs=in_specs, out_specs=out_specs, check_vma=False)
```

profile of v0, /device:TPU:0, one launch (start us, length us, event | category | flops | bytes accessed | tf_op | source)
XLA Modules:
  0.0 279.3 jit_solution(7217253193164067277)
XLA Ops:
  8.7 4.8 %collective-permute-start = (bf16[96,1,256]{2,0,1:T(8,128)(2,1)S(1)}, bf16[96,1,256]{2,0,1:T(8,128)(2,1)S(1)}, u32[]{:S(2)}, u32[]{:S(2)}) collective-permute-start(bf16[96,1,256]{2,0,1:T(8,128)(2,1)S(1)} %get-tuple-element.21), channel_id=1, source_target_pairs={{0,4},{4,8},{8,12},{12,16},{16,20},{20,24},{24,28},{1,5},{5,9},{9,... | collective-permute-start | bytes 147464 | tf_op jit(solution)/shard_map/ppermute | solution.py:15
  15.6 4.0 %collective-permute-done.1 = bf16[96,1,256]{2,0,1:T(8,128)(2,1)S(1)} collective-permute-done((bf16[96,1,256]{2,0,1:T(8,128)(2,1)S(1)}, bf16[96,1,256]{2,0,1:T(8,128)(2,1)S(1)}, u32[]{:S(2)}, u32[]{:S(2)}) %collective-permute-start.1) | collective-permute-done | bytes 49184 | tf_op jit(solution)/shard_map/ppermute | solution.py:17
  22.9 3.6 %collective-permute-done.3 = bf16[96,18,1]{2,0,1:T(8,128)(2,1)S(1)} collective-permute-done((bf16[96,18,1]{2,0,1:T(8,128)(2,1)S(1)}, bf16[96,18,1]{2,0,1:T(8,128)(2,1)S(1)}, u32[]{:S(2)}, u32[]{:S(2)}) %collective-permute-start.3) | collective-permute-done | bytes 3488 | tf_op jit(solution)/shard_map/ppermute | solution.py:17
  29.4 5.5 %fusion.4 = (bf16[96,16,256]{2,0,1:T(8,128)(2,1)S(1)}, f32[16,256,96]{1,2,0:T(8,128)}) fusion(bf16[864,16,256]{2,0,1:T(8,128)(2,1)S(1)} %fusion.39, bf16[864,96,1]{1,0,2:T(8,128)(2,1)S(1)} %bitcast.108), kind=kOutput, calls=%fused_computation.12 | convolution fusion | flops 705036288 | bytes 9603072 | tf_op jit(solution)/shard_map/ko,khw->ohw/dot_general | solution.py:52
  34.9 4.4 %collective-permute-start.4 = (bf16[96,1,256]{2,0,1:T(8,128)(2,1)S(1)}, bf16[96,1,256]{2,0,1:T(8,128)(2,1)S(1)}, u32[]{:S(2)}, u32[]{:S(2)}) collective-permute-start(bf16[96,1,256]{2,0,1:T(8,128)(2,1)S(1)} %get-tuple-element.18), channel_id=1, source_target_pairs={{0,4},{4,8},{8,12},{12,16},{16,20},{20,24},{24,28},{1,5},{5,9},{9,... | collective-permute-start | bytes 147464 | tf_op jit(solution)/shard_map/ppermute | solution.py:15
  41.0 4.3 %collective-permute-done.5 = bf16[96,1,256]{2,0,1:T(8,128)(2,1)S(1)} collective-permute-done((bf16[96,1,256]{2,0,1:T(8,128)(2,1)S(1)}, bf16[96,1,256]{2,0,1:T(8,128)(2,1)S(1)}, u32[]{:S(2)}, u32[]{:S(2)}) %collective-permute-start.5) | collective-permute-done | bytes 49184 | tf_op jit(solution)/shard_map/ppermute | solution.py:17
  46.3 6.9 %collective-permute-start.6 = (bf16[96,18,1]{2,0,1:T(8,128)(2,1)}, bf16[96,18,1]{2,0,1:T(8,128)(2,1)S(1)}, u32[]{:S(2)}, u32[]{:S(2)}) collective-permute-start(bf16[96,18,1]{2,0,1:T(8,128)(2,1)} %get-tuple-element.13), channel_id=1, source_target_pairs={{0,1},{1,2},{2,3},{4,5},{5,6},{6,7},{8,9},{9,10},{10,11},{12,13},{... | collective-permute-start | bytes 10376 | tf_op jit(solution)/shard_map/ppermute | solution.py:15
  53.3 1.6 collective-permute-start.7
  54.9 16.6 %copy.31 = bf16[1536,16,256]{0,2,1:T(8,128)(2,1)} copy(bf16[1536,16,256]{2,1,0:T(8,128)(2,1)} %param.6) | data formatting | bytes 25165824 | tf_op args[1]
  74.9 2.9 %copy-done.2 = bf16[864,16,256]{2,0,1:T(8,128)(2,1)} copy-done((bf16[864,16,256]{2,0,1:T(8,128)(2,1)}, bf16[864,16,256]{2,0,1:T(8,128)(2,1)S(1)}, u32[]{:S(2)}) %copy-start.2) | copy-done | bytes 7077912
  77.8 1.5 fusion.11
  79.4 9.2 %fusion.1 = bf16[1536,16,256]{0,2,1:T(8,128)(2,1)} fusion(bf16[1536,16,256]{0,2,1:T(8,128)(2,1)} %copy.31, bf16[96,16,256]{2,0,1:T(8,128)(2,1)S(1)} %fusion.11, bf16[96,1536]{1,0:T(8,128)(2,1)S(1)} %copy-done), kind=kOutput, calls=%fused_computation.2 | convolution fusion | flops 1233125376 | bytes 26247168 | tf_op jit(solution)/shard_map/ce,chw->ehw/dot_general | solution.py:58
  88.6 8.6 %fusion.26 = bf16[96,16,256]{2,0,1:T(8,128)(2,1)S(1)} fusion(bf16[1536,16,256]{0,2,1:T(8,128)(2,1)} %fusion.1, bf16[96,1536]{1,0:T(8,128)(2,1)S(1)} %copy-done), kind=kOutput, calls=%fused_computation.53 | convolution fusion | flops 1208352768 | bytes 13664256 | tf_op jit(solution)/shard_map/ce,ehw->chw/dot_general | solution.py:62
  97.2 3.4 %collective-permute-start.8 = (bf16[96,1,256]{2,0,1:T(8,128)(2,1)S(1)}, bf16[96,1,256]{2,0,1:T(8,128)(2,1)S(1)}, u32[]{:S(2)}, u32[]{:S(2)}) collective-permute-start(bf16[96,1,256]{2,0,1:T(8,128)(2,1)S(1)} %get-tuple-element.16), channel_id=1, source_target_pairs={{0,4},{4,8},{8,12},{12,16},{16,20},{20,24},{24,28},{1,5},{5,9},{9,... | collective-permute-start | bytes 147464 | tf_op jit(solution)/shard_map/ppermute | solution.py:15
  100.6 1.6 collective-permute-start.9
  102.2 2.9 %convolution_bitcast_fusion = f32[96,1536]{1,0:T(8,128)} fusion(bf16[96,16,256]{2,0,1:T(8,128)(2,1)S(1)} %fusion.11, bf16[1536,16,256]{0,2,1:T(8,128)(2,1)S(1)} %copy-done.1), kind=kOutput, calls=%fused_computation.3 | convolution fusion | flops 1207959552 | bytes 13959168 | tf_op jit(solution)/shard_map/chw,ehw->ce/dot_general | solution.py:61
  105.1 1.9 collective-permute-done.9
  108.6 3.3 %collective-permute-start.11 = (bf16[96,18,1]{2,0,1:T(8,128)(2,1)S(1)}, bf16[96,18,1]{2,0,1:T(8,128)(2,1)S(1)}, u32[]{:S(2)}, u32[]{:S(2)}) collective-permute-start(bf16[96,18,1]{2,0,1:T(8,128)(2,1)S(1)} %get-tuple-element.8), channel_id=1, source_target_pairs={{0,1},{1,2},{2,3},{4,5},{5,6},{6,7},{8,9},{9,10},{10,11},{12,13},{... | collective-permute-start | bytes 10376 | tf_op jit(solution)/shard_map/ppermute | solution.py:15
  112.0 2.7 fusion.57
  117.2 2.9 %copy-done.8 = bf16[864,16,256]{2,0,1:T(8,128)(2,1)} copy-done((bf16[864,16,256]{2,0,1:T(8,128)(2,1)}, bf16[864,16,256]{2,0,1:T(8,128)(2,1)S(1)}, u32[]{:S(2)}) %copy-start.8) | copy-done | bytes 7077912
  120.1 9.2 %fusion.43 = f32[864,96,1]{1,0,2:T(8,128)} fusion(bf16[864,16,256]{2,0,1:T(8,128)(2,1)} %copy-done.7, f32[16,256,96]{1,2,0:T(8,128)S(1)} %copy-done.10, bf16[864,16,256]{2,0,1:T(8,128)(2,1)} %copy-done.8, bf16[864,96,1]{1,0,2:T(8,128)(2,1)S(1)} %bitcast.107), kind=kOutput, calls=%fused_computation.92 | convolution fusion | flops 1362886656 | bytes 16226304 | tf_op jit(solution)/shard_map/khw,ohw->ko/dot_general | solution.py:77
  129.3 138.7 %all-reduce.3.cloned.1.call-done = (f32[9,96,96]{2,1,0:T(8,128)}, f32[9,96,96]{2,1,0:T(8,128)}, f32[96,1536]{1,0:T(8,128)}) async-done(((f32[9,96,96]{2,1,0:T(8,128)}, f32[9,96,96]{2,1,0:T(8,128)}, f32[96,1536]{1,0:T(8,128)}), (f32[9,96,96]{2,1,0:T(8,128)}, f32[9,96,96]{2,1,0:T(8,128)}, f32[96,1536]{1,0:T(8,128)})) %all-reduce.3.cloned.1.call-update) | async-done | bytes 1253392 | tf_op jit(solution)/shard_map/psum | solution.py:80
  268.0 1.9 copy.79
  269.9 1.8 copy.80
  (83 shorter events, 20.7 us)
Async XLA Ops:
  7.2 72.2 %copy-start = (bf16[96,1536]{1,0:T(8,128)(2,1)S(1)}, bf16[96,1536]{1,0:T(8,128)(2,1)}, u32[]{:S(2)}) copy-start(bf16[96,1536]{1,0:T(8,128)(2,1)} %param.9) | copy-start | bytes 884740
  7.2 8.1 %copy-start.3 = (bf16[96,16,256]{2,1,0:T(8,128)(2,1)S(1)}, bf16[96,16,256]{2,1,0:T(8,128)(2,1)}, u32[]{:S(2)}) copy-start(bf16[96,16,256]{2,1,0:T(8,128)(2,1)} %param.5) | copy-start | bytes 2359300
  7.2 260.8 %all-reduce.3.cloned.1.call-start = ((), (), s32[]{:S(2)}) async-start(), calls=%async_computation | async-start | bytes 2949120 | tf_op jit(solution)/shard_map/psum | solution.py:80
  8.7 6.6 %collective-permute-start = (bf16[96,1,256]{2,0,1:T(8,128)(2,1)S(1)}, bf16[96,1,256]{2,0,1:T(8,128)(2,1)S(1)}, u32[]{:S(2)}, u32[]{:S(2)}) collective-permute-start(bf16[96,1,256]{2,0,1:T(8,128)(2,1)S(1)} %get-tuple-element.21), channel_id=1, source_target_pairs={{0,4},{4,8},{8,12},{12,16},{16,20},{20,24},{24,28},{1,5},{5,9},{9,... | collective-permute-start | bytes 147464 | tf_op jit(solution)/shard_map/ppermute | solution.py:15
  13.6 6.0 %collective-permute-start.1 = (bf16[96,1,256]{2,0,1:T(8,128)(2,1)S(1)}, bf16[96,1,256]{2,0,1:T(8,128)(2,1)S(1)}, u32[]{:S(2)}, u32[]{:S(2)}) collective-permute-start(bf16[96,1,256]{2,0,1:T(8,128)(2,1)S(1)} %get-tuple-element.20), channel_id=1, source_target_pairs={{4,0},{8,4},{12,8},{16,12},{20,16},{24,20},{28,24},{5,1},{9,5},{13... | collective-permute-start | bytes 147464 | tf_op jit(solution)/shard_map/ppermute | solution.py:17
  19.8 2.7 collective-permute-start.2
  21.1 5.4 %collective-permute-start.3 = (bf16[96,18,1]{2,0,1:T(8,128)(2,1)S(1)}, bf16[96,18,1]{2,0,1:T(8,128)(2,1)S(1)}, u32[]{:S(2)}, u32[]{:S(2)}) collective-permute-start(bf16[96,18,1]{2,0,1:T(8,128)(2,1)S(1)} %get-tuple-element.14), channel_id=1, source_target_pairs={{1,0},{2,1},{3,2},{5,4},{6,5},{7,6},{9,8},{10,9},{11,10},{13,12},{... | collective-permute-start | bytes 10376 | tf_op jit(solution)/shard_map/ppermute | solution.py:17
  28.9 6.0 %copy-start.7 = (bf16[864,16,256]{2,0,1:T(8,128)(2,1)}, bf16[864,16,256]{2,0,1:T(8,128)(2,1)S(1)}, u32[]{:S(2)}) copy-start(bf16[864,16,256]{2,0,1:T(8,128)(2,1)S(1)} %fusion.39) | copy-start | bytes 21233668
  34.9 6.1 %collective-permute-start.4 = (bf16[96,1,256]{2,0,1:T(8,128)(2,1)S(1)}, bf16[96,1,256]{2,0,1:T(8,128)(2,1)S(1)}, u32[]{:S(2)}, u32[]{:S(2)}) collective-permute-start(bf16[96,1,256]{2,0,1:T(8,128)(2,1)S(1)} %get-tuple-element.18), channel_id=1, source_target_pairs={{0,4},{4,8},{8,12},{12,16},{16,20},{20,24},{24,28},{1,5},{5,9},{9,... | collective-permute-start | bytes 147464 | tf_op jit(solution)/shard_map/ppermute | solution.py:15
  39.3 6.0 %collective-permute-start.5 = (bf16[96,1,256]{2,0,1:T(8,128)(2,1)S(1)}, bf16[96,1,256]{2,0,1:T(8,128)(2,1)S(1)}, u32[]{:S(2)}, u32[]{:S(2)}) collective-permute-start(bf16[96,1,256]{2,0,1:T(8,128)(2,1)S(1)} %get-tuple-element.19), channel_id=1, source_target_pairs={{4,0},{8,4},{12,8},{16,12},{20,16},{24,20},{28,24},{5,1},{9,5},{13... | collective-permute-start | bytes 147464 | tf_op jit(solution)/shard_map/ppermute | solution.py:17
  46.3 26.0 %collective-permute-start.6 = (bf16[96,18,1]{2,0,1:T(8,128)(2,1)}, bf16[96,18,1]{2,0,1:T(8,128)(2,1)S(1)}, u32[]{:S(2)}, u32[]{:S(2)}) collective-permute-start(bf16[96,18,1]{2,0,1:T(8,128)(2,1)} %get-tuple-element.13), channel_id=1, source_target_pairs={{0,1},{1,2},{2,3},{4,5},{5,6},{6,7},{8,9},{9,10},{10,11},{12,13},{... | collective-permute-start | bytes 10376 | tf_op jit(solution)/shard_map/ppermute | solution.py:15
  53.3 18.3 %copy-start.4 = (bf16[9,96,96]{2,1,0:T(8,128)(2,1)S(1)}, bf16[9,96,96]{2,1,0:T(8,128)(2,1)}, u32[]{:S(2)}) copy-start(bf16[9,96,96]{2,1,0:T(8,128)(2,1)} %param.8) | copy-start | bytes 497668
  53.3 19.1 %collective-permute-start.7 = (bf16[96,18,1]{2,0,1:T(8,128)(2,1)S(1)}, bf16[96,18,1]{2,0,1:T(8,128)(2,1)S(1)}, u32[]{:S(2)}, u32[]{:S(2)}) collective-permute-start(bf16[96,18,1]{2,0,1:T(8,128)(2,1)S(1)} %get-tuple-element.12), channel_id=1, source_target_pairs={{1,0},{2,1},{3,2},{5,4},{6,5},{7,6},{9,8},{10,9},{11,10},{13,12},{... | collective-permute-start | bytes 10376 | tf_op jit(solution)/shard_map/ppermute | solution.py:17
  74.9 2.9 %copy-start.2 = (bf16[864,16,256]{2,0,1:T(8,128)(2,1)}, bf16[864,16,256]{2,0,1:T(8,128)(2,1)S(1)}, u32[]{:S(2)}) copy-start(bf16[864,16,256]{2,0,1:T(8,128)(2,1)S(1)} %slice_dynamic-update-slice_fusion.6) | copy-start | bytes 21233668
  88.6 13.6 %copy-start.1 = (bf16[1536,16,256]{0,2,1:T(8,128)(2,1)S(1)}, bf16[1536,16,256]{0,2,1:T(8,128)(2,1)}, u32[]{:S(2)}) copy-start(bf16[1536,16,256]{0,2,1:T(8,128)(2,1)} %fusion.1) | copy-start | bytes 37748740
  97.2 7.9 %collective-permute-start.8 = (bf16[96,1,256]{2,0,1:T(8,128)(2,1)S(1)}, bf16[96,1,256]{2,0,1:T(8,128)(2,1)S(1)}, u32[]{:S(2)}, u32[]{:S(2)}) collective-permute-start(bf16[96,1,256]{2,0,1:T(8,128)(2,1)S(1)} %get-tuple-element.16), channel_id=1, source_target_pairs={{0,4},{4,8},{8,12},{12,16},{16,20},{20,24},{24,28},{1,5},{5,9},{9,... | collective-permute-start | bytes 147464 | tf_op jit(solution)/shard_map/ppermute | solution.py:15
  100.6 11.3 %slice-start = ((s8[7077888]{0:T(1024)(128)(4,1)}), s8[4194304]{0:T(1024)(128)(4,1)S(1)}, s32[]{:S(2)}) async-start(s8[7077888]{0:T(1024)(128)(4,1)} %bitcast.101), calls=%async_computation.1 | async-start | bytes 8388608
  100.6 11.3 %slice-start.1 = ((s8[7077888]{0:T(1024)(128)(4,1)}), s8[2883584]{0:T(1024)(128)(4,1)S(1)}, s32[]{:S(2)}) async-start(s8[7077888]{0:T(1024)(128)(4,1)} %bitcast.101), calls=%async_computation.2 | async-start | bytes 5767168
  100.6 6.4 %collective-permute-start.9 = (bf16[96,1,256]{2,0,1:T(8,128)(2,1)S(1)}, bf16[96,1,256]{2,0,1:T(8,128)(2,1)S(1)}, u32[]{:S(2)}, u32[]{:S(2)}) collective-permute-start(bf16[96,1,256]{2,0,1:T(8,128)(2,1)S(1)} %get-tuple-element.17), channel_id=1, source_target_pairs={{4,0},{8,4},{12,8},{16,12},{20,16},{24,20},{28,24},{5,1},{9,5},{13... | collective-permute-start | bytes 147464 | tf_op jit(solution)/shard_map/ppermute | solution.py:17
  107.3 7.4 %collective-permute-start.10 = (bf16[96,18,1]{2,0,1:T(8,128)(2,1)S(1)}, bf16[96,18,1]{2,0,1:T(8,128)(2,1)S(1)}, u32[]{:S(2)}, u32[]{:S(2)}) collective-permute-start(bf16[96,18,1]{2,0,1:T(8,128)(2,1)S(1)} %get-tuple-element.9), channel_id=1, source_target_pairs={{1,0},{2,1},{3,2},{5,4},{6,5},{7,6},{9,8},{10,9},{11,10},{13,12},{... | collective-permute-start | bytes 10376 | tf_op jit(solution)/shard_map/ppermute | solution.py:17
  108.6 6.1 %collective-permute-start.11 = (bf16[96,18,1]{2,0,1:T(8,128)(2,1)S(1)}, bf16[96,18,1]{2,0,1:T(8,128)(2,1)S(1)}, u32[]{:S(2)}, u32[]{:S(2)}) collective-permute-start(bf16[96,18,1]{2,0,1:T(8,128)(2,1)S(1)} %get-tuple-element.8), channel_id=1, source_target_pairs={{0,1},{1,2},{2,3},{4,5},{5,6},{6,7},{8,9},{9,10},{10,11},{12,13},{... | collective-permute-start | bytes 10376 | tf_op jit(solution)/shard_map/ppermute | solution.py:15
  117.1 3.0 %copy-start.6 = (bf16[9,96,96]{2,1,0:T(8,128)(2,1)S(1)}, bf16[9,96,96]{2,1,0:T(8,128)(2,1)}, u32[]{:S(2)}) copy-start(bf16[9,96,96]{2,1,0:T(8,128)(2,1)} %copy.33) | copy-start | bytes 497668
  117.1 3.0 %copy-start.10 = (f32[16,256,96]{1,2,0:T(8,128)S(1)}, f32[16,256,96]{1,2,0:T(8,128)}, u32[]{:S(2)}) copy-start(f32[16,256,96]{1,2,0:T(8,128)} %get-tuple-element.23) | copy-start | bytes 4718596
  268.0 3.7 %copy-start.5 = (f32[96,1536]{1,0:T(8,128)S(1)}, f32[96,1536]{1,0:T(8,128)}, u32[]{:S(2)}) copy-start(f32[96,1536]{1,0:T(8,128)} %get-tuple-element.26) | copy-start | bytes 1769476
  (2 other events, 3.8 us)
Sparse Core Ops, SparseCore 0:
  129.4 138.5 all-reduce.2
where the time goes:
time: 280 us; the launch traced here: 279 us
  waiting for transfers between devices  153 us (55%)
  matrix products  39.7 us (14%)
  local copies, waits for them, and re-layouts  34.2 us (12%)
  starting transfers between devices  32.5 us (12%)
  between operations  14.5 us (5%)
  other arithmetic  5.01 us (2%)
    psum x1, waiting for transfers between devices, shards(): result = lax.psum((grad_in, grad_out, grad_proj), ('row', 'col'))  139 us
    unnamed x46, local copies, waits for them, and re-layouts  31.5 us
    ppermute x6, starting transfers between devices, padded_2(): lax.ppermute(tail, axis, [(i, (i + 1) % count) for i in range(ends)])  24.1 us
    ppermute x6, waiting for transfers between devices, padded_2(): lax.ppermute(head, axis, [((i + 1) % count, i) for i in range(ends)])  13.7 us
    dot_general x1, matrix products, shards(): jnp.einsum('khw,ohw->ko', x_taps, dpre, preferred_element_type=jnp.float32)  9.17 us
    dot_general x1, matrix products, shards(): jnp.einsum('ce,chw->ehw', projector, student, preferred_element_type=jnp....  9.17 us
    dot_general x1, matrix products, shards(): jnp.einsum('ce,ehw->chw', projector, dpred, preferred_element_type=jnp.fl...  8.61 us
    ppermute x6, starting transfers between devices, padded_2(): lax.ppermute(head, axis, [((i + 1) % count, i) for i in range(ends)])  8.33 us
  transfers between devices with their start and end apart: 13, of which 8 were waited for; matrix products, arithmetic and copies ran while one was open for 9% of the time, Pallas kernels for 0%

commit v1 on v0

v1 whole, which is shorter than its diff:
```python
import jax
import jax.numpy as jnp
from jax import lax
from jax.experimental import pallas as pl
from jax.experimental.pallas import tpu as pltpu
from jax.sharding import PartitionSpec as P

F32 = jnp.float32
BF16 = jnp.bfloat16
PITCH = 5


def dot(a, b):
    return jnp.dot(a, b, preferred_element_type=F32)


def dot_nt(a, b):
    return lax.dot_general(a, b, (((1,), (1,)), ((), ())), preferred_element_type=F32)


def split(v):
    hi = v.astype(BF16)
    return hi, (v - hi.astype(F32)).astype(BF16)


def lanes_of(shape):
    return lax.broadcasted_iota(jnp.int32, shape, 1)


def roll(v, by):
    by = by % v.shape[1]
    return v if by == 0 else pltpu.roll(v, by, 1)


def teach_kernel(x_ref, p_ref, t_ref, x2_ref, pt_ref, tr_ref, g_ref, up_ref, dn_ref, buf, sem):
    chans, height, width = x_ref.shape
    ends = t_ref.shape[0]
    parts = sem.shape[0]
    step = ends // parts
    copies = [
        pltpu.make_async_copy(
            t_ref.at[pl.ds(k * step, step)], buf.at[pl.ds(k * step, step)], sem.at[k]
        )
        for k in range(parts)
    ]
    for c in copies:
        c.start()
    rows = jnp.swapaxes(x_ref[...], 0, 1)
    for h in range(height):
        x2_ref[:, h * width : (h + 1) * width] = rows[h]
    proj = p_ref[...]
    hi, lo = split(dot_nt(proj, proj))
    g_ref[:, :chans] = hi
    g_ref[:, chans:] = lo
    for k in range(parts):
        copies[k].wait()
        rows = jnp.swapaxes(buf[k * step : (k + 1) * step], 0, 1)
        for h in range(height):
            tr_ref[k * step : (k + 1) * step, h * width : (h + 1) * width] = rows[h]
        d = dot(p_ref[:, k * step : (k + 1) * step], tr_ref[k * step : (k + 1) * step, :])
        if k == 0:
            pt_ref[...] = d
        else:
            pt_ref[...] += d
    for ref, row, xrow in ((up_ref, 0, 0), (dn_ref, height - 1, height - 3)):
        ref[:, : 3 * width] = x2_ref[:, xrow * width : (xrow + 3) * width]
        hi, lo = split(pt_ref[:, row * width : (row + 1) * width])
        ref[:, 3 * width : 4 * width] = hi
        ref[:, 4 * width :] = lo


def strip_kernel(x2_ref, pt_ref, top_ref, bot_ref, ml_ref, mr_ref):
    width = top_ref.shape[1] // 5
    height = x2_ref.shape[1] // width
    lane = lanes_of((x2_ref.shape[0], 128))
    left = jnp.zeros((x2_ref.shape[0], 128), F32)
    right = left
    for r in range(height + 6):
        if r < 3:
            ref, base = top_ref, r * width
        elif r < height + 3:
            ref, base = x2_ref, (r - 3) * width
        else:
            ref, base = bot_ref, (r - height - 3) * width
        first = ref[:, base : base + 128].astype(F32)
        last = ref[:, base + width - 128 : base + width].astype(F32)
        at = r * PITCH
        left = jnp.where((lane >= at + 2) & (lane < at + 5), roll(first, at + 2), left)
        right = jnp.where((lane >= at) & (lane < at + 3), roll(last, at - 125), right)
    ml_ref[:, :128] = left.astype(BF16)
    mr_ref[:, :128] = right.astype(BF16)
    left = jnp.zeros((x2_ref.shape[0], 128), F32)
    right = left
    for r in range(height + 2):
        if 1 <= r <= height:
            base = (r - 1) * width
            first = pt_ref[:, base : base + 128]
            last = pt_ref[:, base + width - 128 : base + width]
        else:
            ref = top_ref if r == 0 else bot_ref
            a, b = 3 * width, 4 * width
            first = ref[:, a : a + 128].astype(F32) + ref[:, b : b + 128].astype(F32)
            last = ref[:, b - 128 : b].astype(F32) + ref[:, b + width - 128 :].astype(F32)
        at = r * PITCH
        left = jnp.where(lane == at, roll(first, at), left)
        right = jnp.where(lane == at, roll(last, at - 127), right)
    for ref, v in ((ml_ref, left), (mr_ref, right)):
        hi = v.astype(BF16).astype(F32)
        ref[:, 128:] = (hi + roll(v - hi, 1)).astype(BF16)


def gelu_parts(pre):
    cdf = 0.5 * (1.0 + lax.erf(pre * 0.7071067811865476))
    return pre * cdf, cdf


def main_kernel(
    flags, x2_ref, top_ref, bot_ref, ls_ref, rs_ref, ml_ref, mr_ref, pt_ref, tr_ref, g_ref,
    kin_ref, kout_ref, kback_ref, proj_ref, out_ref,
    x3, h3, d3, grad, s2, dpre2, inv_npix=1.0,
):
    chans = x2_ref.shape[0]
    width = top_ref.shape[1] // 5
    height = x2_ref.shape[1] // width
    has_up, has_dn = flags[0].astype(F32), flags[1].astype(F32)
    has_l, has_r = flags[2].astype(F32), flags[3].astype(F32)
    lane = lanes_of((chans, 128))
    kin, kout, kback = kin_ref[...], kout_ref[...], kback_ref[...]
    gram = g_ref[...]

    def taps(v):
        return jnp.concatenate(
            [roll(v, -(a * PITCH + b)) for a in range(3) for b in range(3)], 0
        ).astype(BF16)

    col = lax.rem(lane, PITCH)
    rowi = lax.div(lane, PITCH)
    halo_l = ls_ref[:, :128].astype(F32)
    halo_r = rs_ref[:, :128].astype(F32)
    strip = jnp.concatenate(
        [
            jnp.where(col < 3, halo_l, roll(ml_ref[:, :128].astype(F32), 1)),
            jnp.where(col >= 2, halo_r, roll(mr_ref[:, :128].astype(F32), -1)),
        ],
        1,
    )
    lane2 = lanes_of((1, 128))
    col1 = lax.rem(lane2, PITCH)
    row1 = lax.div(lane2, PITCH)

    def row_mask(rim):
        inside = jnp.where(row1 < rim, has_up, 1.0)
        return jnp.where(row1 >= height + rim, has_dn, inside)

    hid, _ = gelu_parts(dot(kin, taps(strip)))
    mask = row_mask(2)
    mask = jnp.concatenate(
        [mask * jnp.where(col1 < 2, has_l, 1.0), mask * jnp.where(col1 >= 1, has_r, 1.0)], 1
    )
    hid = (hid * mask).astype(BF16).astype(F32)
    stud = (roll(strip, -(2 * PITCH + 2)) + dot(kout, taps(hid))).astype(BF16)
    halves = jnp.concatenate([ls_ref[:, 128:].astype(F32), rs_ref[:, 128:].astype(F32)], 1)
    pts = halves + roll(halves, -1)
    ds_strip = (dot(gram, jnp.concatenate([stud, stud], 0)) - pts) * inv_npix
    mask = row_mask(1)
    ds_strip = ds_strip * jnp.concatenate([mask * has_l, mask * has_r], 1)
    ds_strip = ds_strip.astype(BF16).astype(F32)

    def put(dst, r, seg, left, at_l, right, at_r):
        lo, hi = r * width, (r + 1) * width
        seg32 = seg.astype(F32)
        ahead = roll(seg32, 1)
        first = jnp.where(lane == 0, roll(left, -at_l), ahead[:, :128])
        dst[0:chans, lo : lo + 128] = first.astype(BF16)
        dst[0:chans, lo + 128 : hi] = ahead[:, 128:].astype(BF16)
        dst[chans : 2 * chans, lo:hi] = seg
        back = roll(seg32, -1)
        last = jnp.where(lane == 127, roll(right, 127 - at_r), back[:, width - 128 :])
        dst[2 * chans :, lo : hi - 128] = back[:, : width - 128].astype(BF16)
        dst[2 * chans :, hi - 128 : hi] = last.astype(BF16)

    def rows3(src, r):
        return jnp.concatenate(
            [src[:, (r + a) * width : (r + a + 1) * width] for a in range(3)], 0
        )

    for r in range(height + 6):
        if r < 3:
            seg = top_ref[:, r * width : (r + 1) * width]
        elif r < height + 3:
            seg = x2_ref[:, (r - 3) * width : (r - 2) * width]
        else:
            seg = bot_ref[:, (r - height - 3) * width : (r - height - 2) * width]
        put(x3, r, seg, halo_l, r * PITCH + 2, halo_r, r * PITCH + 2)

    for r in range(height + 4):
        pre = dot(kin, rows3(x3, r))
        hid_r, cdf = gelu_parts(pre)
        if r < 2:
            hid_r = hid_r * has_up
        elif r >= height + 2:
            hid_r = hid_r * has_dn
        else:
            dens = jnp.exp(-0.5 * pre * pre) * 0.3989422804014327
            grad[:, (r - 2) * width : (r - 1) * width] = cdf + pre * dens
        at = r * PITCH + 1
        put(h3, r, hid_r.astype(BF16), hid[:, :128], at, hid[:, 128:], at)

    for r in range(height + 2):
        seg = x3[chans : 2 * chans, (r + 2) * width : (r + 3) * width]
        stud = (seg.astype(F32) + dot(kout, rows3(h3, r))).astype(BF16)
        if r == 0:
            pt = top_ref[:, 3 * width : 4 * width].astype(F32) + top_ref[:, 4 * width :].astype(F32)
        elif r == height + 1:
            pt = bot_ref[:, 3 * width : 4 * width].astype(F32) + bot_ref[:, 4 * width :].astype(F32)
        else:
            pt = pt_ref[:, (r - 1) * width : r * width]
            s2[:, (r - 1) * width : r * width] = stud
        ds = (dot(gram, jnp.concatenate([stud, stud], 0)) - pt) * inv_npix
        if r == 0:
            ds = ds * has_up
        elif r == height + 1:
            ds = ds * has_dn
        at = r * PITCH
        put(d3, r, ds.astype(BF16), ds_strip[:, :128], at, ds_strip[:, 128:], at)

    for r in range(height):
        span = slice(r * width, (r + 1) * width)
        dpre2[:, span] = (dot(kback, rows3(d3, r)) * grad[:, span]).astype(BF16)

    pixels = height * width
    per = 3 * chans
    offset = pl.cdiv(3 * per, 128) * 128
    for a in range(3):
        base = (a + 2) * width
        out_ref[:, a * per : (a + 1) * per] = dot_nt(dpre2[...], x3[:, base : base + pixels])
        base = (a + 1) * width
        out_ref[:, offset + a * per : offset + (a + 1) * per] = dot_nt(
            d3[chans : 2 * chans, width : width + pixels], h3[:, base : base + pixels]
        )
    out_ref[:, 3 * per : offset] = jnp.zeros((chans, offset - 3 * per), F32)
    out_ref[:, offset + 3 * per : 2 * offset] = jnp.zeros((chans, offset - 3 * per), F32)
    stud = s2[...]
    hi, lo = split(dot_nt(stud, stud))
    proj = proj_ref[...]
    gp = dot(jnp.concatenate([hi, lo], 1), jnp.concatenate([proj, proj], 0))
    out_ref[:, 2 * offset :] = (gp - dot_nt(stud, tr_ref[...])) * inv_npix


def unpack_kernel(v_ref, gin_ref, gout_ref, gproj_ref):
    chans = v_ref.shape[0]
    offset = pl.cdiv(9 * chans, 128) * 128
    for t in range(9):
        gin_ref[t] = v_ref[:, t * chans : (t + 1) * chans].T
        at = offset + t * chans
        gout_ref[t] = v_ref[:, at : at + chans].T
    gproj_ref[...] = v_ref[:, 2 * offset :]


VMEM = pl.BlockSpec(memory_space=pltpu.VMEM)
PARAMS = pltpu.CompilerParams(vmem_limit_bytes=44 << 20)


def swap(v, axis, bit):
    return lax.ppermute(v, axis, [(i, i ^ bit) for i in range(lax.axis_size(axis))])


def bits_of(axis):
    return [1 << k for k in range(lax.axis_size(axis).bit_length() - 1)]


def sum_all(v):
    col, row = bits_of("col"), bits_of("row")
    halved = [("col", col[0], 0), ("col", col[1], 0), ("row", row[0], 1)]
    rest = [("col", b) for b in col[2:]] + [("row", b) for b in row[1:]]
    for axis, bit, dim in halved:
        mine = (lax.axis_index(axis) & bit) // bit
        half = v.shape[dim] // 2
        give = lax.dynamic_slice_in_dim(v, (1 - mine) * half, half, dim)
        keep = lax.dynamic_slice_in_dim(v, mine * half, half, dim)
        v = keep + swap(give, axis, bit)
    for axis, bit in rest:
        v = v + swap(v, axis, bit)
    for axis, bit, dim in halved[::-1]:
        got = swap(v, axis, bit)
        upper = (lax.axis_index(axis) & bit) != 0
        v = jnp.concatenate([jnp.where(upper, got, v), jnp.where(upper, v, got)], dim)
    return v


def shift(v, axis, by):
    n = lax.axis_size(axis)
    return lax.ppermute(v, axis, [(i, i + by) for i in range(n) if 0 <= i + by < n])


def shards(features, teacher, conv_in, conv_out, projector):
    chans, height, width = features.shape
    ends = teacher.shape[0]
    pixels = height * width
    kin = jnp.transpose(conv_in, (2, 0, 1)).reshape(chans, 9 * chans)
    kout = jnp.transpose(conv_out, (2, 0, 1)).reshape(chans, 9 * chans)
    kback = jnp.transpose(conv_out[::-1], (1, 0, 2)).reshape(chans, 9 * chans)
    parts = 6
    x2, pt, tr, gram, up, dn = pl.pallas_call(
        teach_kernel,
        in_specs=[VMEM, VMEM, pl.BlockSpec(memory_space=pl.ANY)],
        out_specs=[VMEM] * 6,
        out_shape=[
            jax.ShapeDtypeStruct((chans, pixels), BF16),
            jax.ShapeDtypeStruct((chans, pixels), F32),
            pltpu.VMEM((ends, pixels), BF16),
            jax.ShapeDtypeStruct((chans, 2 * chans), BF16),
            jax.ShapeDtypeStruct((chans, 5 * width), BF16),
            jax.ShapeDtypeStruct((chans, 5 * width), BF16),
        ],
        scratch_shapes=[
            pltpu.VMEM((ends, height, width), BF16),
            pltpu.SemaphoreType.DMA((parts,)),
        ],
        compiler_params=PARAMS,
        name="teach",
    )(features, projector, teacher)
    bot = shift(up, "row", -1)
    top = shift(dn, "row", 1)
    ml, mr = pl.pallas_call(
        strip_kernel,
        in_specs=[VMEM] * 4,
        out_specs=[VMEM] * 2,
        out_shape=[jax.ShapeDtypeStruct((chans, 256), BF16)] * 2,
        compiler_params=PARAMS,
        name="strips",
    )(x2, pt, top, bot)
    rs = shift(ml, "col", -1)
    ls = shift(mr, "col", 1)
    row, col = lax.axis_index("row"), lax.axis_index("col")
    flags = jnp.stack(
        [row > 0, row < lax.axis_size("row") - 1, col > 0, col < lax.axis_size("col") - 1]
    ).astype(jnp.int32)
    npix = pixels * lax.axis_size("row") * lax.axis_size("col")
    offset = -(-9 * chans // 128) * 128

    def body(*refs):
        main_kernel(*refs, inv_npix=1.0 / npix)

    v = pl.pallas_call(
        body,
        in_specs=[pl.BlockSpec(memory_space=pltpu.SMEM)] + [VMEM] * 14,
        out_specs=VMEM,
        out_shape=jax.ShapeDtypeStruct((chans, 2 * offset + ends), F32),
        scratch_shapes=[
            pltpu.VMEM((3 * chans, (height + 6) * width), BF16),
            pltpu.VMEM((3 * chans, (height + 4) * width), BF16),
            pltpu.VMEM((3 * chans, (height + 2) * width), BF16),
            pltpu.VMEM((chans, pixels), F32),
            pltpu.VMEM((chans, pixels), BF16),
            pltpu.VMEM((chans, pixels), BF16),
        ],
        compiler_params=PARAMS,
        name="block",
    )(flags, x2, top, bot, ls, rs, ml, mr, pt, tr, gram, kin, kout, kback, projector)
    v = sum_all(v)
    return pl.pallas_call(
        unpack_kernel,
        in_specs=[VMEM],
        out_specs=[VMEM] * 3,
        out_shape=[
            jax.ShapeDtypeStruct((9, chans, chans), F32),
            jax.ShapeDtypeStruct((9, chans, chans), F32),
            jax.ShapeDtypeStruct((chans, ends), F32),
        ],
        compiler_params=PARAMS,
        name="unpack",
    )(v)


def solution(mesh):
    in_specs = (P(None, "row", "col"), P(None, "row", "col"), P(), P(), P())
    out_specs = (P(), P(), P())
    return jax.shard_map(shards, mesh=mesh, in_specs=in_specs, out_specs=out_specs, check_vma=False)
```

time: 280 us -> 123 us (0.44)
  waiting for transfers between devices: 153 us -> 43.3 us
  matrix products: 39.7 us -> 0 us
  Pallas kernels: 0 us -> 34.3 us
  local copies, waits for them, and re-layouts: 34.2 us -> 18.1 us
  between operations: 14.5 us -> 0.84 us
  starting transfers between devices: 32.5 us -> 24.8 us
  other arithmetic: 5.01 us -> 0.57 us
    psum x1 -> x0, waiting for transfers between devices: 139 us -> none  [shards(): result = lax.psum((grad_in, grad_out, grad_proj), ('row', 'col'))]
    dot_general x7 -> x0, matrix products: 39.7 us -> none  [the longest x1 9.17 us: shards(): jnp.einsum('khw,ohw->ko', x_taps, dpre, preferred_element_type=jnp.float32)]
    pallas_call x0 -> x4, Pallas kernels: none -> 34.3 us  [the longest x1 22.7 us: shards(): pl.pallas_call(body, in_specs=[pl.BlockSpec(memory_space=pltpu.SMEM)] + [...]
    ppermute x12, waiting for transfers between devices: 14.7 us -> 43.3 us  [the longest x8 33.8 us: swap(): lax.ppermute(v, axis, [(i, i ^ bit) for i in range(lax.axis_size(axis))])]
    unnamed x46 -> x36, local copies, waits for them, and re-layouts: 31.5 us -> 15.4 us
    ppermute x12, starting transfers between devices: 32.4 us -> 24.8 us  [the longest x8 15.8 us: swap(): lax.ppermute(v, axis, [(i, i ^ bit) for i in range(lax.axis_size(axis))])]
  transfers between devices with their start and end apart: 13 -> 12, of which waited for: 8 -> 10; matrix products, arithmetic and copies ran while one was open for 9% -> 2% of each run, Pallas kernels for 0% -> 0%
where the time goes in v1:
time: 123 us; the launch traced here: 122 us
  waiting for transfers between devices  43.3 us (35%)
  Pallas kernels  34.3 us (28%)
  starting transfers between devices  24.8 us (20%)
  local copies, waits for them, and re-layouts  18.1 us (15%)
    ppermute x8, waiting for transfers between devices, swap(): lax.ppermute(v, axis, [(i, i ^ bit) for i in range(lax.axis_size(axis))])  33.8 us
    pallas_call x1, Pallas kernels, shards(): pl.pallas_call(body, in_specs=[pl.BlockSpec(memory_space=pltpu.SMEM)] + [...  22.7 us
    ppermute x8, starting transfers between devices, swap(): lax.ppermute(v, axis, [(i, i ^ bit) for i in range(lax.axis_size(axis))])  15.8 us
    unnamed x36, local copies, waits for them, and re-layouts  15.4 us
    ppermute x4, waiting for transfers between devices, shift(): lax.ppermute(v, axis, [(i, i + by) for i in range(n) if 0 <= i + by < n])  9.5 us
    pallas_call x1, Pallas kernels, shards(): pl.pallas_call(teach_kernel, in_specs=[VMEM, VMEM, pl.BlockSpec(memory_sp...  9.08 us
    ppermute x4, starting transfers between devices, shift(): lax.ppermute(v, axis, [(i, i + by) for i in range(n) if 0 <= i + by < n])  9.02 us
  transfers between devices with their start and end apart: 12, of which 10 were waited for; matrix products, arithmetic and copies ran while one was open for 2% of the time, Pallas kernels for 0%

profile of v1, /device:TPU:0, one launch (start us, length us, event | category | flops | bytes accessed | tf_op | source)
XLA Modules:
  0.0 122.0 jit_solution(10666823021578440460)
XLA Ops:
  0.6 9.1 %teach.1 = (bf16[96,4096]{1,0:T(8,128)(2,1)}, f32[96,4096]{1,0:T(8,128)}, bf16[1536,4096]{1,0:T(8,128)(2,1)S(1)}, bf16[96,192]{1,0:T(8,128)(2,1)}, bf16[96,1280]{1,0:T(8,128)(2,1)}, /*index=5*/bf16[96,1280]{1,0:T(8,128)(2,1)}) custom-call(bf16[96,16,256]{2,1,0:T(8,128)(2,1)} %x_ref.1, bf16[96,1536]{1,0:T(8,128)(2,1)} %refs_14_.1, bf16[1536,16,256]{2,1,0:T(8,128)(2,1)} %t_ref.1), custom_call_target="tpu_custom_call" | custom-call | tf_op jit(solution)/shard_map/teach/pallas_call | solution.py:304
  9.7 4.5 %copy-done = bf16[1536,4096]{1,0:T(8,128)(2,1)} copy-done((bf16[1536,4096]{1,0:T(8,128)(2,1)}, bf16[1536,4096]{1,0:T(8,128)(2,1)S(1)}, u32[]{:S(2)}) %copy-start) | copy-done | bytes 12582936
  14.2 4.8 %collective-permute-start = (bf16[96,1280]{1,0:T(8,128)(2,1)}, bf16[96,1280]{1,0:T(8,128)(2,1)S(1)}, u32[]{:S(2)}, u32[]{:S(2)}) collective-permute-start(bf16[96,1280]{1,0:T(8,128)(2,1)} %get-tuple-element.12), channel_id=1, source_target_pairs={{0,4},{4,8},{8,12},{12,16},{16,20},{20,24},{24,28},{1,5},{5,9},{9,... | collective-permute-start | bytes 737288 | tf_op jit(solution)/shard_map/ppermute | solution.py:293
  19.1 1.3 %collective-permute-start.1 = (bf16[96,1280]{1,0:T(8,128)(2,1)}, bf16[96,1280]{1,0:T(8,128)(2,1)S(1)}, u32[]{:S(2)}, u32[]{:S(2)}) collective-permute-start(bf16[96,1280]{1,0:T(8,128)(2,1)} %get-tuple-element.13), channel_id=1, source_target_pairs={{4,0},{8,4},{12,8},{16,12},{20,16},{24,20},{28,24},{5,1},{9,5},{13... | collective-permute-start | bytes 737288 | tf_op jit(solution)/shard_map/ppermute | solution.py:293
  20.4 9.4 %collective-permute-done.top_ref.refs_2_ = bf16[96,1280]{1,0:T(8,128)(2,1)S(1)} collective-permute-done((bf16[96,1280]{1,0:T(8,128)(2,1)}, bf16[96,1280]{1,0:T(8,128)(2,1)S(1)}, u32[]{:S(2)}, u32[]{:S(2)}) %collective-permute-start) | collective-permute-done | bytes 245792 | tf_op jit(solution)/shard_map/ppermute | solution.py:293
  29.9 1.4 %copy-done.1 = f32[96,4096]{1,0:T(8,128)S(1)} copy-done((f32[96,4096]{1,0:T(8,128)S(1)}, f32[96,4096]{1,0:T(8,128)}, u32[]{:S(2)}) %copy-start.1) | copy-done | bytes 1572888
  34.0 1.4 %collective-permute-start.2 = (bf16[96,256]{1,0:T(8,128)(2,1)S(1)}, bf16[96,256]{1,0:T(8,128)(2,1)S(1)}, u32[]{:S(2)}, u32[]{:S(2)}) collective-permute-start(bf16[96,256]{1,0:T(8,128)(2,1)S(1)} %get-tuple-element.15.refs_7_), channel_id=1, source_target_pairs={{0,1},{1,2},{2,3},{4,5},{5,6},{6,7},{8,9},{9,10},{10,11},{12,13},{... | collective-permute-start | bytes 147464 | tf_op jit(solution)/shard_map/ppermute | solution.py:293
  35.4 1.5 %collective-permute-start.3 = (bf16[96,256]{1,0:T(8,128)(2,1)S(1)}, bf16[96,256]{1,0:T(8,128)(2,1)S(1)}, u32[]{:S(2)}, u32[]{:S(2)}) collective-permute-start(bf16[96,256]{1,0:T(8,128)(2,1)S(1)} %get-tuple-element.16.refs_6_), channel_id=1, source_target_pairs={{1,0},{2,1},{3,2},{5,4},{6,5},{7,6},{9,8},{10,9},{11,10},{13,12},{... | collective-permute-start | bytes 147464 | tf_op jit(solution)/shard_map/ppermute | solution.py:293
  47.3 22.7 %block.1 = f32[96,3328]{1,0:T(8,128)S(1)} custom-call(s32[4]{0:T(128)S(1)} %add_convert_fusion.refs_0_, bf16[96,4096]{1,0:T(8,128)(2,1)S(1)} %copy-done.4, bf16[96,1280]{1,0:T(8,128)(2,1)S(1)} %collective-permute-done.top_ref.refs_2_, bf16[96,1280]{1,0:T(8,128)(2,1)S(1)} %copy-done.7, bf16[96,256]{1,0:T(8,128)(2,1)S(1)} %copy-done.13, ...), custom_call_target="tpu_custom_call" | custom-call | tf_op jit(solution)/shard_map/block/pallas_call | solution.py:345
  70.1 2.9 %collective-permute-start.4 = (f32[48,3328]{1,0:T(8,128)S(1)}, f32[48,3328]{1,0:T(8,128)S(1)}, u32[]{:S(2)}, u32[]{:S(2)}) collective-permute-start(f32[48,3328]{1,0:T(8,128)S(1)} %constant_dynamic-slice_fusion.2), channel_id=1, source_target_pairs={{0,1},{1,0},{2,3},{3,2},{4,5},{5,4},{6,7},{7,6},{8,9},{9,8},{10,11... | collective-permute-start | bytes 1916936 | tf_op jit(solution)/shard_map/ppermute | solution.py:265
  72.9 1.7 %collective-permute-done.4 = f32[48,3328]{1,0:T(8,128)S(1)} collective-permute-done((f32[48,3328]{1,0:T(8,128)S(1)}, f32[48,3328]{1,0:T(8,128)S(1)}, u32[]{:S(2)}, u32[]{:S(2)}) %collective-permute-start.4) | collective-permute-done | bytes 639008 | tf_op jit(solution)/shard_map/ppermute | solution.py:265
  74.7 2.1 %collective-permute-start.5 = (f32[24,3328]{1,0:T(8,128)S(1)}, f32[24,3328]{1,0:T(8,128)S(1)}, u32[]{:S(2)}, u32[]{:S(2)}) collective-permute-start(f32[24,3328]{1,0:T(8,128)S(1)} %constant_dynamic-slice_fusion.1), channel_id=1, source_target_pairs={{0,2},{1,3},{2,0},{3,1},{4,6},{5,7},{6,4},{7,5},{8,10},{9,11},{10,... | collective-permute-start | bytes 958472 | tf_op jit(solution)/shard_map/ppermute | solution.py:265
  76.8 7.8 %collective-permute-done.5 = f32[24,3328]{1,0:T(8,128)S(1)} collective-permute-done((f32[24,3328]{1,0:T(8,128)S(1)}, f32[24,3328]{1,0:T(8,128)S(1)}, u32[]{:S(2)}, u32[]{:S(2)}) %collective-permute-start.5) | collective-permute-done | bytes 319520 | tf_op jit(solution)/shard_map/ppermute | solution.py:265
  84.7 2.4 %collective-permute-start.6 = (f32[24,1664]{1,0:T(8,128)S(1)}, f32[24,1664]{1,0:T(8,128)S(1)}, u32[]{:S(2)}, u32[]{:S(2)}) collective-permute-start(f32[24,1664]{1,0:T(8,128)S(1)} %constant_dynamic-slice_fusion), channel_id=1, source_target_pairs={{0,4},{4,0},{8,12},{12,8},{16,20},{20,16},{24,28},{28,24},{1,5},{5... | collective-permute-start | bytes 479240 | tf_op jit(solution)/shard_map/ppermute | solution.py:265
  87.1 3.9 %collective-permute-done.6 = f32[24,1664]{1,0:T(8,128)S(1)} collective-permute-done((f32[24,1664]{1,0:T(8,128)S(1)}, f32[24,1664]{1,0:T(8,128)S(1)}, u32[]{:S(2)}, u32[]{:S(2)}) %collective-permute-start.6) | collective-permute-done | bytes 159776 | tf_op jit(solution)/shard_map/ppermute | solution.py:265
  91.0 2.8 %collective-permute-start.7 = (f32[24,1664]{1,0:T(8,128)S(1)}, f32[24,1664]{1,0:T(8,128)S(1)}, u32[]{:S(2)}, u32[]{:S(2)}) collective-permute-start(f32[24,1664]{1,0:T(8,128)S(1)} %dynamic-slice_add_fusion.2), channel_id=1, source_target_pairs={{0,8},{4,12},{8,0},{12,4},{16,24},{20,28},{24,16},{28,20},{1,9},{5... | collective-permute-start | bytes 479240 | tf_op jit(solution)/shard_map/ppermute | solution.py:265
  93.8 3.3 %collective-permute-done.7 = f32[24,1664]{1,0:T(8,128)S(1)} collective-permute-done((f32[24,1664]{1,0:T(8,128)S(1)}, f32[24,1664]{1,0:T(8,128)S(1)}, u32[]{:S(2)}, u32[]{:S(2)}) %collective-permute-start.7) | collective-permute-done | bytes 159776 | tf_op jit(solution)/shard_map/ppermute | solution.py:265
  97.1 3.1 %collective-permute-start.8 = (f32[24,1664]{1,0:T(8,128)S(1)}, f32[24,1664]{1,0:T(8,128)S(1)}, u32[]{:S(2)}, u32[]{:S(2)}) collective-permute-start(f32[24,1664]{1,0:T(8,128)S(1)} %add.45), channel_id=1, source_target_pairs={{0,16},{4,20},{8,24},{12,28},{16,0},{20,4},{24,8},{28,12},{1,17},{... | collective-permute-start | bytes 479240 | tf_op jit(solution)/shard_map/ppermute | solution.py:265
  100.2 5.2 %collective-permute-done.8 = f32[24,1664]{1,0:T(8,128)S(1)} collective-permute-done((f32[24,1664]{1,0:T(8,128)S(1)}, f32[24,1664]{1,0:T(8,128)S(1)}, u32[]{:S(2)}, u32[]{:S(2)}) %collective-permute-start.8) | collective-permute-done | bytes 159776 | tf_op jit(solution)/shard_map/ppermute | solution.py:265
  106.2 4.6 %collective-permute-done.9 = f32[24,1664]{1,0:T(8,128)S(1)} collective-permute-done((f32[24,1664]{1,0:T(8,128)S(1)}, f32[24,1664]{1,0:T(8,128)S(1)}, u32[]{:S(2)}, u32[]{:S(2)}) %collective-permute-start.9) | collective-permute-done | bytes 159776 | tf_op jit(solution)/shard_map/ppermute | solution.py:265
  110.8 1.7 %collective-permute-start.10 = (f32[24,3328]{1,0:T(8,128)S(1)}, f32[24,3328]{1,0:T(8,128)S(1)}, u32[]{:S(2)}, u32[]{:S(2)}) collective-permute-start(f32[24,3328]{1,0:T(8,128)S(1)} %pad_maximum_fusion.2), channel_id=1, source_target_pairs={{0,2},{1,3},{2,0},{3,1},{4,6},{5,7},{6,4},{7,5},{8,10},{9,11},{10,... | collective-permute-start | bytes 958472 | tf_op jit(solution)/shard_map/ppermute | solution.py:265
  112.5 5.3 %collective-permute-done.10 = f32[24,3328]{1,0:T(8,128)S(1)} collective-permute-done((f32[24,3328]{1,0:T(8,128)S(1)}, f32[24,3328]{1,0:T(8,128)S(1)}, u32[]{:S(2)}, u32[]{:S(2)}) %collective-permute-start.10) | collective-permute-done | bytes 319520 | tf_op jit(solution)/shard_map/ppermute | solution.py:265
  118.1 2.1 %collective-permute-done.11 = f32[48,3328]{1,0:T(8,128)S(1)} collective-permute-done((f32[48,3328]{1,0:T(8,128)S(1)}, f32[48,3328]{1,0:T(8,128)S(1)}, u32[]{:S(2)}, u32[]{:S(2)}) %collective-permute-start.11) | collective-permute-done | bytes 639008 | tf_op jit(solution)/shard_map/ppermute | solution.py:265
  120.3 1.7 %unpack.1 = (f32[9,96,96]{2,1,0:T(8,128)}, f32[9,96,96]{2,1,0:T(8,128)}, f32[96,1536]{1,0:T(8,128)}) custom-call(f32[96,3328]{1,0:T(8,128)S(1)} %pad_maximum_fusion.v_ref), custom_call_target="tpu_custom_call" | custom-call | tf_op jit(solution)/shard_map/unpack/pallas_call | solution.py:362
  (60 shorter events, 14.6 us)
Async XLA Ops:
  0.6 19.8 %copy-start.16 = (bf16[9,96,96]{2,1,0:T(8,128)(2,1)S(1)}, bf16[9,96,96]{2,1,0:T(8,128)(2,1)}, u32[]{:S(2)}) copy-start(bf16[9,96,96]{2,1,0:T(8,128)(2,1)} %param.8) | copy-start | bytes 497668
  9.7 4.5 %copy-start = (bf16[1536,4096]{1,0:T(8,128)(2,1)}, bf16[1536,4096]{1,0:T(8,128)(2,1)S(1)}, u32[]{:S(2)}) copy-start(bf16[1536,4096]{1,0:T(8,128)(2,1)S(1)} %get-tuple-element.17.refs_9_) | copy-start | bytes 37748740
  14.2 15.6 %collective-permute-start = (bf16[96,1280]{1,0:T(8,128)(2,1)}, bf16[96,1280]{1,0:T(8,128)(2,1)S(1)}, u32[]{:S(2)}, u32[]{:S(2)}) collective-permute-start(bf16[96,1280]{1,0:T(8,128)(2,1)} %get-tuple-element.12), channel_id=1, source_target_pairs={{0,4},{4,8},{8,12},{12,16},{16,20},{20,24},{24,28},{1,5},{5,9},{9,... | collective-permute-start | bytes 737288 | tf_op jit(solution)/shard_map/ppermute | solution.py:293
  19.1 10.8 %collective-permute-start.1 = (bf16[96,1280]{1,0:T(8,128)(2,1)}, bf16[96,1280]{1,0:T(8,128)(2,1)S(1)}, u32[]{:S(2)}, u32[]{:S(2)}) collective-permute-start(bf16[96,1280]{1,0:T(8,128)(2,1)} %get-tuple-element.13), channel_id=1, source_target_pairs={{4,0},{8,4},{12,8},{16,12},{20,16},{24,20},{28,24},{5,1},{9,5},{13... | collective-permute-start | bytes 737288 | tf_op jit(solution)/shard_map/ppermute | solution.py:293
  29.9 1.4 %copy-start.1 = (f32[96,4096]{1,0:T(8,128)S(1)}, f32[96,4096]{1,0:T(8,128)}, u32[]{:S(2)}) copy-start(f32[96,4096]{1,0:T(8,128)} %get-tuple-element.14.pt_ref.refs_8_) | copy-start | bytes 4718596
  31.3 1.1 copy-start.3
  32.4 5.6 %copy-start.17 = (bf16[9,96,96]{2,1,0:T(8,128)(2,1)S(1)}, bf16[9,96,96]{2,1,0:T(8,128)(2,1)}, u32[]{:S(2)}) copy-start(bf16[9,96,96]{2,1,0:T(8,128)(2,1)} %param.7) | copy-start | bytes 497668
  32.4 8.5 %copy-start.5 = (bf16[96,1536]{1,0:T(8,128)(2,1)S(1)}, bf16[96,1536]{1,0:T(8,128)(2,1)}, u32[]{:S(2)}) copy-start(bf16[96,1536]{1,0:T(8,128)(2,1)} %refs_14_.1) | copy-start | bytes 884740
  34.0 6.9 %copy-start.2 = (f32[96,4096]{1,0:T(8,128)S(1)}, f32[96,4096]{1,0:T(8,128)}, u32[]{:S(2)}) copy-start(f32[96,4096]{1,0:T(8,128)} %get-tuple-element.14.pt_ref.refs_8_) | copy-start | bytes 4718596
  34.0 6.9 %copy-start.11 = (bf16[96,192]{1,0:T(8,128)(2,1)S(1)}, bf16[96,192]{1,0:T(8,128)(2,1)}, u32[]{:S(2)}) copy-start(bf16[96,192]{1,0:T(8,128)(2,1)} %get-tuple-element.18.refs_10_) | copy-start | bytes 110596
  34.0 5.6 %collective-permute-start.2 = (bf16[96,256]{1,0:T(8,128)(2,1)S(1)}, bf16[96,256]{1,0:T(8,128)(2,1)S(1)}, u32[]{:S(2)}, u32[]{:S(2)}) collective-permute-start(bf16[96,256]{1,0:T(8,128)(2,1)S(1)} %get-tuple-element.15.refs_7_), channel_id=1, source_target_pairs={{0,1},{1,2},{2,3},{4,5},{5,6},{6,7},{8,9},{9,10},{10,11},{12,13},{... | collective-permute-start | bytes 147464 | tf_op jit(solution)/shard_map/ppermute | solution.py:293
  35.4 4.9 %collective-permute-start.3 = (bf16[96,256]{1,0:T(8,128)(2,1)S(1)}, bf16[96,256]{1,0:T(8,128)(2,1)S(1)}, u32[]{:S(2)}, u32[]{:S(2)}) collective-permute-start(bf16[96,256]{1,0:T(8,128)(2,1)S(1)} %get-tuple-element.16.refs_6_), channel_id=1, source_target_pairs={{1,0},{2,1},{3,2},{5,4},{6,5},{7,6},{9,8},{10,9},{11,10},{13,12},{... | collective-permute-start | bytes 147464 | tf_op jit(solution)/shard_map/ppermute | solution.py:293
  40.9 1.1 copy-start.4
  42.0 0.9 copy-start.7
  43.0 0.9 copy-start.8
  43.9 0.9 copy-start.9
  70.1 4.6 %collective-permute-start.4 = (f32[48,3328]{1,0:T(8,128)S(1)}, f32[48,3328]{1,0:T(8,128)S(1)}, u32[]{:S(2)}, u32[]{:S(2)}) collective-permute-start(f32[48,3328]{1,0:T(8,128)S(1)} %constant_dynamic-slice_fusion.2), channel_id=1, source_target_pairs={{0,1},{1,0},{2,3},{3,2},{4,5},{5,4},{6,7},{7,6},{8,9},{9,8},{10,11... | collective-permute-start | bytes 1916936 | tf_op jit(solution)/shard_map/ppermute | solution.py:265
  74.7 9.9 %collective-permute-start.5 = (f32[24,3328]{1,0:T(8,128)S(1)}, f32[24,3328]{1,0:T(8,128)S(1)}, u32[]{:S(2)}, u32[]{:S(2)}) collective-permute-start(f32[24,3328]{1,0:T(8,128)S(1)} %constant_dynamic-slice_fusion.1), channel_id=1, source_target_pairs={{0,2},{1,3},{2,0},{3,1},{4,6},{5,7},{6,4},{7,5},{8,10},{9,11},{10,... | collective-permute-start | bytes 958472 | tf_op jit(solution)/shard_map/ppermute | solution.py:265
  84.7 6.3 %collective-permute-start.6 = (f32[24,1664]{1,0:T(8,128)S(1)}, f32[24,1664]{1,0:T(8,128)S(1)}, u32[]{:S(2)}, u32[]{:S(2)}) collective-permute-start(f32[24,1664]{1,0:T(8,128)S(1)} %constant_dynamic-slice_fusion), channel_id=1, source_target_pairs={{0,4},{4,0},{8,12},{12,8},{16,20},{20,16},{24,28},{28,24},{1,5},{5... | collective-permute-start | bytes 479240 | tf_op jit(solution)/shard_map/ppermute | solution.py:265
  91.0 6.0 %collective-permute-start.7 = (f32[24,1664]{1,0:T(8,128)S(1)}, f32[24,1664]{1,0:T(8,128)S(1)}, u32[]{:S(2)}, u32[]{:S(2)}) collective-permute-start(f32[24,1664]{1,0:T(8,128)S(1)} %dynamic-slice_add_fusion.2), channel_id=1, source_target_pairs={{0,8},{4,12},{8,0},{12,4},{16,24},{20,28},{24,16},{28,20},{1,9},{5... | collective-permute-start | bytes 479240 | tf_op jit(solution)/shard_map/ppermute | solution.py:265
  97.1 8.3 %collective-permute-start.8 = (f32[24,1664]{1,0:T(8,128)S(1)}, f32[24,1664]{1,0:T(8,128)S(1)}, u32[]{:S(2)}, u32[]{:S(2)}) collective-permute-start(f32[24,1664]{1,0:T(8,128)S(1)} %add.45), channel_id=1, source_target_pairs={{0,16},{4,20},{8,24},{12,28},{16,0},{20,4},{24,8},{28,12},{1,17},{... | collective-permute-start | bytes 479240 | tf_op jit(solution)/shard_map/ppermute | solution.py:265
  105.4 5.3 %collective-permute-start.9 = (f32[24,1664]{1,0:T(8,128)S(1)}, f32[24,1664]{1,0:T(8,128)S(1)}, u32[]{:S(2)}, u32[]{:S(2)}) collective-permute-start(f32[24,1664]{1,0:T(8,128)S(1)} %add.46), channel_id=1, source_target_pairs={{0,4},{4,0},{8,12},{12,8},{16,20},{20,16},{24,28},{28,24},{1,5},{5... | collective-permute-start | bytes 479240 | tf_op jit(solution)/shard_map/ppermute | solution.py:265
  110.8 7.1 %collective-permute-start.10 = (f32[24,3328]{1,0:T(8,128)S(1)}, f32[24,3328]{1,0:T(8,128)S(1)}, u32[]{:S(2)}, u32[]{:S(2)}) collective-permute-start(f32[24,3328]{1,0:T(8,128)S(1)} %pad_maximum_fusion.2), channel_id=1, source_target_pairs={{0,2},{1,3},{2,0},{3,1},{4,6},{5,7},{6,4},{7,5},{8,10},{9,11},{10,... | collective-permute-start | bytes 958472 | tf_op jit(solution)/shard_map/ppermute | solution.py:265
  118.0 2.1 %collective-permute-start.11 = (f32[48,3328]{1,0:T(8,128)S(1)}, f32[48,3328]{1,0:T(8,128)S(1)}, u32[]{:S(2)}, u32[]{:S(2)}) collective-permute-start(f32[48,3328]{1,0:T(8,128)S(1)} %pad_maximum_fusion.1), channel_id=1, source_target_pairs={{0,1},{1,0},{2,3},{3,2},{4,5},{5,4},{6,7},{7,6},{8,9},{9,8},{10,11... | collective-permute-start | bytes 1916936 | tf_op jit(solution)/shard_map/ppermute | solution.py:265
  (6 other events, 4.4 us)

commit v2 on v1

--- a/solution.py
+++ b/solution.py
@@ -1,3 +1,5 @@
+import functools
+
 import jax
 import jax.numpy as jnp
 from jax import lax
@@ -32,7 +34,22 @@
     return v if by == 0 else pltpu.roll(v, by, 1)
 
 
-def teach_kernel(x_ref, p_ref, t_ref, x2_ref, pt_ref, tr_ref, g_ref, up_ref, dn_ref, buf, sem):
+def strip_rows(left, right, first, last, at, lane):
+    left = jnp.where((lane >= at + 2) & (lane < at + 5), roll(first, at + 2), left)
+    right = jnp.where((lane >= at) & (lane < at + 3), roll(last, at - 125), right)
+    return left, right
+
+
+def strip_point(left, right, first, last, at, lane):
+    left = jnp.where(lane == at, roll(first, at), left)
+    right = jnp.where(lane == at, roll(last, at - 127), right)
+    return left, right
+
+
+def teach_kernel(
+    x_ref, p_ref, cin_ref, cout_ref, t_ref,
+    x2_ref, pt_ref, g_ref, up_ref, dn_ref, own_ref, k_ref, buf, tr, sem,
+):
     chans, height, width = x_ref.shape
     ends = t_ref.shape[0]
     parts = sem.shape[0]
@@ -52,16 +69,34 @@
     hi, lo = split(dot_nt(proj, proj))
     g_ref[:, :chans] = hi
     g_ref[:, chans:] = lo
+    k_ref[0] = jnp.concatenate([cin_ref[t].T for t in range(9)], 1)
+    k_ref[1] = jnp.concatenate([cout_ref[t].T for t in range(9)], 1)
+    k_ref[2] = jnp.concatenate([cout_ref[8 - t] for t in range(9)], 1)
+    lane = lanes_of((chans, 128))
+    left = right = jnp.zeros((chans, 128), F32)
+    for h in range(height):
+        first = x2_ref[:, h * width : h * width + 128].astype(F32)
+        last = x2_ref[:, (h + 1) * width - 128 : (h + 1) * width].astype(F32)
+        left, right = strip_rows(left, right, first, last, (h + 3) * PITCH, lane)
+    own_ref[0] = left
+    own_ref[1] = right
     for k in range(parts):
         copies[k].wait()
         rows = jnp.swapaxes(buf[k * step : (k + 1) * step], 0, 1)
         for h in range(height):
-            tr_ref[k * step : (k + 1) * step, h * width : (h + 1) * width] = rows[h]
-        d = dot(p_ref[:, k * step : (k + 1) * step], tr_ref[k * step : (k + 1) * step, :])
+            tr[k % 2, :, h * width : (h + 1) * width] = rows[h]
+        d = dot(p_ref[:, k * step : (k + 1) * step], tr[k % 2])
         if k == 0:
             pt_ref[...] = d
         else:
             pt_ref[...] += d
+    left = right = jnp.zeros((chans, 128), F32)
+    for h in range(height):
+        first = pt_ref[:, h * width : h * width + 128]
+        last = pt_ref[:, (h + 1) * width - 128 : (h + 1) * width]
+        left, right = strip_point(left, right, first, last, (h + 1) * PITCH, lane)
+    own_ref[2] = left
+    own_ref[3] = right
     for ref, row, xrow in ((up_ref, 0, 0), (dn_ref, height - 1, height - 3)):
         ref[:, : 3 * width] = x2_ref[:, xrow * width : (xrow + 3) * width]
         hi, lo = split(pt_ref[:, row * width : (row + 1) * width])
@@ -69,41 +104,24 @@
         ref[:, 4 * width :] = lo
 
 
-def strip_kernel(x2_ref, pt_ref, top_ref, bot_ref, ml_ref, mr_ref):
+def strip_kernel(own_ref, top_ref, bot_ref, ml_ref, mr_ref, *, height):
+    chans = top_ref.shape[0]
     width = top_ref.shape[1] // 5
-    height = x2_ref.shape[1] // width
-    lane = lanes_of((x2_ref.shape[0], 128))
-    left = jnp.zeros((x2_ref.shape[0], 128), F32)
-    right = left
-    for r in range(height + 6):
-        if r < 3:
-            ref, base = top_ref, r * width
-        elif r < height + 3:
-            ref, base = x2_ref, (r - 3) * width
-        else:
-            ref, base = bot_ref, (r - height - 3) * width
-        first = ref[:, base : base + 128].astype(F32)
-        last = ref[:, base + width - 128 : base + width].astype(F32)
-        at = r * PITCH
-        left = jnp.where((lane >= at + 2) & (lane < at + 5), roll(first, at + 2), left)
-        right = jnp.where((lane >= at) & (lane < at + 3), roll(last, at - 125), right)
+    lane = lanes_of((chans, 128))
+    left, right = own_ref[0], own_ref[1]
+    for r in range(3):
+        for ref, at in ((top_ref, r * PITCH), (bot_ref, (r + height + 3) * PITCH)):
+            first = ref[:, r * width : r * width + 128].astype(F32)
+            last = ref[:, (r + 1) * width - 128 : (r + 1) * width].astype(F32)
+            left, right = strip_rows(left, right, first, last, at, lane)
     ml_ref[:, :128] = left.astype(BF16)
     mr_ref[:, :128] = right.astype(BF16)
-    left = jnp.zeros((x2_ref.shape[0], 128), F32)
-    right = left
-    for r in range(height + 2):
-        if 1 <= r <= height:
-            base = (r - 1) * width
-            first = pt_ref[:, base : base + 128]
-            last = pt_ref[:, base + width - 128 : base + width]
-        else:
-            ref = top_ref if r == 0 else bot_ref
-            a, b = 3 * width, 4 * width
-            first = ref[:, a : a + 128].astype(F32) + ref[:, b : b + 128].astype(F32)
-            last = ref[:, b - 128 : b].astype(F32) + ref[:, b + width - 128 :].astype(F32)
-        at = r * PITCH
-        left = jnp.where(lane == at, roll(first, at), left)
-        right = jnp.where(lane == at, roll(last, at - 127), right)
+    left, right = own_ref[2], own_ref[3]
+    a, b = 3 * width, 4 * width
+    for ref, at in ((top_ref, 0), (bot_ref, (height + 1) * PITCH)):
+        first = ref[:, a : a + 128].astype(F32) + ref[:, b : b + 128].astype(F32)
+        last = ref[:, b - 128 : b].astype(F32) + ref[:, b + width - 128 :].astype(F32)
+        left, right = strip_point(left, right, first, last, at, lane)
     for ref, v in ((ml_ref, left), (mr_ref, right)):
         hi = v.astype(BF16).astype(F32)
         ref[:, 128:] = (hi + roll(v - hi, 1)).astype(BF16)
@@ -115,17 +133,23 @@
 
 
 def main_kernel(
-    flags, x2_ref, top_ref, bot_ref, ls_ref, rs_ref, ml_ref, mr_ref, pt_ref, tr_ref, g_ref,
-    kin_ref, kout_ref, kback_ref, proj_ref, out_ref,
-    x3, h3, d3, grad, s2, dpre2, inv_npix=1.0,
+    flags, *refs, inv_npix, count,
 ):
+    hbm, refs = refs[:count], refs[count:]
+    out_ref, x3, h3, d3, grad, s2, dpre2, wide, tr, sem, *refs = refs
+    copies = [pltpu.make_async_copy(a, b, sem.at[i]) for i, (a, b) in enumerate(zip(hbm, refs))]
+    for c in copies:
+        c.start()
+    ls_ref, rs_ref, ml_ref, mr_ref, k_ref, g_ref, x2_ref, top_ref, bot_ref, pt_ref, proj_ref, t_ref = refs
+    for c in copies[:-3]:
+        c.wait()
     chans = x2_ref.shape[0]
     width = top_ref.shape[1] // 5
     height = x2_ref.shape[1] // width
     has_up, has_dn = flags[0].astype(F32), flags[1].astype(F32)
     has_l, has_r = flags[2].astype(F32), flags[3].astype(F32)
     lane = lanes_of((chans, 128))
-    kin, kout, kback = kin_ref[...], kout_ref[...], kback_ref[...]
+    kin, kout, kback = k_ref[0], k_ref[1], k_ref[2]
     gram = g_ref[...]
 
     def taps(v):
@@ -209,14 +233,18 @@
     for r in range(height + 2):
         seg = x3[chans : 2 * chans, (r + 2) * width : (r + 3) * width]
         stud = (seg.astype(F32) + dot(kout, rows3(h3, r))).astype(BF16)
+        s2[:chans, r * width : (r + 1) * width] = stud
+        s2[chans:, r * width : (r + 1) * width] = stud
+
+    copies[-3].wait()
+    for r in range(height + 2):
         if r == 0:
             pt = top_ref[:, 3 * width : 4 * width].astype(F32) + top_ref[:, 4 * width :].astype(F32)
         elif r == height + 1:
             pt = bot_ref[:, 3 * width : 4 * width].astype(F32) + bot_ref[:, 4 * width :].astype(F32)
         else:
             pt = pt_ref[:, (r - 1) * width : r * width]
-            s2[:, (r - 1) * width : r * width] = stud
-        ds = (dot(gram, jnp.concatenate([stud, stud], 0)) - pt) * inv_npix
+        ds = (dot(gram, s2[:, r * width : (r + 1) * width]) - pt) * inv_npix
         if r == 0:
             ds = ds * has_up
         elif r == height + 1:
@@ -230,35 +258,63 @@
 
     pixels = height * width
     per = 3 * chans
-    offset = pl.cdiv(3 * per, 128) * 128
-    for a in range(3):
-        base = (a + 2) * width
-        out_ref[:, a * per : (a + 1) * per] = dot_nt(dpre2[...], x3[:, base : base + pixels])
-        base = (a + 1) * width
-        out_ref[:, offset + a * per : offset + (a + 1) * per] = dot_nt(
-            d3[chans : 2 * chans, width : width + pixels], h3[:, base : base + pixels]
-        )
-    out_ref[:, 3 * per : offset] = jnp.zeros((chans, offset - 3 * per), F32)
-    out_ref[:, offset + 3 * per : 2 * offset] = jnp.zeros((chans, offset - 3 * per), F32)
-    stud = s2[...]
+    quarter = 9 * chans // 4
+    piece = chans // 3
+    for n, (src, lag, grads) in enumerate(
+        ((x3, 2, dpre2[...]), (h3, 1, d3[chans : 2 * chans, width : width + pixels]))
+    ):
+        for a in range(3):
+            base = (a + lag) * width
+            wide[a * per : (a + 1) * per, :chans] = dot_nt(src[:, base : base + pixels], grads)
+        for k in range(3):
+            at = (3 * n + k) * quarter
+            rows = wide[k * quarter : (k + 1) * quarter, :]
+            extra = roll(wide[3 * quarter : 4 * quarter, :], chans - k * piece)
+            lane_q = lanes_of((quarter, 128))
+            out_ref[at : at + quarter, :] = jnp.where(lane_q < chans, rows, extra)
+
+    copies[-2].wait()
+    copies[-1].wait()
+    stud = s2[:chans, width : width + pixels]
     hi, lo = split(dot_nt(stud, stud))
     proj = proj_ref[...]
     gp = dot(jnp.concatenate([hi, lo], 1), jnp.concatenate([proj, proj], 0))
-    out_ref[:, 2 * offset :] = (gp - dot_nt(stud, tr_ref[...])) * inv_npix
+    parts, step = tr.shape[0], tr.shape[1]
+    start = 6 * quarter
+    for k in range(t_ref.shape[0] // step):
+        rows = jnp.swapaxes(t_ref[k * step : (k + 1) * step], 0, 1)
+        for h in range(height):
+            tr[k % parts, :, h * width : (h + 1) * width] = rows[h]
+        cross = dot_nt(tr[k % parts], stud)
+        for j in range(k * step // 128, (k + 1) * step // 128):
+            lo = j * 128 - k * step
+            part = gp[:, j * 128 : (j + 1) * 128] - cross[lo : lo + 128].T
+            out_ref[start + j * chans : start + (j + 1) * chans, :] = part * inv_npix
+    end = start + t_ref.shape[0] // 128 * chans
+    out_ref[end:, :] = jnp.zeros((out_ref.shape[0] - end, 128), F32)
 
 
 def unpack_kernel(v_ref, gin_ref, gout_ref, gproj_ref):
-    chans = v_ref.shape[0]
-    offset = pl.cdiv(9 * chans, 128) * 128
-    for t in range(9):
-        gin_ref[t] = v_ref[:, t * chans : (t + 1) * chans].T
-        at = offset + t * chans
-        gout_ref[t] = v_ref[:, at : at + chans].T
-    gproj_ref[...] = v_ref[:, 2 * offset :]
+    chans = gproj_ref.shape[0]
+    quarter = 9 * chans // 4
+    piece = chans // 3
+    for n, ref in enumerate((gin_ref, gout_ref)):
+        for k in range(3):
+            at = (3 * n + k) * quarter
+            ref[k * quarter : (k + 1) * quarter, :] = v_ref[at : at + quarter, :chans]
+            ref[3 * quarter :, k * piece : (k + 1) * piece] = v_ref[at : at + quarter, chans:]
+    start = 6 * quarter
+    for j in range(gproj_ref.shape[1] // 128):
+        at = start + j * chans
+        gproj_ref[:, j * 128 : (j + 1) * 128] = v_ref[at : at + chans, :]
 
 
 VMEM = pl.BlockSpec(memory_space=pltpu.VMEM)
-PARAMS = pltpu.CompilerParams(vmem_limit_bytes=44 << 20)
+ANY = pl.BlockSpec(memory_space=pl.ANY)
+
+
+def grant(mib):
+    return pltpu.CompilerParams(vmem_limit_bytes=mib << 20)
 
 
 def swap(v, axis, bit):
@@ -271,7 +327,7 @@
 
 def sum_all(v):
     col, row = bits_of("col"), bits_of("row")
-    halved = [("col", col[0], 0), ("col", col[1], 0), ("row", row[0], 1)]
+    halved = [("col", col[0], 0), ("col", col[1], 0), ("row", row[0], 0)]
     rest = [("col", b) for b in col[2:]] + [("row", b) for b in row[1:]]
     for axis, bit, dim in halved:
         mine = (lax.axis_index(axis) & bit) // bit
@@ -297,39 +353,38 @@
     chans, height, width = features.shape
     ends = teacher.shape[0]
     pixels = height * width
-    kin = jnp.transpose(conv_in, (2, 0, 1)).reshape(chans, 9 * chans)
-    kout = jnp.transpose(conv_out, (2, 0, 1)).reshape(chans, 9 * chans)
-    kback = jnp.transpose(conv_out[::-1], (1, 0, 2)).reshape(chans, 9 * chans)
     parts = 6
-    x2, pt, tr, gram, up, dn = pl.pallas_call(
+    x2, pt, gram, up, dn, own, kernels = pl.pallas_call(
         teach_kernel,
-        in_specs=[VMEM, VMEM, pl.BlockSpec(memory_space=pl.ANY)],
-        out_specs=[VMEM] * 6,
+        in_specs=[VMEM] * 4 + [ANY],
+        out_specs=[VMEM] * 7,
         out_shape=[
             jax.ShapeDtypeStruct((chans, pixels), BF16),
             jax.ShapeDtypeStruct((chans, pixels), F32),
-            pltpu.VMEM((ends, pixels), BF16),
             jax.ShapeDtypeStruct((chans, 2 * chans), BF16),
             jax.ShapeDtypeStruct((chans, 5 * width), BF16),
             jax.ShapeDtypeStruct((chans, 5 * width), BF16),
+            jax.ShapeDtypeStruct((4, chans, 128), F32),
+            jax.ShapeDtypeStruct((3, chans, 9 * chans), BF16),
         ],
         scratch_shapes=[
             pltpu.VMEM((ends, height, width), BF16),
+            pltpu.VMEM((2, ends // parts, pixels), BF16),
             pltpu.SemaphoreType.DMA((parts,)),
         ],
-        compiler_params=PARAMS,
+        compiler_params=grant(60),
         name="teach",
-    )(features, projector, teacher)
+    )(features, projector, conv_in, conv_out, teacher)
     bot = shift(up, "row", -1)
     top = shift(dn, "row", 1)
     ml, mr = pl.pallas_call(
-        strip_kernel,
-        in_specs=[VMEM] * 4,
+        functools.partial(strip_kernel, height=height),
+        in_specs=[VMEM] * 3,
         out_specs=[VMEM] * 2,
         out_shape=[jax.ShapeDtypeStruct((chans, 256), BF16)] * 2,
-        compiler_params=PARAMS,
+        compiler_params=grant(8),
         name="strips",
-    )(x2, pt, top, bot)
+    )(own, top, bot)
     rs = shift(ml, "col", -1)
     ls = shift(mr, "col", 1)
     row, col = lax.axis_index("row"), lax.axis_index("col")
@@ -337,40 +392,43 @@
         [row > 0, row < lax.axis_size("row") - 1, col > 0, col < lax.axis_size("col") - 1]
     ).astype(jnp.int32)
     npix = pixels * lax.axis_size("row") * lax.axis_size("col")
-    offset = -(-9 * chans // 128) * 128
-
-    def body(*refs):
-        main_kernel(*refs, inv_npix=1.0 / npix)
-
+    total = 2 * 9 * chans * chans // 128 + ends // 128 * chans
+    total = -(-total // 64) * 64
+    arrays = (ls, rs, ml, mr, kernels, gram, x2, top, bot, pt, projector, teacher)
     v = pl.pallas_call(
-        body,
-        in_specs=[pl.BlockSpec(memory_space=pltpu.SMEM)] + [VMEM] * 14,
+        functools.partial(main_kernel, inv_npix=1.0 / npix, count=len(arrays)),
+        in_specs=[pl.BlockSpec(memory_space=pltpu.SMEM)] + [ANY] * len(arrays),
         out_specs=VMEM,
-        out_shape=jax.ShapeDtypeStruct((chans, 2 * offset + ends), F32),
+        out_shape=jax.ShapeDtypeStruct((total, 128), F32),
         scratch_shapes=[
             pltpu.VMEM((3 * chans, (height + 6) * width), BF16),
             pltpu.VMEM((3 * chans, (height + 4) * width), BF16),
             pltpu.VMEM((3 * chans, (height + 2) * width), BF16),
             pltpu.VMEM((chans, pixels), F32),
+            pltpu.VMEM((2 * chans, (height + 2) * width), BF16),
             pltpu.VMEM((chans, pixels), BF16),
-            pltpu.VMEM((chans, pixels), BF16),
-        ],
-        compiler_params=PARAMS,
+            pltpu.VMEM((9 * chans, 128), F32),
+            pltpu.VMEM((2, ends // parts, pixels), BF16),
+            pltpu.SemaphoreType.DMA((len(arrays),)),
+        ]
+        + [pltpu.VMEM(a.shape, a.dtype) for a in arrays],
+        compiler_params=grant(60),
         name="block",
-    )(flags, x2, top, bot, ls, rs, ml, mr, pt, tr, gram, kin, kout, kback, projector)
+    )(flags, *arrays)
     v = sum_all(v)
-    return pl.pallas_call(
+    gin, gout, gproj = pl.pallas_call(
         unpack_kernel,
         in_specs=[VMEM],
         out_specs=[VMEM] * 3,
         out_shape=[
-            jax.ShapeDtypeStruct((9, chans, chans), F32),
-            jax.ShapeDtypeStruct((9, chans, chans), F32),
+            jax.ShapeDtypeStruct((9 * chans, chans), F32),
+            jax.ShapeDtypeStruct((9 * chans, chans), F32),
             jax.ShapeDtypeStruct((chans, ends), F32),
         ],
-        compiler_params=PARAMS,
+        compiler_params=grant(12),
         name="unpack",
     )(v)
+    return gin.reshape(9, chans, chans), gout.reshape(9, chans, chans), gproj
 
 
 def solution(mesh):

time: 123 us -> 105 us (0.85)
  local copies, waits for them, and re-layouts: 18.1 us -> 2.99 us
  waiting for transfers between devices: 43.3 us -> 48.9 us
  Pallas kernels: 34.3 us -> 29.4 us
  starting transfers between devices: 24.8 us -> 21.7 us
    unnamed x36 -> x16, local copies, waits for them, and re-layouts: 15.4 us -> 1.71 us
    pallas_call x3, Pallas kernels: 32.6 us -> 28.2 us  [the longest x1 18.1 us: shards(): pl.pallas_call(functools.partial(main_kernel, inv_npix=1.0 / npix, count=...]
    ppermute x8, starting transfers between devices: 15.8 us -> 12.8 us  [swap(): lax.ppermute(v, axis, [(i, i ^ bit) for i in range(lax.axis_size(axis))])]
    ppermute x8, waiting for transfers between devices: 33.8 us -> 36.6 us  [swap(): lax.ppermute(v, axis, [(i, i ^ bit) for i in range(lax.axis_size(axis))])]
    ppermute x4, waiting for transfers between devices: 9.5 us -> 12.2 us  [shift(): lax.ppermute(v, axis, [(i, i + by) for i in range(n) if 0 <= i + by < n])]
    reshape x3 -> x0, local copies, waits for them, and re-layouts: 2.43 us -> none  [the longest x1 0.81 us: shards(): kback = jnp.transpose(conv_out[::-1], (1, 0, 2)).reshape(chans, 9 * chans)]
  transfers between devices with their start and end apart: 12 -> 12, of which waited for: 10 -> 10; matrix products, arithmetic and copies ran while one was open for 2% -> 1% of each run, Pallas kernels for 0% -> 0%
where the time goes in v2:
time: 105 us
  waiting for transfers between devices  48.9 us (47%)
  Pallas kernels  29.4 us (28%)
  starting transfers between devices  21.7 us (21%)
  local copies, waits for them, and re-layouts  2.99 us (3%)
  other arithmetic  1.09 us (1%)
    ppermute x8, waiting for transfers between devices, swap(): lax.ppermute(v, axis, [(i, i ^ bit) for i in range(lax.axis_size(axis))])  36.6 us
    pallas_call x1, Pallas kernels, shards(): pl.pallas_call(functools.partial(main_kernel, inv_npix=1.0 / npix, count=...  18.1 us
    ppermute x8, starting transfers between devices, swap(): lax.ppermute(v, axis, [(i, i ^ bit) for i in range(lax.axis_size(axis))])  12.8 us
    ppermute x4, waiting for transfers between devices, shift(): lax.ppermute(v, axis, [(i, i + by) for i in range(n) if 0 <= i + by < n])  12.2 us
    pallas_call x1, Pallas kernels, shards(): pl.pallas_call(teach_kernel, in_specs=[VMEM] * 4 + [ANY], out_specs=[VMEM...  9.78 us
    ppermute x4, starting transfers between devices, shift(): lax.ppermute(v, axis, [(i, i + by) for i in range(n) if 0 <= i + by < n])  8.91 us
  transfers between devices with their start and end apart: 12, of which 10 were waited for; matrix products, arithmetic and copies ran while one was open for 1% of the time, Pallas kernels for 0%

profile of v2, /device:TPU:0, one launch (start us, length us, event | category | flops | bytes accessed | tf_op | source)
XLA Modules:
  0.0 105.0 jit_solution(7233154606578902095)
XLA Ops:
  0.6 9.8 %teach.1 = (bf16[96,4096]{1,0:T(8,128)(2,1)}, f32[96,4096]{1,0:T(8,128)}, bf16[96,192]{1,0:T(8,128)(2,1)}, bf16[96,1280]{1,0:T(8,128)(2,1)}, bf16[96,1280]{1,0:T...) custom-call(bf16[96,16,256]{2,1,0:T(8,128)(2,1)} %x_ref.1, bf16[96,1536]{1,0:T(8,128)(2,1)} %refs_10_.1, ...), custom_call_target="tpu_custom_call" | custom-call | tf_op jit(solution)/shard_map/teach/pallas_call | solution.py:357
  10.4 4.9 %collective-permute-start = (bf16[96,1280]{1,0:T(8,128)(2,1)}, bf16[96,1280]{1,0:T(8,128)(2,1)S(1)}, u32[]{:S(2)}, u32[]{:S(2)}) collective-permute-start(bf16[96,1280]{1,0:T(8,128)(2,1)} %get-tuple-element.16), channel_id=1, source_target_pairs={{0,4},{4,8},{8,12},{12,16},{16,20},{20,24},{24,28},{1,5},{5,9},{9,... | collective-permute-start | bytes 737288 | tf_op jit(solution)/shard_map/ppermute | solution.py:349
  15.3 1.3 %collective-permute-start.1 = (bf16[96,1280]{1,0:T(8,128)(2,1)}, bf16[96,1280]{1,0:T(8,128)(2,1)S(1)}, u32[]{:S(2)}, u32[]{:S(2)}) collective-permute-start(bf16[96,1280]{1,0:T(8,128)(2,1)} %get-tuple-element.17), channel_id=1, source_target_pairs={{4,0},{8,4},{12,8},{16,12},{20,16},{24,20},{28,24},{5,1},{9,5},{13... | collective-permute-start | bytes 737288 | tf_op jit(solution)/shard_map/ppermute | solution.py:349
  16.6 9.4 %collective-permute-done.top_ref.refs_7_ = bf16[96,1280]{1,0:T(8,128)(2,1)S(1)} collective-permute-done((bf16[96,1280]{1,0:T(8,128)(2,1)}, bf16[96,1280]{1,0:T(8,128)(2,1)S(1)}, u32[]{:S(2)}, u32[]{:S(2)}) %collective-permute-start) | collective-permute-done | bytes 245792 | tf_op jit(solution)/shard_map/ppermute | solution.py:349
  26.1 1.1 %copy-done.2 = f32[4,96,128]{2,1,0:T(8,128)S(1)} copy-done((f32[4,96,128]{2,1,0:T(8,128)S(1)}, f32[4,96,128]{2,1,0:T(8,128)}, u32[]{:S(2)}) %copy-start.2) | copy-done | bytes 196632
  27.4 1.3 %collective-permute-start.2 = (bf16[96,256]{1,0:T(8,128)(2,1)S(1)}, bf16[96,256]{1,0:T(8,128)(2,1)S(1)}, u32[]{:S(2)}, u32[]{:S(2)}) collective-permute-start(bf16[96,256]{1,0:T(8,128)(2,1)S(1)} %get-tuple-element.18.refs_3_), channel_id=1, source_target_pairs={{0,1},{1,2},{2,3},{4,5},{5,6},{6,7},{8,9},{9,10},{10,11},{12,13},{... | collective-permute-start | bytes 147464 | tf_op jit(solution)/shard_map/ppermute | solution.py:349
  28.7 1.5 %collective-permute-start.3 = (bf16[96,256]{1,0:T(8,128)(2,1)S(1)}, bf16[96,256]{1,0:T(8,128)(2,1)S(1)}, u32[]{:S(2)}, u32[]{:S(2)}) collective-permute-start(bf16[96,256]{1,0:T(8,128)(2,1)S(1)} %get-tuple-element.19.refs_2_), channel_id=1, source_target_pairs={{1,0},{2,1},{3,2},{5,4},{6,5},{7,6},{9,8},{10,9},{11,10},{13,12},{... | collective-permute-start | bytes 147464 | tf_op jit(solution)/shard_map/ppermute | solution.py:349
  30.8 2.8 %collective-permute-done.3.refs_1_ = bf16[96,256]{1,0:T(8,128)(2,1)S(1)} collective-permute-done((bf16[96,256]{1,0:T(8,128)(2,1)S(1)}, bf16[96,256]{1,0:T(8,128)(2,1)S(1)}, u32[]{:S(2)}, u32[]{:S(2)}) %collective-permute-start.3) | collective-permute-done | bytes 49184 | tf_op jit(solution)/shard_map/ppermute | solution.py:349
  34.2 18.1 %block.1 = f32[2496,128]{1,0:T(8,128)} custom-call(s32[4]{0:T(128)} %add_convert_fusion.flags, bf16[96,256]{1,0:T(8,128)(2,1)} %copy-done.6, bf16[96,256]{1,0:T(8,128)(2,1)} %copy-done.7, bf16[96,256]{1,0:T(8,128)(2,1)} %copy-done.3, bf16[96,256]{1,0:T(8,128)(2,1)} %copy-done.4, bf16[3,96,864]{2,1,0:T(8,128)(2,1)} %get-tuple-element.20.refs_4_, ...), custom_call_target="tpu_custom_call" | custom-call | tf_op jit(solution)/shard_map/block/pallas_call | solution.py:398
  52.4 1.2 %constant_dynamic-slice_fusion.2 = f32[1248,128]{1,0:T(8,128)S(1)} fusion(f32[2496,128]{1,0:T(8,128)} %block.1, s32[]{:T(128)S(6)} %select_n.65), kind=kLoop, calls=%fused_computation.15 | loop fusion | bytes 1277956 | tf_op jit(solution)/shard_map/dynamic_slice | solution.py:335
  53.6 2.8 %collective-permute-start.4 = (f32[1248,128]{1,0:T(8,128)S(1)}, f32[1248,128]{1,0:T(8,128)S(1)}, u32[]{:S(2)}, u32[]{:S(2)}) collective-permute-start(f32[1248,128]{1,0:T(8,128)S(1)} %constant_dynamic-slice_fusion.2), channel_id=1, source_target_pairs={{0,1},{1,0},{2,3},{3,2},{4,5},{5,4},{6,7},{7,6},{8,9},{9,8},{10,11... | collective-permute-start | bytes 1916936 | tf_op jit(solution)/shard_map/ppermute | solution.py:321
  56.5 1.7 %collective-permute-done.4 = f32[1248,128]{1,0:T(8,128)S(1)} collective-permute-done((f32[1248,128]{1,0:T(8,128)S(1)}, f32[1248,128]{1,0:T(8,128)S(1)}, u32[]{:S(2)}, u32[]{:S(2)}) %collective-permute-start.4) | collective-permute-done | bytes 639008 | tf_op jit(solution)/shard_map/ppermute | solution.py:321
  58.6 9.6 %collective-permute-done.5 = f32[624,128]{1,0:T(8,128)S(1)} collective-permute-done((f32[624,128]{1,0:T(8,128)S(1)}, f32[624,128]{1,0:T(8,128)S(1)}, u32[]{:S(2)}, u32[]{:S(2)}) %collective-permute-start.5) | collective-permute-done | bytes 319520 | tf_op jit(solution)/shard_map/ppermute | solution.py:321
  68.2 2.4 %collective-permute-start.6 = (f32[312,128]{1,0:T(8,128)S(1)}, f32[312,128]{1,0:T(8,128)S(1)}, u32[]{:S(2)}, u32[]{:S(2)}) collective-permute-start(f32[312,128]{1,0:T(8,128)S(1)} %constant_dynamic-slice_fusion), channel_id=1, source_target_pairs={{0,4},{4,0},{8,12},{12,8},{16,20},{20,16},{24,28},{28,24},{1,5},{5... | collective-permute-start | bytes 479240 | tf_op jit(solution)/shard_map/ppermute | solution.py:321
  70.7 3.8 %collective-permute-done.6 = f32[312,128]{1,0:T(8,128)S(1)} collective-permute-done((f32[312,128]{1,0:T(8,128)S(1)}, f32[312,128]{1,0:T(8,128)S(1)}, u32[]{:S(2)}, u32[]{:S(2)}) %collective-permute-start.6) | collective-permute-done | bytes 159776 | tf_op jit(solution)/shard_map/ppermute | solution.py:321
  74.5 2.7 %collective-permute-start.7 = (f32[312,128]{1,0:T(8,128)S(1)}, f32[312,128]{1,0:T(8,128)S(1)}, u32[]{:S(2)}, u32[]{:S(2)}) collective-permute-start(f32[312,128]{1,0:T(8,128)S(1)} %dynamic-slice_add_fusion.2), channel_id=1, source_target_pairs={{0,8},{4,12},{8,0},{12,4},{16,24},{20,28},{24,16},{28,20},{1,9},{5... | collective-permute-start | bytes 479240 | tf_op jit(solution)/shard_map/ppermute | solution.py:321
  77.2 3.3 %collective-permute-done.7 = f32[312,128]{1,0:T(8,128)S(1)} collective-permute-done((f32[312,128]{1,0:T(8,128)S(1)}, f32[312,128]{1,0:T(8,128)S(1)}, u32[]{:S(2)}, u32[]{:S(2)}) %collective-permute-start.7) | collective-permute-done | bytes 159776 | tf_op jit(solution)/shard_map/ppermute | solution.py:321
  80.5 3.1 %collective-permute-start.8 = (f32[312,128]{1,0:T(8,128)S(1)}, f32[312,128]{1,0:T(8,128)S(1)}, u32[]{:S(2)}, u32[]{:S(2)}) collective-permute-start(f32[312,128]{1,0:T(8,128)S(1)} %add.45), channel_id=1, source_target_pairs={{0,16},{4,20},{8,24},{12,28},{16,0},{20,4},{24,8},{28,12},{1,17},{... | collective-permute-start | bytes 479240 | tf_op jit(solution)/shard_map/ppermute | solution.py:321
  83.6 5.2 %collective-permute-done.8 = f32[312,128]{1,0:T(8,128)S(1)} collective-permute-done((f32[312,128]{1,0:T(8,128)S(1)}, f32[312,128]{1,0:T(8,128)S(1)}, u32[]{:S(2)}, u32[]{:S(2)}) %collective-permute-start.8) | collective-permute-done | bytes 159776 | tf_op jit(solution)/shard_map/ppermute | solution.py:321
  88.8 0.9 collective-permute-start.9
  89.7 4.5 %collective-permute-done.9 = f32[312,128]{1,0:T(8,128)S(1)} collective-permute-done((f32[312,128]{1,0:T(8,128)S(1)}, f32[312,128]{1,0:T(8,128)S(1)}, u32[]{:S(2)}, u32[]{:S(2)}) %collective-permute-start.9) | collective-permute-done | bytes 159776 | tf_op jit(solution)/shard_map/ppermute | solution.py:321
  94.7 6.6 %collective-permute-done.10 = f32[624,128]{1,0:T(8,128)S(1)} collective-permute-done((f32[624,128]{1,0:T(8,128)S(1)}, f32[624,128]{1,0:T(8,128)S(1)}, u32[]{:S(2)}, u32[]{:S(2)}) %collective-permute-start.10) | collective-permute-done | bytes 319520 | tf_op jit(solution)/shard_map/ppermute | solution.py:321
  101.4 2.1 %collective-permute-done.11 = f32[1248,128]{1,0:T(8,128)S(1)} collective-permute-done((f32[1248,128]{1,0:T(8,128)S(1)}, f32[1248,128]{1,0:T(8,128)S(1)}, u32[]{:S(2)}, u32[]{:S(2)}) %collective-permute-start.11) | collective-permute-done | bytes 639008 | tf_op jit(solution)/shard_map/ppermute | solution.py:321
  103.7 1.3 %unpack.1 = (f32[864,96]{1,0:T(8,128)}, f32[864,96]{1,0:T(8,128)}, f32[96,1536]{1,0:T(8,128)}) custom-call(f32[2496,128]{1,0:T(8,128)S(1)} %pad_maximum_fusion.v_ref), custom_call_target="tpu_custom_call" | custom-call | tf_op jit(solution)/shard_map/unpack/pallas_call | solution.py:419
  (35 shorter events, 2.9 us)
Async XLA Ops:
  10.4 15.6 %collective-permute-start = (bf16[96,1280]{1,0:T(8,128)(2,1)}, bf16[96,1280]{1,0:T(8,128)(2,1)S(1)}, u32[]{:S(2)}, u32[]{:S(2)}) collective-permute-start(bf16[96,1280]{1,0:T(8,128)(2,1)} %get-tuple-element.16), channel_id=1, source_target_pairs={{0,4},{4,8},{8,12},{12,16},{16,20},{20,24},{24,28},{1,5},{5,9},{9,... | collective-permute-start | bytes 737288 | tf_op jit(solution)/shard_map/ppermute | solution.py:349
  15.3 10.8 %collective-permute-start.1 = (bf16[96,1280]{1,0:T(8,128)(2,1)}, bf16[96,1280]{1,0:T(8,128)(2,1)S(1)}, u32[]{:S(2)}, u32[]{:S(2)}) collective-permute-start(bf16[96,1280]{1,0:T(8,128)(2,1)} %get-tuple-element.17), channel_id=1, source_target_pairs={{4,0},{8,4},{12,8},{16,12},{20,16},{24,20},{28,24},{5,1},{9,5},{13... | collective-permute-start | bytes 737288 | tf_op jit(solution)/shard_map/ppermute | solution.py:349
  26.0 7.6 %copy-start = (bf16[96,1280]{1,0:T(8,128)(2,1)}, bf16[96,1280]{1,0:T(8,128)(2,1)S(1)}, u32[]{:S(2)}) copy-start(bf16[96,1280]{1,0:T(8,128)(2,1)S(1)} %collective-permute-done.top_ref.refs_7_) | copy-start | bytes 737284
  26.1 7.6 %copy-start.1 = (bf16[96,1280]{1,0:T(8,128)(2,1)}, bf16[96,1280]{1,0:T(8,128)(2,1)S(1)}, u32[]{:S(2)}) copy-start(bf16[96,1280]{1,0:T(8,128)(2,1)S(1)} %collective-permute-done.1.bot_ref.refs_8_) | copy-start | bytes 737284
  26.1 1.1 %copy-start.2 = (f32[4,96,128]{2,1,0:T(8,128)S(1)}, f32[4,96,128]{2,1,0:T(8,128)}, u32[]{:S(2)}) copy-start(f32[4,96,128]{2,1,0:T(8,128)} %get-tuple-element.15.own_ref) | copy-start | bytes 589828
  27.4 6.2 %copy-start.3 = (bf16[96,256]{1,0:T(8,128)(2,1)}, bf16[96,256]{1,0:T(8,128)(2,1)S(1)}, u32[]{:S(2)}) copy-start(bf16[96,256]{1,0:T(8,128)(2,1)S(1)} %get-tuple-element.19.refs_2_) | copy-start | bytes 147460
  27.4 6.2 %copy-start.4 = (bf16[96,256]{1,0:T(8,128)(2,1)}, bf16[96,256]{1,0:T(8,128)(2,1)S(1)}, u32[]{:S(2)}) copy-start(bf16[96,256]{1,0:T(8,128)(2,1)S(1)} %get-tuple-element.18.refs_3_) | copy-start | bytes 147460
  27.4 3.4 %collective-permute-start.2 = (bf16[96,256]{1,0:T(8,128)(2,1)S(1)}, bf16[96,256]{1,0:T(8,128)(2,1)S(1)}, u32[]{:S(2)}, u32[]{:S(2)}) collective-permute-start(bf16[96,256]{1,0:T(8,128)(2,1)S(1)} %get-tuple-element.18.refs_3_), channel_id=1, source_target_pairs={{0,1},{1,2},{2,3},{4,5},{5,6},{6,7},{8,9},{9,10},{10,11},{12,13},{... | collective-permute-start | bytes 147464 | tf_op jit(solution)/shard_map/ppermute | solution.py:349
  28.7 4.9 %collective-permute-start.3 = (bf16[96,256]{1,0:T(8,128)(2,1)S(1)}, bf16[96,256]{1,0:T(8,128)(2,1)S(1)}, u32[]{:S(2)}, u32[]{:S(2)}) collective-permute-start(bf16[96,256]{1,0:T(8,128)(2,1)S(1)} %get-tuple-element.19.refs_2_), channel_id=1, source_target_pairs={{1,0},{2,1},{3,2},{5,4},{6,5},{7,6},{9,8},{10,9},{11,10},{13,12},{... | collective-permute-start | bytes 147464 | tf_op jit(solution)/shard_map/ppermute | solution.py:349
  30.8 2.8 %copy-start.6 = (bf16[96,256]{1,0:T(8,128)(2,1)}, bf16[96,256]{1,0:T(8,128)(2,1)S(1)}, u32[]{:S(2)}) copy-start(bf16[96,256]{1,0:T(8,128)(2,1)S(1)} %collective-permute-done.2.refs_0_) | copy-start | bytes 147460
  33.6 0.6 copy-start.7
  52.4 5.8 %copy-start.5 = (f32[2496,128]{1,0:T(8,128)S(1)}, f32[2496,128]{1,0:T(8,128)}, u32[]{:S(2)}) copy-start(f32[2496,128]{1,0:T(8,128)} %block.1) | copy-start | bytes 3833860
  53.6 4.5 %collective-permute-start.4 = (f32[1248,128]{1,0:T(8,128)S(1)}, f32[1248,128]{1,0:T(8,128)S(1)}, u32[]{:S(2)}, u32[]{:S(2)}) collective-permute-start(f32[1248,128]{1,0:T(8,128)S(1)} %constant_dynamic-slice_fusion.2), channel_id=1, source_target_pairs={{0,1},{1,0},{2,3},{3,2},{4,5},{5,4},{6,7},{7,6},{8,9},{9,8},{10,11... | collective-permute-start | bytes 1916936 | tf_op jit(solution)/shard_map/ppermute | solution.py:321
  58.3 9.9 %collective-permute-start.5 = (f32[624,128]{1,0:T(8,128)S(1)}, f32[624,128]{1,0:T(8,128)S(1)}, u32[]{:S(2)}, u32[]{:S(2)}) collective-permute-start(f32[624,128]{1,0:T(8,128)S(1)} %constant_dynamic-slice_fusion.1), channel_id=1, source_target_pairs={{0,2},{1,3},{2,0},{3,1},{4,6},{5,7},{6,4},{7,5},{8,10},{9,11},{10,... | collective-permute-start | bytes 958472 | tf_op jit(solution)/shard_map/ppermute | solution.py:321
  68.2 6.3 %collective-permute-start.6 = (f32[312,128]{1,0:T(8,128)S(1)}, f32[312,128]{1,0:T(8,128)S(1)}, u32[]{:S(2)}, u32[]{:S(2)}) collective-permute-start(f32[312,128]{1,0:T(8,128)S(1)} %constant_dynamic-slice_fusion), channel_id=1, source_target_pairs={{0,4},{4,0},{8,12},{12,8},{16,20},{20,16},{24,28},{28,24},{1,5},{5... | collective-permute-start | bytes 479240 | tf_op jit(solution)/shard_map/ppermute | solution.py:321
  74.5 6.0 %collective-permute-start.7 = (f32[312,128]{1,0:T(8,128)S(1)}, f32[312,128]{1,0:T(8,128)S(1)}, u32[]{:S(2)}, u32[]{:S(2)}) collective-permute-start(f32[312,128]{1,0:T(8,128)S(1)} %dynamic-slice_add_fusion.2), channel_id=1, source_target_pairs={{0,8},{4,12},{8,0},{12,4},{16,24},{20,28},{24,16},{28,20},{1,9},{5... | collective-permute-start | bytes 479240 | tf_op jit(solution)/shard_map/ppermute | solution.py:321
  80.5 8.3 %collective-permute-start.8 = (f32[312,128]{1,0:T(8,128)S(1)}, f32[312,128]{1,0:T(8,128)S(1)}, u32[]{:S(2)}, u32[]{:S(2)}) collective-permute-start(f32[312,128]{1,0:T(8,128)S(1)} %add.45), channel_id=1, source_target_pairs={{0,16},{4,20},{8,24},{12,28},{16,0},{20,4},{24,8},{28,12},{1,17},{... | collective-permute-start | bytes 479240 | tf_op jit(solution)/shard_map/ppermute | solution.py:321
  88.8 5.3 %collective-permute-start.9 = (f32[312,128]{1,0:T(8,128)S(1)}, f32[312,128]{1,0:T(8,128)S(1)}, u32[]{:S(2)}, u32[]{:S(2)}) collective-permute-start(f32[312,128]{1,0:T(8,128)S(1)} %add.46), channel_id=1, source_target_pairs={{0,4},{4,0},{8,12},{12,8},{16,20},{20,16},{24,28},{28,24},{1,5},{5... | collective-permute-start | bytes 479240 | tf_op jit(solution)/shard_map/ppermute | solution.py:321
  94.2 7.1 %collective-permute-start.10 = (f32[624,128]{1,0:T(8,128)S(1)}, f32[624,128]{1,0:T(8,128)S(1)}, u32[]{:S(2)}, u32[]{:S(2)}) collective-permute-start(f32[624,128]{1,0:T(8,128)S(1)} %pad_maximum_fusion.2), channel_id=1, source_target_pairs={{0,2},{1,3},{2,0},{3,1},{4,6},{5,7},{6,4},{7,5},{8,10},{9,11},{10,... | collective-permute-start | bytes 958472 | tf_op jit(solution)/shard_map/ppermute | solution.py:321
  101.4 2.1 %collective-permute-start.11 = (f32[1248,128]{1,0:T(8,128)S(1)}, f32[1248,128]{1,0:T(8,128)S(1)}, u32[]{:S(2)}, u32[]{:S(2)}) collective-permute-start(f32[1248,128]{1,0:T(8,128)S(1)} %pad_maximum_fusion.1), channel_id=1, source_target_pairs={{0,1},{1,0},{2,3},{3,2},{4,5},{5,4},{6,7},{7,6},{8,9},{9,8},{10,11... | collective-permute-start | bytes 1916936 | tf_op jit(solution)/shard_map/ppermute | solution.py:321

commit v3 on v0

v3 whole, which is shorter than its diff:
```python
import functools

import jax
import jax.numpy as jnp
from jax import lax
from jax.experimental import pallas as pl
from jax.experimental.pallas import tpu as pltpu
from jax.sharding import PartitionSpec as P

F32 = jnp.float32
BF16 = jnp.bfloat16
PITCH = 3
RIGHT = 64


def dot(a, b):
    return jnp.dot(a, b, preferred_element_type=F32)


def dot_nt(a, b):
    return lax.dot_general(a, b, (((1,), (1,)), ((), ())), preferred_element_type=F32)


def split(v):
    hi = v.astype(BF16)
    return hi, (v - hi.astype(F32)).astype(BF16)


def lanes_of(shape):
    return lax.broadcasted_iota(jnp.int32, shape, 1)


def roll(v, by):
    by = by % v.shape[1]
    return v if by == 0 else pltpu.roll(v, by, 1)


def weight_kernel(cin_ref, cout_ref, p_ref, k_ref, pt_ref):
    k_ref[0] = jnp.concatenate([cin_ref[t].T for t in range(9)], 1)
    k_ref[1] = jnp.concatenate([cout_ref[t].T for t in range(9)], 1)
    k_ref[2] = jnp.concatenate([cout_ref[8 - t] for t in range(9)], 1)
    pt_ref[...] = p_ref[...].T


def feature_kernel(x_ref, x2_ref, up_ref, dn_ref):
    height, width = x_ref.shape[1:]
    rows = jnp.swapaxes(x_ref[...], 0, 1)
    for h in range(height):
        x2_ref[:, h * width : (h + 1) * width] = rows[h]
    for h in range(2):
        up_ref[:, h * width : (h + 1) * width] = rows[h]
        dn_ref[:, h * width : (h + 1) * width] = rows[height - 2 + h]


def strip_kernel(x2_ref, top_ref, bot_ref, ml_ref, mr_ref, own_ref):
    chans = x2_ref.shape[0]
    width = top_ref.shape[1] // 2
    height = x2_ref.shape[1] // width
    lane = lanes_of((chans, 128))
    left = right = own = jnp.zeros((chans, 128), F32)
    for r in range(height + 4):
        if r < 2:
            ref, base = top_ref, r * width
        elif r < height + 2:
            ref, base = x2_ref, (r - 2) * width
        else:
            ref, base = bot_ref, (r - height - 2) * width
        first = ref[:, base : base + 128].astype(F32)
        last = ref[:, base + width - 128 : base + width].astype(F32)
        at = r * PITCH
        left = jnp.where((lane >= at + 1) & (lane < at + 3), roll(first, at + 1), left)
        right = jnp.where((lane >= at) & (lane < at + 2), roll(last, at - 126), right)
        own = jnp.where(lane == at + 2, roll(first, at + 2), own)
        own = jnp.where(lane == at + RIGHT, roll(last, at + RIGHT - 127), own)
    ml_ref[...] = left.astype(BF16)
    mr_ref[...] = right.astype(BF16)
    own_ref[...] = own.astype(BF16)


def gelu_and_slope(pre):
    cdf = 0.5 * (1.0 + lax.erf(pre * 0.7071067811865476))
    dens = jnp.exp(-0.5 * pre * pre) * 0.3989422804014327
    return pre * cdf, cdf + pre * dens


def main_kernel(flags, *refs, inv_npix, count):
    hbm, refs = refs[:count], refs[count:]
    out_ref, x3, h3, d3, grad, s2, dpre2, wide, gp, tr, sem, *refs = refs
    parts = sem.shape[0] - count + 1
    copies = [
        pltpu.make_async_copy(a, b, sem.at[i]) for i, (a, b) in enumerate(zip(hbm[:-1], refs))
    ]
    for c in copies:
        c.start()
    k_ref, x2_ref, own_ref, ls_ref, rs_ref, top_ref, bot_ref, pt_ref, proj_ref, t_ref = refs
    ends = t_ref.shape[0]
    step = ends // parts
    pieces = [
        pltpu.make_async_copy(
            hbm[-1].at[pl.ds(k * step, step)],
            t_ref.at[pl.ds(k * step, step)],
            sem.at[count - 1 + k],
        )
        for k in range(parts)
    ]
    for c in pieces:
        c.start()
    for c in copies[:-2]:
        c.wait()
    chans = x2_ref.shape[0]
    width = top_ref.shape[1] // 2
    height = x2_ref.shape[1] // width
    pixels = height * width
    has_up, has_dn = flags[0].astype(F32), flags[1].astype(F32)
    has_l, has_r = flags[2].astype(F32), flags[3].astype(F32)
    lane = lanes_of((chans, 128))
    kin, kout, kback = k_ref[0], k_ref[1], k_ref[2]

    def taps(v):
        return jnp.concatenate(
            [roll(v, -(a * PITCH + b)) for a in range(3) for b in range(3)], 0
        ).astype(BF16)

    part = lax.rem(lane, RIGHT)
    col = lax.rem(part, PITCH)
    halo_l, halo_r = ls_ref[...].astype(F32), roll(rs_ref[...].astype(F32), RIGHT)
    strip = jnp.where(lane < RIGHT, jnp.where(col < 2, halo_l, 0.0), jnp.where(col > 0, halo_r, 0.0))
    strip = jnp.where(part < (height + 4) * PITCH, strip, 0.0) + own_ref[...].astype(F32)
    strip_taps = taps(strip)
    lane1 = lanes_of((1, 128))
    part1 = lax.rem(lane1, RIGHT)
    mask = jnp.where(part1 == 0, has_up, jnp.where(part1 == (height + 1) * PITCH, has_dn, 1.0))
    mask = jnp.where(lane1 < RIGHT, mask * has_l, mask * has_r)
    mask = jnp.where((lax.rem(part1, PITCH) == 0) & (part1 < (height + 2) * PITCH), mask, 0.0)
    hid_s, grad_s = gelu_and_slope(dot(kin, strip_taps))
    hid_s = (hid_s * mask).astype(BF16).astype(F32)
    grad_s = grad_s * mask

    def put(dst, r, seg, rim, at):
        lo, hi = r * width, (r + 1) * width
        seg32 = seg.astype(F32)
        ahead = roll(seg32, 1)
        first = roll(rim, -at) if rim is not None else 0.0
        first = jnp.where(lane == 0, first, ahead[:, :128])
        dst[0:chans, lo : lo + 128] = first.astype(BF16)
        dst[0:chans, lo + 128 : hi] = ahead[:, 128:].astype(BF16)
        dst[chans : 2 * chans, lo:hi] = seg
        back = roll(seg32, -1)
        last = roll(rim, 127 - RIGHT - at) if rim is not None else 0.0
        last = jnp.where(lane == 127, last, back[:, width - 128 :])
        dst[2 * chans :, lo : hi - 128] = back[:, : width - 128].astype(BF16)
        dst[2 * chans :, hi - 128 : hi] = last.astype(BF16)

    def rows3(src, r):
        return jnp.concatenate(
            [src[:, (r + a) * width : (r + a + 1) * width] for a in range(3)], 0
        )

    for r in range(height + 4):
        if r < 2:
            seg = top_ref[:, r * width : (r + 1) * width]
        elif r < height + 2:
            seg = x2_ref[:, (r - 2) * width : (r - 1) * width]
        else:
            seg = bot_ref[:, (r - height - 2) * width : (r - height - 1) * width]
        put(x3, r, seg, strip, r * PITCH + 1)

    for r in range(height + 2):
        hid, slope = gelu_and_slope(dot(kin, rows3(x3, r)))
        if r == 0:
            hid, slope = hid * has_up, slope * has_up
        elif r == height + 1:
            hid, slope = hid * has_dn, slope * has_dn
        grad[:, r * width : (r + 1) * width] = slope
        put(h3, r, hid.astype(BF16), hid_s, r * PITCH)

    for r in range(height):
        span = slice(r * width, (r + 1) * width)
        seg = x2_ref[:, span].astype(F32)
        s2[:, span] = (seg + dot(kout, rows3(h3, r))).astype(BF16)

    for k in range(parts):
        pieces[k].wait()
        rows = jnp.swapaxes(t_ref[k * step : (k + 1) * step], 0, 1)
        for h in range(height):
            tr[k * step : (k + 1) * step, h * width : (h + 1) * width] = rows[h]

    for c in copies[-2:]:
        c.wait()
    proj_t, proj = pt_ref[...], proj_ref[...]
    rim = jnp.zeros((3 * chans, 2 * width), BF16)
    d3[:, : 2 * width] = rim
    d3[:, (height + 2) * width :] = rim
    ds_s = jnp.zeros((chans, 128), F32)
    for r in range(height):
        span = slice(r * width, (r + 1) * width)
        stud = s2[:, span]
        pred = dot(proj_t, stud)
        dpred = ((pred - tr[:, span].astype(F32)) * inv_npix).astype(BF16)
        cross = dot_nt(dpred, stud)
        if r == 0:
            gp[...] = cross
        else:
            gp[...] += cross
        ds = dot(proj, dpred).astype(BF16)
        put(d3, r + 2, ds, None, 0)
        at = (r + 2) * PITCH
        ds32 = ds.astype(F32)
        ds_s = jnp.where(lane == at + 2, roll(ds32[:, :128], at + 2), ds_s)
        ds_s = jnp.where(lane == at + RIGHT, roll(ds32[:, width - 128 :], at + RIGHT - 127), ds_s)

    for r in range(height + 2):
        span = slice(r * width, (r + 1) * width)
        dpre2[:, span] = (dot(kback, rows3(d3, r)) * grad[:, span]).astype(BF16)
    dpre_s = (dot(kback, taps(ds_s)) * grad_s).astype(BF16)

    per = 3 * chans
    quarter = 9 * chans // 4
    piece = chans // 3
    lane_q = lanes_of((quarter, 128))
    for n in range(2):
        for a in range(3):
            base = a * width
            if n == 0:
                g = dot_nt(x3[:, base : base + pixels + 2 * width], dpre2[...])
                g += dot_nt(strip_taps[a * per : (a + 1) * per], dpre_s)
            else:
                grads = d3[chans : 2 * chans, 2 * width : 2 * width + pixels]
                g = dot_nt(h3[:, base : base + pixels], grads)
            wide[a * per : (a + 1) * per, :chans] = g
        for k in range(3):
            at = (3 * n + k) * quarter
            rows = wide[k * quarter : (k + 1) * quarter, :]
            extra = roll(wide[3 * quarter : 4 * quarter, :], chans - k * piece)
            out_ref[at : at + quarter, :] = jnp.where(lane_q < chans, rows, extra)

    start = 6 * quarter
    for j in range(ends // 128):
        at = start + j * chans
        out_ref[at : at + chans, :] = gp[j * 128 : (j + 1) * 128, :].T
    end = start + ends // 128 * chans
    out_ref[end:, :] = jnp.zeros((out_ref.shape[0] - end, 128), F32)


def unpack_kernel(v_ref, gin_ref, gout_ref, gproj_ref):
    chans = gproj_ref.shape[0]
    quarter = 9 * chans // 4
    piece = chans // 3
    for n, ref in enumerate((gin_ref, gout_ref)):
        for k in range(3):
            at = (3 * n + k) * quarter
            ref[k * quarter : (k + 1) * quarter, :] = v_ref[at : at + quarter, :chans]
            ref[3 * quarter :, k * piece : (k + 1) * piece] = v_ref[at : at + quarter, chans:]
    start = 6 * quarter
    for j in range(gproj_ref.shape[1] // 128):
        at = start + j * chans
        gproj_ref[:, j * 128 : (j + 1) * 128] = v_ref[at : at + chans, :]


VMEM = pl.BlockSpec(memory_space=pltpu.VMEM)
ANY = pl.BlockSpec(memory_space=pl.ANY)


def grant(mib):
    return pltpu.CompilerParams(vmem_limit_bytes=mib << 20)


def swap(v, bits):
    n = lax.axis_size("row") * lax.axis_size("col")
    return lax.ppermute(v, ("row", "col"), [(i, i ^ bits[i & 1]) for i in range(n)])


def sum_all(v):
    me = lax.axis_index("row") * lax.axis_size("col") + lax.axis_index("col")
    n = lax.axis_size("row") * lax.axis_size("col")
    bits = [1 << k for k in range(1, n.bit_length() - 1)]
    steps = [(1, 1)]
    for k in range(len(bits)):
        other = k ^ 1 if k ^ 1 < len(bits) else k
        steps.append((bits[k], bits[other]))
    halved, rest = steps[:3], steps[3:]

    def upper(pair):
        return (me & jnp.where(me % 2 == 0, pair[0], pair[1])) != 0

    for pair in halved:
        mine = upper(pair).astype(jnp.int32)
        half = v.shape[0] // 2
        give = lax.dynamic_slice_in_dim(v, (1 - mine) * half, half, 0)
        keep = lax.dynamic_slice_in_dim(v, mine * half, half, 0)
        v = keep + swap(give, pair)
    for pair in rest:
        v = v + swap(v, pair)
    for pair in halved[::-1]:
        got = swap(v, pair)
        top = upper(pair)
        v = jnp.concatenate([jnp.where(top, got, v), jnp.where(top, v, got)], 0)
    return v


def shift(v, axis, by):
    n = lax.axis_size(axis)
    return lax.ppermute(v, axis, [(i, i + by) for i in range(n) if 0 <= i + by < n])


def shards(features, teacher, conv_in, conv_out, projector):
    chans, height, width = features.shape
    ends = teacher.shape[0]
    pixels = height * width
    parts = 6
    x2, up, dn = pl.pallas_call(
        feature_kernel,
        in_specs=[VMEM],
        out_specs=[VMEM] * 3,
        out_shape=[
            jax.ShapeDtypeStruct((chans, pixels), BF16),
            jax.ShapeDtypeStruct((chans, 2 * width), BF16),
            jax.ShapeDtypeStruct((chans, 2 * width), BF16),
        ],
        compiler_params=grant(8),
        name="features",
    )(features)
    bot = shift(up, "row", -1)
    top = shift(dn, "row", 1)
    kernels, proj_t = pl.pallas_call(
        weight_kernel,
        in_specs=[VMEM] * 3,
        out_specs=[VMEM] * 2,
        out_shape=[
            jax.ShapeDtypeStruct((3, chans, 9 * chans), BF16),
            jax.ShapeDtypeStruct((ends, chans), BF16),
        ],
        compiler_params=grant(8),
        name="weights",
    )(conv_in, conv_out, projector)
    ml, mr, own = pl.pallas_call(
        strip_kernel,
        in_specs=[VMEM] * 3,
        out_specs=[VMEM] * 3,
        out_shape=[jax.ShapeDtypeStruct((chans, 128), BF16)] * 3,
        compiler_params=grant(8),
        name="strips",
    )(x2, top, bot)
    rs = shift(ml, "col", -1)
    ls = shift(mr, "col", 1)
    row, col = lax.axis_index("row"), lax.axis_index("col")
    flags = jnp.stack(
        [row > 0, row < lax.axis_size("row") - 1, col > 0, col < lax.axis_size("col") - 1]
    ).astype(jnp.int32)
    npix = pixels * lax.axis_size("row") * lax.axis_size("col")
    total = 2 * 9 * chans * chans // 128 + ends // 128 * chans
    total = -(-total // 64) * 64
    arrays = (kernels, x2, own, ls, rs, top, bot, proj_t, projector, teacher)
    v = pl.pallas_call(
        functools.partial(main_kernel, inv_npix=1.0 / npix, count=len(arrays)),
        in_specs=[pl.BlockSpec(memory_space=pltpu.SMEM)] + [ANY] * len(arrays),
        out_specs=VMEM,
        out_shape=jax.ShapeDtypeStruct((total, 128), F32),
        scratch_shapes=[
            pltpu.VMEM((3 * chans, (height + 4) * width), BF16),
            pltpu.VMEM((3 * chans, (height + 2) * width), BF16),
            pltpu.VMEM((3 * chans, (height + 4) * width), BF16),
            pltpu.VMEM((chans, (height + 2) * width), F32),
            pltpu.VMEM((chans, pixels), BF16),
            pltpu.VMEM((chans, (height + 2) * width), BF16),
            pltpu.VMEM((9 * chans, 128), F32),
            pltpu.VMEM((ends, chans), F32),
            pltpu.VMEM((ends, pixels), BF16),
            pltpu.SemaphoreType.DMA((len(arrays) - 1 + parts,)),
        ]
        + [pltpu.VMEM(a.shape, a.dtype) for a in arrays],
        compiler_params=grant(60),
        name="block",
    )(flags, *arrays)
    v = sum_all(v)
    gin, gout, gproj = pl.pallas_call(
        unpack_kernel,
        in_specs=[VMEM],
        out_specs=[VMEM] * 3,
        out_shape=[
            jax.ShapeDtypeStruct((9 * chans, chans), F32),
            jax.ShapeDtypeStruct((9 * chans, chans), F32),
            jax.ShapeDtypeStruct((chans, ends), F32),
        ],
        compiler_params=grant(12),
        name="unpack",
    )(v)
    return gin.reshape(9, chans, chans), gout.reshape(9, chans, chans), gproj


def solution(mesh):
    in_specs = (P(None, "row", "col"), P(None, "row", "col"), P(), P(), P())
    out_specs = (P(), P(), P())
    return jax.shard_map(shards, mesh=mesh, in_specs=in_specs, out_specs=out_specs, check_vma=False)
```

time: 280 us -> 96.5 us (0.34)
  waiting for transfers between devices: 153 us -> 39.3 us
  matrix products: 39.7 us -> 0 us
  local copies, waits for them, and re-layouts: 34.2 us -> 5.18 us
  Pallas kernels: 0 us -> 27.1 us
  between operations: 14.5 us -> 0.86 us
  starting transfers between devices: 32.5 us -> 22.7 us
  other arithmetic: 5.01 us -> 1.16 us
    psum x1 -> x0, waiting for transfers between devices: 139 us -> none  [shards(): result = lax.psum((grad_in, grad_out, grad_proj), ('row', 'col'))]
    dot_general x7 -> x0, matrix products: 39.7 us -> none  [the longest x1 9.17 us: shards(): jnp.einsum('khw,ohw->ko', x_taps, dpre, preferred_element_type=jnp.float32)]
    unnamed x46 -> x26, local copies, waits for them, and re-layouts: 31.5 us -> 3.9 us
    pallas_call x0 -> x5, Pallas kernels: none -> 27.1 us  [the longest x1 24.6 us: shards(): pl.pallas_call(functools.partial(main_kernel, inv_npix=1.0 / npix, count=...]
    ppermute x12, waiting for transfers between devices: 14.7 us -> 39.3 us  [the longest x8 33.2 us: swap(): lax.ppermute(v, ('row', 'col'), [(i, i ^ bits[i & 1]) for i in range(n)])]
    ppermute x12, starting transfers between devices: 32.4 us -> 22.7 us  [the longest x8 14 us: swap(): lax.ppermute(v, ('row', 'col'), [(i, i ^ bits[i & 1]) for i in range(n)])]
  transfers between devices with their start and end apart: 13 -> 12, of which waited for: 8 -> 11; matrix products, arithmetic and copies ran while one was open for 9% -> 1% of each run, Pallas kernels for 0% -> 0%
where the time goes in v3:
time: 96.5 us; the launch traced here: 96.3 us
  waiting for transfers between devices  39.3 us (41%)
  Pallas kernels  27.1 us (28%)
  starting transfers between devices  22.7 us (24%)
  local copies, waits for them, and re-layouts  5.18 us (5%)
  other arithmetic  1.16 us (1%)
    ppermute x8, waiting for transfers between devices, swap(): lax.ppermute(v, ('row', 'col'), [(i, i ^ bits[i & 1]) for i in range(n)])  33.2 us
    pallas_call x1, Pallas kernels, shards(): pl.pallas_call(functools.partial(main_kernel, inv_npix=1.0 / npix, count=...  24.6 us
    ppermute x8, starting transfers between devices, swap(): lax.ppermute(v, ('row', 'col'), [(i, i ^ bits[i & 1]) for i in range(n)])  14 us
    ppermute x4, starting transfers between devices, shift(): lax.ppermute(v, axis, [(i, i + by) for i in range(n) if 0 <= i + by < n])  8.71 us
    ppermute x4, waiting for transfers between devices, shift(): lax.ppermute(v, axis, [(i, i + by) for i in range(n) if 0 <= i + by < n])  6.1 us
    unnamed x26, local copies, waits for them, and re-layouts  3.9 us
  transfers between devices with their start and end apart: 12, of which 11 were waited for; matrix products, arithmetic and copies ran while one was open for 1% of the time, Pallas kernels for 0%

profile of v3, /device:TPU:0, one launch (start us, length us, event | category | flops | bytes accessed | tf_op | source)
XLA Modules:
  0.0 96.3 jit_solution(7190278881136850677)
XLA Ops:
  0.7 1.2 %copy-done.2 = bf16[96,16,256]{2,1,0:T(8,128)(2,1)S(1)} copy-done((bf16[96,16,256]{2,1,0:T(8,128)(2,1)S(1)}, bf16[96,16,256]{2,1,0:T(8,128)(2,1)}, u32[]{:S(2)}) %copy-start.2) | copy-done | bytes 786456
  2.1 4.8 %collective-permute-start = (bf16[96,512]{1,0:T(8,128)(2,1)S(1)}, bf16[96,512]{1,0:T(8,128)(2,1)S(1)}, u32[]{:S(2)}, u32[]{:S(2)}) collective-permute-start(bf16[96,512]{1,0:T(8,128)(2,1)S(1)} %get-tuple-element.16), channel_id=1, source_target_pairs={{0,4},{4,8},{8,12},{12,16},{16,20},{20,24},{24,28},{1,5},{5,9},{9,... | collective-permute-start | bytes 294920 | tf_op jit(solution)/shard_map/ppermute | solution.py:303
  6.9 1.3 %collective-permute-start.1 = (bf16[96,512]{1,0:T(8,128)(2,1)S(1)}, bf16[96,512]{1,0:T(8,128)(2,1)S(1)}, u32[]{:S(2)}, u32[]{:S(2)}) collective-permute-start(bf16[96,512]{1,0:T(8,128)(2,1)S(1)} %get-tuple-element.17), channel_id=1, source_target_pairs={{4,0},{8,4},{12,8},{16,12},{20,16},{24,20},{28,24},{5,1},{9,5},{13... | collective-permute-start | bytes 294920 | tf_op jit(solution)/shard_map/ppermute | solution.py:303
  9.1 4.3 %collective-permute-done.1.bot_ref.refs_6_ = bf16[96,512]{1,0:T(8,128)(2,1)S(1)} collective-permute-done((bf16[96,512]{1,0:T(8,128)(2,1)S(1)}, bf16[96,512]{1,0:T(8,128)(2,1)S(1)}, u32[]{:S(2)}, u32[]{:S(2)}) %collective-permute-start.1) | collective-permute-done | bytes 98336 | tf_op jit(solution)/shard_map/ppermute | solution.py:303
  14.6 1.3 %collective-permute-start.2 = (bf16[96,128]{1,0:T(8,128)(2,1)S(1)}, bf16[96,128]{1,0:T(8,128)(2,1)S(1)}, u32[]{:S(2)}, u32[]{:S(2)}) collective-permute-start(bf16[96,128]{1,0:T(8,128)(2,1)S(1)} %get-tuple-element.19), channel_id=1, source_target_pairs={{0,1},{1,2},{2,3},{4,5},{5,6},{6,7},{8,9},{9,10},{10,11},{12,13},{... | collective-permute-start | bytes 73736 | tf_op jit(solution)/shard_map/ppermute | solution.py:303
  15.9 1.3 %collective-permute-start.3 = (bf16[96,128]{1,0:T(8,128)(2,1)S(1)}, bf16[96,128]{1,0:T(8,128)(2,1)S(1)}, u32[]{:S(2)}, u32[]{:S(2)}) collective-permute-start(bf16[96,128]{1,0:T(8,128)(2,1)S(1)} %get-tuple-element.20), channel_id=1, source_target_pairs={{1,0},{2,1},{3,2},{5,4},{6,5},{7,6},{9,8},{10,9},{11,10},{13,12},{... | collective-permute-start | bytes 73736 | tf_op jit(solution)/shard_map/ppermute | solution.py:303
  21.3 24.6 %block.1 = f32[2496,128]{1,0:T(8,128)} custom-call(s32[4]{0:T(128)} %add_convert_fusion.flags, bf16[3,96,864]{2,1,0:T(8,128)(2,1)} %copy-done.3, bf16[96,4096]{1,0:T(8,128)(2,1)} %copy-done, bf16[96,128]{1,0:T(8,128)(2,1)} %copy-done.9, bf16[96,128]{1,0:T(8,128)(2,1)} %copy-done.11, bf16[96,128]{1,0:T(8,128)(2,1)} %copy-done.12, bf16[96,512]{1,0:T(8,128)(2,1)} %copy-done.4, ...), custom_call_target="tpu_custom_call" | custom-call | tf_op jit(solution)/shard_map/block/pallas_call | solution.py:354
  45.9 1.2 %constant_dynamic-slice_fusion.2 = f32[1248,128]{1,0:T(8,128)S(1)} fusion(f32[2496,128]{1,0:T(8,128)} %block.1, s32[]{:T(128)S(6)} %select_n.82), kind=kLoop, calls=%fused_computation.15 | loop fusion | bytes 1277956 | tf_op jit(solution)/shard_map/dynamic_slice | solution.py:289
  47.2 2.6 %collective-permute-start.4 = (f32[1248,128]{1,0:T(8,128)S(1)}, f32[1248,128]{1,0:T(8,128)S(1)}, u32[]{:S(2)}, u32[]{:S(2)}) collective-permute-start(f32[1248,128]{1,0:T(8,128)S(1)} %constant_dynamic-slice_fusion.2), channel_id=1, source_target_pairs={{0,1},{1,0},{2,3},{3,2},{4,5},{5,4},{6,7},{7,6},{8,9},{9,8},{10,11... | collective-permute-start | bytes 1916936 | tf_op jit(solution)/shard_map/ppermute | solution.py:270
  49.8 1.7 %collective-permute-done.4 = f32[1248,128]{1,0:T(8,128)S(1)} collective-permute-done((f32[1248,128]{1,0:T(8,128)S(1)}, f32[1248,128]{1,0:T(8,128)S(1)}, u32[]{:S(2)}, u32[]{:S(2)}) %collective-permute-start.4) | collective-permute-done | bytes 639008 | tf_op jit(solution)/shard_map/ppermute | solution.py:270
  51.6 1.5 %collective-permute-start.5 = (f32[624,128]{1,0:T(8,128)S(1)}, f32[624,128]{1,0:T(8,128)S(1)}, u32[]{:S(2)}, u32[]{:S(2)}) collective-permute-start(f32[624,128]{1,0:T(8,128)S(1)} %constant_dynamic-slice_fusion.1), channel_id=1, source_target_pairs={{0,2},{1,5},{2,0},{3,7},{4,6},{5,1},{6,4},{7,3},{8,10},{9,13},{10,... | collective-permute-start | bytes 958472 | tf_op jit(solution)/shard_map/ppermute | solution.py:270
  53.1 5.6 %collective-permute-done.5 = f32[624,128]{1,0:T(8,128)S(1)} collective-permute-done((f32[624,128]{1,0:T(8,128)S(1)}, f32[624,128]{1,0:T(8,128)S(1)}, u32[]{:S(2)}, u32[]{:S(2)}) %collective-permute-start.5) | collective-permute-done | bytes 319520 | tf_op jit(solution)/shard_map/ppermute | solution.py:270
  58.7 2.5 %collective-permute-start.6 = (f32[312,128]{1,0:T(8,128)S(1)}, f32[312,128]{1,0:T(8,128)S(1)}, u32[]{:S(2)}, u32[]{:S(2)}) collective-permute-start(f32[312,128]{1,0:T(8,128)S(1)} %constant_dynamic-slice_fusion), channel_id=1, source_target_pairs={{0,4},{1,3},{2,6},{3,1},{4,0},{5,7},{6,2},{7,5},{8,12},{9,11},{10,... | collective-permute-start | bytes 479240 | tf_op jit(solution)/shard_map/ppermute | solution.py:270
  61.2 3.3 %collective-permute-done.6 = f32[312,128]{1,0:T(8,128)S(1)} collective-permute-done((f32[312,128]{1,0:T(8,128)S(1)}, f32[312,128]{1,0:T(8,128)S(1)}, u32[]{:S(2)}, u32[]{:S(2)}) %collective-permute-start.6) | collective-permute-done | bytes 159776 | tf_op jit(solution)/shard_map/ppermute | solution.py:270
  64.5 1.6 %collective-permute-start.7 = (f32[312,128]{1,0:T(8,128)S(1)}, f32[312,128]{1,0:T(8,128)S(1)}, u32[]{:S(2)}, u32[]{:S(2)}) collective-permute-start(f32[312,128]{1,0:T(8,128)S(1)} %dynamic-slice_add_fusion.2), channel_id=1, source_target_pairs={{0,8},{1,17},{2,10},{3,19},{4,12},{5,21},{6,14},{7,23},{8,0},{9,25... | collective-permute-start | bytes 479240 | tf_op jit(solution)/shard_map/ppermute | solution.py:270
  66.2 4.3 %collective-permute-done.7 = f32[312,128]{1,0:T(8,128)S(1)} collective-permute-done((f32[312,128]{1,0:T(8,128)S(1)}, f32[312,128]{1,0:T(8,128)S(1)}, u32[]{:S(2)}, u32[]{:S(2)}) %collective-permute-start.7) | collective-permute-done | bytes 159776 | tf_op jit(solution)/shard_map/ppermute | solution.py:270
  70.5 2.1 %collective-permute-start.8 = (f32[312,128]{1,0:T(8,128)S(1)}, f32[312,128]{1,0:T(8,128)S(1)}, u32[]{:S(2)}, u32[]{:S(2)}) collective-permute-start(f32[312,128]{1,0:T(8,128)S(1)} %add.47), channel_id=1, source_target_pairs={{0,16},{1,9},{2,18},{3,11},{4,20},{5,13},{6,22},{7,15},{8,24},{9,1... | collective-permute-start | bytes 479240 | tf_op jit(solution)/shard_map/ppermute | solution.py:270
  72.5 5.9 %collective-permute-done.8 = f32[312,128]{1,0:T(8,128)S(1)} collective-permute-done((f32[312,128]{1,0:T(8,128)S(1)}, f32[312,128]{1,0:T(8,128)S(1)}, u32[]{:S(2)}, u32[]{:S(2)}) %collective-permute-start.8) | collective-permute-done | bytes 159776 | tf_op jit(solution)/shard_map/ppermute | solution.py:270
  78.5 2.1 %collective-permute-start.9 = (f32[312,128]{1,0:T(8,128)S(1)}, f32[312,128]{1,0:T(8,128)S(1)}, u32[]{:S(2)}, u32[]{:S(2)}) collective-permute-start(f32[312,128]{1,0:T(8,128)S(1)} %add.48), channel_id=1, source_target_pairs={{0,4},{1,3},{2,6},{3,1},{4,0},{5,7},{6,2},{7,5},{8,12},{9,11},{10,... | collective-permute-start | bytes 479240 | tf_op jit(solution)/shard_map/ppermute | solution.py:270
  80.5 4.9 %collective-permute-done.9 = f32[312,128]{1,0:T(8,128)S(1)} collective-permute-done((f32[312,128]{1,0:T(8,128)S(1)}, f32[312,128]{1,0:T(8,128)S(1)}, u32[]{:S(2)}, u32[]{:S(2)}) %collective-permute-start.9) | collective-permute-done | bytes 159776 | tf_op jit(solution)/shard_map/ppermute | solution.py:270
  85.5 1.5 %collective-permute-start.10 = (f32[624,128]{1,0:T(8,128)S(1)}, f32[624,128]{1,0:T(8,128)S(1)}, u32[]{:S(2)}, u32[]{:S(2)}) collective-permute-start(f32[624,128]{1,0:T(8,128)S(1)} %pad_maximum_fusion.2), channel_id=1, source_target_pairs={{0,2},{1,5},{2,0},{3,7},{4,6},{5,1},{6,4},{7,3},{8,10},{9,13},{10,... | collective-permute-start | bytes 958472 | tf_op jit(solution)/shard_map/ppermute | solution.py:270
  87.0 5.6 %collective-permute-done.10 = f32[624,128]{1,0:T(8,128)S(1)} collective-permute-done((f32[624,128]{1,0:T(8,128)S(1)}, f32[624,128]{1,0:T(8,128)S(1)}, u32[]{:S(2)}, u32[]{:S(2)}) %collective-permute-start.10) | collective-permute-done | bytes 319520 | tf_op jit(solution)/shard_map/ppermute | solution.py:270
  92.7 2.1 %collective-permute-done.11 = f32[1248,128]{1,0:T(8,128)S(1)} collective-permute-done((f32[1248,128]{1,0:T(8,128)S(1)}, f32[1248,128]{1,0:T(8,128)S(1)}, u32[]{:S(2)}, u32[]{:S(2)}) %collective-permute-start.11) | collective-permute-done | bytes 639008 | tf_op jit(solution)/shard_map/ppermute | solution.py:270
  95.0 1.3 %unpack.1 = (f32[864,96]{1,0:T(8,128)}, f32[864,96]{1,0:T(8,128)}, f32[96,1536]{1,0:T(8,128)}) custom-call(f32[2496,128]{1,0:T(8,128)S(1)} %pad_maximum_fusion.v_ref), custom_call_target="tpu_custom_call" | custom-call | tf_op jit(solution)/shard_map/unpack/pallas_call | solution.py:376
  (46 shorter events, 7.0 us)
Async XLA Ops:
  0.6 17.2 %copy-start.1 = (bf16[96,1536]{1,0:T(8,128)(2,1)S(1)}, bf16[96,1536]{1,0:T(8,128)(2,1)}, u32[]{:S(2)}) copy-start(bf16[96,1536]{1,0:T(8,128)(2,1)} %refs_8_.1) | copy-start | bytes 884740
  0.6 1.2 %copy-start.2 = (bf16[96,16,256]{2,1,0:T(8,128)(2,1)S(1)}, bf16[96,16,256]{2,1,0:T(8,128)(2,1)}, u32[]{:S(2)}) copy-start(bf16[96,16,256]{2,1,0:T(8,128)(2,1)} %x_ref.1) | copy-start | bytes 2359300
  1.8 16.1 %copy-start.7 = (bf16[9,96,96]{2,1,0:T(8,128)(2,1)S(1)}, bf16[9,96,96]{2,1,0:T(8,128)(2,1)}, u32[]{:S(2)}) copy-start(bf16[9,96,96]{2,1,0:T(8,128)(2,1)} %cin_ref.1) | copy-start | bytes 497668
  1.8 16.1 %copy-start.8 = (bf16[9,96,96]{2,1,0:T(8,128)(2,1)S(1)}, bf16[9,96,96]{2,1,0:T(8,128)(2,1)}, u32[]{:S(2)}) copy-start(bf16[9,96,96]{2,1,0:T(8,128)(2,1)} %cout_ref.1) | copy-start | bytes 497668
  2.0 18.7 %copy-start = (bf16[96,4096]{1,0:T(8,128)(2,1)}, bf16[96,4096]{1,0:T(8,128)(2,1)S(1)}, u32[]{:S(2)}) copy-start(bf16[96,4096]{1,0:T(8,128)(2,1)S(1)} %get-tuple-element.15.x2_ref.refs_1_) | copy-start | bytes 2359300
  2.1 7.0 %collective-permute-start = (bf16[96,512]{1,0:T(8,128)(2,1)S(1)}, bf16[96,512]{1,0:T(8,128)(2,1)S(1)}, u32[]{:S(2)}, u32[]{:S(2)}) collective-permute-start(bf16[96,512]{1,0:T(8,128)(2,1)S(1)} %get-tuple-element.16), channel_id=1, source_target_pairs={{0,4},{4,8},{8,12},{12,16},{16,20},{20,24},{24,28},{1,5},{5,9},{9,... | collective-permute-start | bytes 294920 | tf_op jit(solution)/shard_map/ppermute | solution.py:303
  6.9 6.5 %collective-permute-start.1 = (bf16[96,512]{1,0:T(8,128)(2,1)S(1)}, bf16[96,512]{1,0:T(8,128)(2,1)S(1)}, u32[]{:S(2)}, u32[]{:S(2)}) collective-permute-start(bf16[96,512]{1,0:T(8,128)(2,1)S(1)} %get-tuple-element.17), channel_id=1, source_target_pairs={{4,0},{8,4},{12,8},{16,12},{20,16},{24,20},{28,24},{5,1},{9,5},{13... | collective-permute-start | bytes 294920 | tf_op jit(solution)/shard_map/ppermute | solution.py:303
  9.1 11.6 %copy-start.4 = (bf16[96,512]{1,0:T(8,128)(2,1)}, bf16[96,512]{1,0:T(8,128)(2,1)S(1)}, u32[]{:S(2)}) copy-start(bf16[96,512]{1,0:T(8,128)(2,1)S(1)} %collective-permute-done.top_ref.refs_5_) | copy-start | bytes 294916
  13.4 7.3 %copy-start.5 = (bf16[96,512]{1,0:T(8,128)(2,1)}, bf16[96,512]{1,0:T(8,128)(2,1)S(1)}, u32[]{:S(2)}) copy-start(bf16[96,512]{1,0:T(8,128)(2,1)S(1)} %collective-permute-done.1.bot_ref.refs_6_) | copy-start | bytes 294916
  14.6 5.2 %collective-permute-start.2 = (bf16[96,128]{1,0:T(8,128)(2,1)S(1)}, bf16[96,128]{1,0:T(8,128)(2,1)S(1)}, u32[]{:S(2)}, u32[]{:S(2)}) collective-permute-start(bf16[96,128]{1,0:T(8,128)(2,1)S(1)} %get-tuple-element.19), channel_id=1, source_target_pairs={{0,1},{1,2},{2,3},{4,5},{5,6},{6,7},{8,9},{9,10},{10,11},{12,13},{... | collective-permute-start | bytes 73736 | tf_op jit(solution)/shard_map/ppermute | solution.py:303
  15.9 4.8 %collective-permute-start.3 = (bf16[96,128]{1,0:T(8,128)(2,1)S(1)}, bf16[96,128]{1,0:T(8,128)(2,1)S(1)}, u32[]{:S(2)}, u32[]{:S(2)}) collective-permute-start(bf16[96,128]{1,0:T(8,128)(2,1)S(1)} %get-tuple-element.20), channel_id=1, source_target_pairs={{1,0},{2,1},{3,2},{5,4},{6,5},{7,6},{9,8},{10,9},{11,10},{13,12},{... | collective-permute-start | bytes 73736 | tf_op jit(solution)/shard_map/ppermute | solution.py:303
  18.3 0.8 copy-start.3
  19.1 0.7 copy-start.6
  19.8 0.9 copy-start.11
  20.7 0.6 copy-start.12
  45.9 5.6 %copy-start.10 = (f32[2496,128]{1,0:T(8,128)S(1)}, f32[2496,128]{1,0:T(8,128)}, u32[]{:S(2)}) copy-start(f32[2496,128]{1,0:T(8,128)} %block.1) | copy-start | bytes 3833860
  47.2 4.3 %collective-permute-start.4 = (f32[1248,128]{1,0:T(8,128)S(1)}, f32[1248,128]{1,0:T(8,128)S(1)}, u32[]{:S(2)}, u32[]{:S(2)}) collective-permute-start(f32[1248,128]{1,0:T(8,128)S(1)} %constant_dynamic-slice_fusion.2), channel_id=1, source_target_pairs={{0,1},{1,0},{2,3},{3,2},{4,5},{5,4},{6,7},{7,6},{8,9},{9,8},{10,11... | collective-permute-start | bytes 1916936 | tf_op jit(solution)/shard_map/ppermute | solution.py:270
  51.6 7.1 %collective-permute-start.5 = (f32[624,128]{1,0:T(8,128)S(1)}, f32[624,128]{1,0:T(8,128)S(1)}, u32[]{:S(2)}, u32[]{:S(2)}) collective-permute-start(f32[624,128]{1,0:T(8,128)S(1)} %constant_dynamic-slice_fusion.1), channel_id=1, source_target_pairs={{0,2},{1,5},{2,0},{3,7},{4,6},{5,1},{6,4},{7,3},{8,10},{9,13},{10,... | collective-permute-start | bytes 958472 | tf_op jit(solution)/shard_map/ppermute | solution.py:270
  58.7 5.8 %collective-permute-start.6 = (f32[312,128]{1,0:T(8,128)S(1)}, f32[312,128]{1,0:T(8,128)S(1)}, u32[]{:S(2)}, u32[]{:S(2)}) collective-permute-start(f32[312,128]{1,0:T(8,128)S(1)} %constant_dynamic-slice_fusion), channel_id=1, source_target_pairs={{0,4},{1,3},{2,6},{3,1},{4,0},{5,7},{6,2},{7,5},{8,12},{9,11},{10,... | collective-permute-start | bytes 479240 | tf_op jit(solution)/shard_map/ppermute | solution.py:270
  64.5 5.9 %collective-permute-start.7 = (f32[312,128]{1,0:T(8,128)S(1)}, f32[312,128]{1,0:T(8,128)S(1)}, u32[]{:S(2)}, u32[]{:S(2)}) collective-permute-start(f32[312,128]{1,0:T(8,128)S(1)} %dynamic-slice_add_fusion.2), channel_id=1, source_target_pairs={{0,8},{1,17},{2,10},{3,19},{4,12},{5,21},{6,14},{7,23},{8,0},{9,25... | collective-permute-start | bytes 479240 | tf_op jit(solution)/shard_map/ppermute | solution.py:270
  70.5 8.0 %collective-permute-start.8 = (f32[312,128]{1,0:T(8,128)S(1)}, f32[312,128]{1,0:T(8,128)S(1)}, u32[]{:S(2)}, u32[]{:S(2)}) collective-permute-start(f32[312,128]{1,0:T(8,128)S(1)} %add.47), channel_id=1, source_target_pairs={{0,16},{1,9},{2,18},{3,11},{4,20},{5,13},{6,22},{7,15},{8,24},{9,1... | collective-permute-start | bytes 479240 | tf_op jit(solution)/shard_map/ppermute | solution.py:270
  78.5 7.0 %collective-permute-start.9 = (f32[312,128]{1,0:T(8,128)S(1)}, f32[312,128]{1,0:T(8,128)S(1)}, u32[]{:S(2)}, u32[]{:S(2)}) collective-permute-start(f32[312,128]{1,0:T(8,128)S(1)} %add.48), channel_id=1, source_target_pairs={{0,4},{1,3},{2,6},{3,1},{4,0},{5,7},{6,2},{7,5},{8,12},{9,11},{10,... | collective-permute-start | bytes 479240 | tf_op jit(solution)/shard_map/ppermute | solution.py:270
  85.5 7.1 %collective-permute-start.10 = (f32[624,128]{1,0:T(8,128)S(1)}, f32[624,128]{1,0:T(8,128)S(1)}, u32[]{:S(2)}, u32[]{:S(2)}) collective-permute-start(f32[624,128]{1,0:T(8,128)S(1)} %pad_maximum_fusion.2), channel_id=1, source_target_pairs={{0,2},{1,5},{2,0},{3,7},{4,6},{5,1},{6,4},{7,3},{8,10},{9,13},{10,... | collective-permute-start | bytes 958472 | tf_op jit(solution)/shard_map/ppermute | solution.py:270
  92.7 2.1 %collective-permute-start.11 = (f32[1248,128]{1,0:T(8,128)S(1)}, f32[1248,128]{1,0:T(8,128)S(1)}, u32[]{:S(2)}, u32[]{:S(2)}) collective-permute-start(f32[1248,128]{1,0:T(8,128)S(1)} %pad_maximum_fusion.1), channel_id=1, source_target_pairs={{0,1},{1,0},{2,3},{3,2},{4,5},{5,4},{6,7},{7,6},{8,9},{9,8},{10,11... | collective-permute-start | bytes 1916936 | tf_op jit(solution)/shard_map/ppermute | solution.py:270
  (1 other events, 0.6 us)

commit v4 on v3

--- a/solution.py
+++ b/solution.py
@@ -85,7 +85,7 @@
 
 def main_kernel(flags, *refs, inv_npix, count):
     hbm, refs = refs[:count], refs[count:]
-    out_ref, x3, h3, d3, grad, s2, dpre2, wide, gp, tr, sem, *refs = refs
+    out_ref, x3, h3, d3, grad, s2, dpre2, ds2, wide, gp, tr, sem, *refs = refs
     parts = sem.shape[0] - count + 1
     copies = [
         pltpu.make_async_copy(a, b, sem.at[i]) for i, (a, b) in enumerate(zip(hbm[:-1], refs))
@@ -165,6 +165,12 @@
             seg = bot_ref[:, (r - height - 2) * width : (r - height - 1) * width]
         put(x3, r, seg, strip, r * PITCH + 1)
 
+    def teach(k):
+        pieces[k].wait()
+        rows = jnp.swapaxes(t_ref[k * step : (k + 1) * step], 0, 1)
+        for h in range(height):
+            tr[k * step : (k + 1) * step, h * width : (h + 1) * width] = rows[h]
+
     for r in range(height + 2):
         hid, slope = gelu_and_slope(dot(kin, rows3(x3, r)))
         if r == 0:
@@ -178,12 +184,8 @@
         span = slice(r * width, (r + 1) * width)
         seg = x2_ref[:, span].astype(F32)
         s2[:, span] = (seg + dot(kout, rows3(h3, r))).astype(BF16)
-
-    for k in range(parts):
-        pieces[k].wait()
-        rows = jnp.swapaxes(t_ref[k * step : (k + 1) * step], 0, 1)
-        for h in range(height):
-            tr[k * step : (k + 1) * step, h * width : (h + 1) * width] = rows[h]
+        if r % 2 == 1 and r < 12:
+            teach(r // 2)
 
     for c in copies[-2:]:
         c.wait()
@@ -192,41 +194,58 @@
     d3[:, : 2 * width] = rim
     d3[:, (height + 2) * width :] = rim
     ds_s = jnp.zeros((chans, 128), F32)
-    for r in range(height):
-        span = slice(r * width, (r + 1) * width)
-        stud = s2[:, span]
-        pred = dot(proj_t, stud)
-        dpred = ((pred - tr[:, span].astype(F32)) * inv_npix).astype(BF16)
-        cross = dot_nt(dpred, stud)
-        if r == 0:
+    group = width
+    count = pixels // group
+
+    def predict(k):
+        return dot(proj_t, s2[:, k * group : (k + 1) * group])
+
+    pred = predict(0)
+    for k in range(count):
+        span = slice(k * group, (k + 1) * group)
+        following = predict(min(k + 1, count - 1))
+        dpred = (pred - tr[:, span].astype(F32)).astype(BF16)
+        cross = dot_nt(dpred, s2[:, span])
+        if k == 0:
             gp[...] = cross
         else:
             gp[...] += cross
-        ds = dot(proj, dpred).astype(BF16)
-        put(d3, r + 2, ds, None, 0)
-        at = (r + 2) * PITCH
-        ds32 = ds.astype(F32)
-        ds_s = jnp.where(lane == at + 2, roll(ds32[:, :128], at + 2), ds_s)
-        ds_s = jnp.where(lane == at + RIGHT, roll(ds32[:, width - 128 :], at + RIGHT - 127), ds_s)
+        ds_k = (dot(proj, dpred) * inv_npix).astype(BF16)
+        pred = following
+        for r in range(k * group // width, (k + 1) * group // width):
+            at = r * width - k * group
+            ds = ds_k[:, at : at + width]
+            put(d3, r + 2, ds, None, 0)
+            ds2[:chans, r * width : (r + 1) * width] = ds
+            ds2[chans:, (r + 1) * width : (r + 2) * width] = ds
+            at = (r + 2) * PITCH
+            ds32 = ds.astype(F32)
+            ds_s = jnp.where(lane == at + 2, roll(ds32[:, :128], at + 2), ds_s)
+            ds_s = jnp.where(lane == at + RIGHT, roll(ds32[:, width - 128 :], at + RIGHT - 127), ds_s)
+
+    blank = jnp.zeros((chans, width), BF16)
+    for pair, last in ((dpre2, height + 2), (ds2, height)):
+        pair[:chans, last * width :] = blank
+        pair[chans:, :width] = blank
 
     for r in range(height + 2):
         span = slice(r * width, (r + 1) * width)
-        dpre2[:, span] = (dot(kback, rows3(d3, r)) * grad[:, span]).astype(BF16)
+        dpre = (dot(kback, rows3(d3, r)) * grad[:, span]).astype(BF16)
+        dpre2[:chans, span] = dpre
+        dpre2[chans:, (r + 1) * width : (r + 2) * width] = dpre
     dpre_s = (dot(kback, taps(ds_s)) * grad_s).astype(BF16)
 
     per = 3 * chans
     quarter = 9 * chans // 4
     piece = chans // 3
     lane_q = lanes_of((quarter, 128))
-    for n in range(2):
-        for a in range(3):
-            base = a * width
+    for n, (src, pair) in enumerate(((x3, dpre2), (h3, ds2))):
+        size = pair.shape[1]
+        both = dot_nt(src[:, :size], pair[...])
+        third = dot_nt(src[:, 2 * width : width + size], pair[:chans, : size - width])
+        for a, g in enumerate((both[:, :chans], both[:, chans:], third)):
             if n == 0:
-                g = dot_nt(x3[:, base : base + pixels + 2 * width], dpre2[...])
                 g += dot_nt(strip_taps[a * per : (a + 1) * per], dpre_s)
-            else:
-                grads = d3[chans : 2 * chans, 2 * width : 2 * width + pixels]
-                g = dot_nt(h3[:, base : base + pixels], grads)
             wide[a * per : (a + 1) * per, :chans] = g
         for k in range(3):
             at = (3 * n + k) * quarter
@@ -237,7 +256,7 @@
     start = 6 * quarter
     for j in range(ends // 128):
         at = start + j * chans
-        out_ref[at : at + chans, :] = gp[j * 128 : (j + 1) * 128, :].T
+        out_ref[at : at + chans, :] = gp[j * 128 : (j + 1) * 128, :].T * inv_npix
     end = start + ends // 128 * chans
     out_ref[end:, :] = jnp.zeros((out_ref.shape[0] - end, 128), F32)
 
@@ -362,14 +381,15 @@
             pltpu.VMEM((3 * chans, (height + 4) * width), BF16),
             pltpu.VMEM((chans, (height + 2) * width), F32),
             pltpu.VMEM((chans, pixels), BF16),
-            pltpu.VMEM((chans, (height + 2) * width), BF16),
+            pltpu.VMEM((2 * chans, (height + 3) * width), BF16),
+            pltpu.VMEM((2 * chans, (height + 1) * width), BF16),
             pltpu.VMEM((9 * chans, 128), F32),
             pltpu.VMEM((ends, chans), F32),
             pltpu.VMEM((ends, pixels), BF16),
             pltpu.SemaphoreType.DMA((len(arrays) - 1 + parts,)),
         ]
         + [pltpu.VMEM(a.shape, a.dtype) for a in arrays],
-        compiler_params=grant(60),
+        compiler_params=grant(48),
         name="block",
     )(flags, *arrays)
     v = sum_all(v)

time: 96.5 us -> 89.7 us (0.930)
  Pallas kernels: 27.1 us -> 23.1 us
  local copies, waits for them, and re-layouts: 5.18 us -> 1.29 us
  waiting for transfers between devices: 39.3 us -> 42.1 us
  starting transfers between devices: 22.7 us -> 21.5 us
    pallas_call x1, Pallas kernels: 24.6 us -> 20.6 us  [shards(): pl.pallas_call(functools.partial(main_kernel, inv_npix=1.0 / npix, count=...]
    unnamed x26 -> x8, local copies, waits for them, and re-layouts: 3.9 us -> 1.18 us
    ppermute x4, waiting for transfers between devices: 6.1 us -> 8.23 us  [shift(): lax.ppermute(v, axis, [(i, i + by) for i in range(n) if 0 <= i + by < n])]
    dynamic_slice x3, local copies, waits for them, and re-layouts: 1.28 us -> 0.11 us  [sum_all(): give = lax.dynamic_slice_in_dim(v, (1 - mine) * half, half, 0)]
    ppermute x8, starting transfers between devices: 14 us -> 12.8 us  [swap(): lax.ppermute(v, ('row', 'col'), [(i, i ^ bits[i & 1]) for i in range(n)])]
  transfers between devices with their start and end apart: 12 -> 12, of which waited for: 11 -> 11; matrix products, arithmetic and copies ran while one was open for 1% -> 0% of each run, Pallas kernels for 0% -> 0%
where the time goes in v4:
time: 89.7 us; the launch traced here: 89.4 us
  waiting for transfers between devices  42.1 us (47%)
  Pallas kernels  23.1 us (26%)
  starting transfers between devices  21.5 us (24%)
  local copies, waits for them, and re-layouts  1.29 us (1%)
    ppermute x8, waiting for transfers between devices, swap(): lax.ppermute(v, ('row', 'col'), [(i, i ^ bits[i & 1]) for i in range(n)])  33.9 us
    pallas_call x1, Pallas kernels, shards(): pl.pallas_call(functools.partial(main_kernel, inv_npix=1.0 / npix, count=...  20.6 us
    ppermute x8, starting transfers between devices, swap(): lax.ppermute(v, ('row', 'col'), [(i, i ^ bits[i & 1]) for i in range(n)])  12.8 us
    ppermute x4, starting transfers between devices, shift(): lax.ppermute(v, axis, [(i, i + by) for i in range(n) if 0 <= i + by < n])  8.72 us
    ppermute x4, waiting for transfers between devices, shift(): lax.ppermute(v, axis, [(i, i + by) for i in range(n) if 0 <= i + by < n])  8.23 us
  transfers between devices with their start and end apart: 12, of which 11 were waited for; matrix products, arithmetic and copies ran while one was open for 0% of the time, Pallas kernels for 0%

profile of v4, /device:TPU:0, one launch (start us, length us, event | category | flops | bytes accessed | tf_op | source)
XLA Modules:
  0.0 89.4 jit_solution(5244477217277349097)
XLA Ops:
  0.7 1.2 %copy-done.1 = bf16[96,16,256]{2,1,0:T(8,128)(2,1)S(1)} copy-done((bf16[96,16,256]{2,1,0:T(8,128)(2,1)S(1)}, bf16[96,16,256]{2,1,0:T(8,128)(2,1)}, u32[]{:S(2)}) %copy-start.1) | copy-done | bytes 786456
  2.0 4.8 %collective-permute-start = (bf16[96,512]{1,0:T(8,128)(2,1)S(1)}, bf16[96,512]{1,0:T(8,128)(2,1)S(1)}, u32[]{:S(2)}, u32[]{:S(2)}) collective-permute-start(bf16[96,512]{1,0:T(8,128)(2,1)S(1)} %get-tuple-element.16), channel_id=1, source_target_pairs={{0,4},{4,8},{8,12},{12,16},{16,20},{20,24},{24,28},{1,5},{5,9},{9,... | collective-permute-start | bytes 294920 | tf_op jit(solution)/shard_map/ppermute | solution.py:322
  6.9 1.3 %collective-permute-start.1 = (bf16[96,512]{1,0:T(8,128)(2,1)S(1)}, bf16[96,512]{1,0:T(8,128)(2,1)S(1)}, u32[]{:S(2)}, u32[]{:S(2)}) collective-permute-start(bf16[96,512]{1,0:T(8,128)(2,1)S(1)} %get-tuple-element.17), channel_id=1, source_target_pairs={{4,0},{8,4},{12,8},{16,12},{20,16},{24,20},{28,24},{5,1},{9,5},{13... | collective-permute-start | bytes 294920 | tf_op jit(solution)/shard_map/ppermute | solution.py:322
  8.2 0.9 collective-permute-done.top_ref.refs_5_
  9.1 4.3 %collective-permute-done.1.bot_ref.refs_6_ = bf16[96,512]{1,0:T(8,128)(2,1)S(1)} collective-permute-done((bf16[96,512]{1,0:T(8,128)(2,1)S(1)}, bf16[96,512]{1,0:T(8,128)(2,1)S(1)}, u32[]{:S(2)}, u32[]{:S(2)}) %collective-permute-start.1) | collective-permute-done | bytes 98336 | tf_op jit(solution)/shard_map/ppermute | solution.py:322
  13.4 0.6 strips.1
  14.0 1.3 %collective-permute-start.2 = (bf16[96,128]{1,0:T(8,128)(2,1)S(1)}, bf16[96,128]{1,0:T(8,128)(2,1)S(1)}, u32[]{:S(2)}, u32[]{:S(2)}) collective-permute-start(bf16[96,128]{1,0:T(8,128)(2,1)S(1)} %get-tuple-element.19), channel_id=1, source_target_pairs={{0,1},{1,2},{2,3},{4,5},{5,6},{6,7},{8,9},{9,10},{10,11},{12,13},{... | collective-permute-start | bytes 73736 | tf_op jit(solution)/shard_map/ppermute | solution.py:322
  15.3 1.3 %collective-permute-start.3 = (bf16[96,128]{1,0:T(8,128)(2,1)S(1)}, bf16[96,128]{1,0:T(8,128)(2,1)S(1)}, u32[]{:S(2)}, u32[]{:S(2)}) collective-permute-start(bf16[96,128]{1,0:T(8,128)(2,1)S(1)} %get-tuple-element.20), channel_id=1, source_target_pairs={{1,0},{2,1},{3,2},{5,4},{6,5},{7,6},{9,8},{10,9},{11,10},{13,12},{... | collective-permute-start | bytes 73736 | tf_op jit(solution)/shard_map/ppermute | solution.py:322
  17.1 3.0 %collective-permute-done.3.refs_4_ = bf16[96,128]{1,0:T(8,128)(2,1)S(1)} collective-permute-done((bf16[96,128]{1,0:T(8,128)(2,1)S(1)}, bf16[96,128]{1,0:T(8,128)(2,1)S(1)}, u32[]{:S(2)}, u32[]{:S(2)}) %collective-permute-start.3) | collective-permute-done | bytes 24608 | tf_op jit(solution)/shard_map/ppermute | solution.py:322
  20.1 20.6 %block.1 = f32[2496,128]{1,0:T(8,128)S(1)} custom-call(s32[4]{0:T(128)S(1)} %add_convert_fusion.flags, bf16[3,96,864]{2,1,0:T(8,128)(2,1)S(1)} %get-tuple-element.14.refs_0_, bf16[96,4096]{1,0:T(8,128)(2,1)S(1)} %get-tuple-element.15.x2_ref.refs_1_, bf16[96,128]{1,0:T(8,128)(2,1)S(1)} %get-tuple-element.18.refs_2_, ...), custom_call_target="tpu_custom_call" | custom-call | tf_op jit(solution)/shard_map/block/pallas_call | solution.py:373
  40.8 2.6 %collective-permute-start.4 = (f32[1248,128]{1,0:T(8,128)S(1)}, f32[1248,128]{1,0:T(8,128)S(1)}, u32[]{:S(2)}, u32[]{:S(2)}) collective-permute-start(f32[1248,128]{1,0:T(8,128)S(1)} %constant_dynamic-slice_fusion.2), channel_id=1, source_target_pairs={{0,1},{1,0},{2,3},{3,2},{4,5},{5,4},{6,7},{7,6},{8,9},{9,8},{10,11... | collective-permute-start | bytes 1916936 | tf_op jit(solution)/shard_map/ppermute | solution.py:289
  43.4 1.7 %collective-permute-done.4 = f32[1248,128]{1,0:T(8,128)S(1)} collective-permute-done((f32[1248,128]{1,0:T(8,128)S(1)}, f32[1248,128]{1,0:T(8,128)S(1)}, u32[]{:S(2)}, u32[]{:S(2)}) %collective-permute-start.4) | collective-permute-done | bytes 639008 | tf_op jit(solution)/shard_map/ppermute | solution.py:289
  45.6 6.7 %collective-permute-done.5 = f32[624,128]{1,0:T(8,128)S(1)} collective-permute-done((f32[624,128]{1,0:T(8,128)S(1)}, f32[624,128]{1,0:T(8,128)S(1)}, u32[]{:S(2)}, u32[]{:S(2)}) %collective-permute-start.5) | collective-permute-done | bytes 319520 | tf_op jit(solution)/shard_map/ppermute | solution.py:289
  52.4 2.5 %collective-permute-start.6 = (f32[312,128]{1,0:T(8,128)S(1)}, f32[312,128]{1,0:T(8,128)S(1)}, u32[]{:S(2)}, u32[]{:S(2)}) collective-permute-start(f32[312,128]{1,0:T(8,128)S(1)} %constant_dynamic-slice_fusion), channel_id=1, source_target_pairs={{0,4},{1,3},{2,6},{3,1},{4,0},{5,7},{6,2},{7,5},{8,12},{9,11},{10,... | collective-permute-start | bytes 479240 | tf_op jit(solution)/shard_map/ppermute | solution.py:289
  54.9 3.3 %collective-permute-done.6 = f32[312,128]{1,0:T(8,128)S(1)} collective-permute-done((f32[312,128]{1,0:T(8,128)S(1)}, f32[312,128]{1,0:T(8,128)S(1)}, u32[]{:S(2)}, u32[]{:S(2)}) %collective-permute-start.6) | collective-permute-done | bytes 159776 | tf_op jit(solution)/shard_map/ppermute | solution.py:289
  58.2 1.6 %collective-permute-start.7 = (f32[312,128]{1,0:T(8,128)S(1)}, f32[312,128]{1,0:T(8,128)S(1)}, u32[]{:S(2)}, u32[]{:S(2)}) collective-permute-start(f32[312,128]{1,0:T(8,128)S(1)} %dynamic-slice_add_fusion.2), channel_id=1, source_target_pairs={{0,8},{1,17},{2,10},{3,19},{4,12},{5,21},{6,14},{7,23},{8,0},{9,25... | collective-permute-start | bytes 479240 | tf_op jit(solution)/shard_map/ppermute | solution.py:289
  59.8 3.7 %collective-permute-done.7 = f32[312,128]{1,0:T(8,128)S(1)} collective-permute-done((f32[312,128]{1,0:T(8,128)S(1)}, f32[312,128]{1,0:T(8,128)S(1)}, u32[]{:S(2)}, u32[]{:S(2)}) %collective-permute-start.7) | collective-permute-done | bytes 159776 | tf_op jit(solution)/shard_map/ppermute | solution.py:289
  63.5 2.6 %collective-permute-start.8 = (f32[312,128]{1,0:T(8,128)S(1)}, f32[312,128]{1,0:T(8,128)S(1)}, u32[]{:S(2)}, u32[]{:S(2)}) collective-permute-start(f32[312,128]{1,0:T(8,128)S(1)} %add.47), channel_id=1, source_target_pairs={{0,16},{1,9},{2,18},{3,11},{4,20},{5,13},{6,22},{7,15},{8,24},{9,1... | collective-permute-start | bytes 479240 | tf_op jit(solution)/shard_map/ppermute | solution.py:289
  66.2 5.4 %collective-permute-done.8 = f32[312,128]{1,0:T(8,128)S(1)} collective-permute-done((f32[312,128]{1,0:T(8,128)S(1)}, f32[312,128]{1,0:T(8,128)S(1)}, u32[]{:S(2)}, u32[]{:S(2)}) %collective-permute-start.8) | collective-permute-done | bytes 159776 | tf_op jit(solution)/shard_map/ppermute | solution.py:289
  71.6 2.6 %collective-permute-start.9 = (f32[312,128]{1,0:T(8,128)S(1)}, f32[312,128]{1,0:T(8,128)S(1)}, u32[]{:S(2)}, u32[]{:S(2)}) collective-permute-start(f32[312,128]{1,0:T(8,128)S(1)} %add.48), channel_id=1, source_target_pairs={{0,4},{1,3},{2,6},{3,1},{4,0},{5,7},{6,2},{7,5},{8,12},{9,11},{10,... | collective-permute-start | bytes 479240 | tf_op jit(solution)/shard_map/ppermute | solution.py:289
  74.2 4.4 %collective-permute-done.9 = f32[312,128]{1,0:T(8,128)S(1)} collective-permute-done((f32[312,128]{1,0:T(8,128)S(1)}, f32[312,128]{1,0:T(8,128)S(1)}, u32[]{:S(2)}, u32[]{:S(2)}) %collective-permute-start.9) | collective-permute-done | bytes 159776 | tf_op jit(solution)/shard_map/ppermute | solution.py:289
  79.0 6.7 %collective-permute-done.10 = f32[624,128]{1,0:T(8,128)S(1)} collective-permute-done((f32[624,128]{1,0:T(8,128)S(1)}, f32[624,128]{1,0:T(8,128)S(1)}, u32[]{:S(2)}, u32[]{:S(2)}) %collective-permute-start.10) | collective-permute-done | bytes 319520 | tf_op jit(solution)/shard_map/ppermute | solution.py:289
  85.9 2.1 %collective-permute-done.11 = f32[1248,128]{1,0:T(8,128)S(1)} collective-permute-done((f32[1248,128]{1,0:T(8,128)S(1)}, f32[1248,128]{1,0:T(8,128)S(1)}, u32[]{:S(2)}, u32[]{:S(2)}) %collective-permute-start.11) | collective-permute-done | bytes 639008 | tf_op jit(solution)/shard_map/ppermute | solution.py:289
  88.1 1.3 %unpack.1 = (f32[864,96]{1,0:T(8,128)}, f32[864,96]{1,0:T(8,128)}, f32[96,1536]{1,0:T(8,128)}) custom-call(f32[2496,128]{1,0:T(8,128)S(1)} %pad_maximum_fusion.v_ref), custom_call_target="tpu_custom_call" | custom-call | tf_op jit(solution)/shard_map/unpack/pallas_call | solution.py:396
  (28 shorter events, 2.1 us)
Async XLA Ops:
  0.6 16.0 %copy-start = (bf16[96,1536]{1,0:T(8,128)(2,1)S(1)}, bf16[96,1536]{1,0:T(8,128)(2,1)}, u32[]{:S(2)}) copy-start(bf16[96,1536]{1,0:T(8,128)(2,1)} %refs_8_.1) | copy-start | bytes 884740
  0.6 1.2 %copy-start.1 = (bf16[96,16,256]{2,1,0:T(8,128)(2,1)S(1)}, bf16[96,16,256]{2,1,0:T(8,128)(2,1)}, u32[]{:S(2)}) copy-start(bf16[96,16,256]{2,1,0:T(8,128)(2,1)} %x_ref.1) | copy-start | bytes 2359300
  1.8 14.9 %copy-start.2 = (bf16[9,96,96]{2,1,0:T(8,128)(2,1)S(1)}, bf16[9,96,96]{2,1,0:T(8,128)(2,1)}, u32[]{:S(2)}) copy-start(bf16[9,96,96]{2,1,0:T(8,128)(2,1)} %cin_ref.1) | copy-start | bytes 497668
  1.8 14.9 %copy-start.3 = (bf16[9,96,96]{2,1,0:T(8,128)(2,1)S(1)}, bf16[9,96,96]{2,1,0:T(8,128)(2,1)}, u32[]{:S(2)}) copy-start(bf16[9,96,96]{2,1,0:T(8,128)(2,1)} %cout_ref.1) | copy-start | bytes 497668
  2.0 7.0 %collective-permute-start = (bf16[96,512]{1,0:T(8,128)(2,1)S(1)}, bf16[96,512]{1,0:T(8,128)(2,1)S(1)}, u32[]{:S(2)}, u32[]{:S(2)}) collective-permute-start(bf16[96,512]{1,0:T(8,128)(2,1)S(1)} %get-tuple-element.16), channel_id=1, source_target_pairs={{0,4},{4,8},{8,12},{12,16},{16,20},{20,24},{24,28},{1,5},{5,9},{9,... | collective-permute-start | bytes 294920 | tf_op jit(solution)/shard_map/ppermute | solution.py:322
  6.9 6.5 %collective-permute-start.1 = (bf16[96,512]{1,0:T(8,128)(2,1)S(1)}, bf16[96,512]{1,0:T(8,128)(2,1)S(1)}, u32[]{:S(2)}, u32[]{:S(2)}) collective-permute-start(bf16[96,512]{1,0:T(8,128)(2,1)S(1)} %get-tuple-element.17), channel_id=1, source_target_pairs={{4,0},{8,4},{12,8},{16,12},{20,16},{24,20},{28,24},{5,1},{9,5},{13... | collective-permute-start | bytes 294920 | tf_op jit(solution)/shard_map/ppermute | solution.py:322
  14.0 3.1 %collective-permute-start.2 = (bf16[96,128]{1,0:T(8,128)(2,1)S(1)}, bf16[96,128]{1,0:T(8,128)(2,1)S(1)}, u32[]{:S(2)}, u32[]{:S(2)}) collective-permute-start(bf16[96,128]{1,0:T(8,128)(2,1)S(1)} %get-tuple-element.19), channel_id=1, source_target_pairs={{0,1},{1,2},{2,3},{4,5},{5,6},{6,7},{8,9},{9,10},{10,11},{12,13},{... | collective-permute-start | bytes 73736 | tf_op jit(solution)/shard_map/ppermute | solution.py:322
  15.3 4.8 %collective-permute-start.3 = (bf16[96,128]{1,0:T(8,128)(2,1)S(1)}, bf16[96,128]{1,0:T(8,128)(2,1)S(1)}, u32[]{:S(2)}, u32[]{:S(2)}) collective-permute-start(bf16[96,128]{1,0:T(8,128)(2,1)S(1)} %get-tuple-element.20), channel_id=1, source_target_pairs={{1,0},{2,1},{3,2},{5,4},{6,5},{7,6},{9,8},{10,9},{11,10},{13,12},{... | collective-permute-start | bytes 73736 | tf_op jit(solution)/shard_map/ppermute | solution.py:322
  40.8 4.3 %collective-permute-start.4 = (f32[1248,128]{1,0:T(8,128)S(1)}, f32[1248,128]{1,0:T(8,128)S(1)}, u32[]{:S(2)}, u32[]{:S(2)}) collective-permute-start(f32[1248,128]{1,0:T(8,128)S(1)} %constant_dynamic-slice_fusion.2), channel_id=1, source_target_pairs={{0,1},{1,0},{2,3},{3,2},{4,5},{5,4},{6,7},{7,6},{8,9},{9,8},{10,11... | collective-permute-start | bytes 1916936 | tf_op jit(solution)/shard_map/ppermute | solution.py:289
  45.2 7.1 %collective-permute-start.5 = (f32[624,128]{1,0:T(8,128)S(1)}, f32[624,128]{1,0:T(8,128)S(1)}, u32[]{:S(2)}, u32[]{:S(2)}) collective-permute-start(f32[624,128]{1,0:T(8,128)S(1)} %constant_dynamic-slice_fusion.1), channel_id=1, source_target_pairs={{0,2},{1,5},{2,0},{3,7},{4,6},{5,1},{6,4},{7,3},{8,10},{9,13},{10,... | collective-permute-start | bytes 958472 | tf_op jit(solution)/shard_map/ppermute | solution.py:289
  52.4 5.8 %collective-permute-start.6 = (f32[312,128]{1,0:T(8,128)S(1)}, f32[312,128]{1,0:T(8,128)S(1)}, u32[]{:S(2)}, u32[]{:S(2)}) collective-permute-start(f32[312,128]{1,0:T(8,128)S(1)} %constant_dynamic-slice_fusion), channel_id=1, source_target_pairs={{0,4},{1,3},{2,6},{3,1},{4,0},{5,7},{6,2},{7,5},{8,12},{9,11},{10,... | collective-permute-start | bytes 479240 | tf_op jit(solution)/shard_map/ppermute | solution.py:289
  58.2 5.4 %collective-permute-start.7 = (f32[312,128]{1,0:T(8,128)S(1)}, f32[312,128]{1,0:T(8,128)S(1)}, u32[]{:S(2)}, u32[]{:S(2)}) collective-permute-start(f32[312,128]{1,0:T(8,128)S(1)} %dynamic-slice_add_fusion.2), channel_id=1, source_target_pairs={{0,8},{1,17},{2,10},{3,19},{4,12},{5,21},{6,14},{7,23},{8,0},{9,25... | collective-permute-start | bytes 479240 | tf_op jit(solution)/shard_map/ppermute | solution.py:289
  63.5 8.0 %collective-permute-start.8 = (f32[312,128]{1,0:T(8,128)S(1)}, f32[312,128]{1,0:T(8,128)S(1)}, u32[]{:S(2)}, u32[]{:S(2)}) collective-permute-start(f32[312,128]{1,0:T(8,128)S(1)} %add.47), channel_id=1, source_target_pairs={{0,16},{1,9},{2,18},{3,11},{4,20},{5,13},{6,22},{7,15},{8,24},{9,1... | collective-permute-start | bytes 479240 | tf_op jit(solution)/shard_map/ppermute | solution.py:289
  71.6 7.0 %collective-permute-start.9 = (f32[312,128]{1,0:T(8,128)S(1)}, f32[312,128]{1,0:T(8,128)S(1)}, u32[]{:S(2)}, u32[]{:S(2)}) collective-permute-start(f32[312,128]{1,0:T(8,128)S(1)} %add.48), channel_id=1, source_target_pairs={{0,4},{1,3},{2,6},{3,1},{4,0},{5,7},{6,2},{7,5},{8,12},{9,11},{10,... | collective-permute-start | bytes 479240 | tf_op jit(solution)/shard_map/ppermute | solution.py:289
  78.7 7.1 %collective-permute-start.10 = (f32[624,128]{1,0:T(8,128)S(1)}, f32[624,128]{1,0:T(8,128)S(1)}, u32[]{:S(2)}, u32[]{:S(2)}) collective-permute-start(f32[624,128]{1,0:T(8,128)S(1)} %pad_maximum_fusion.2), channel_id=1, source_target_pairs={{0,2},{1,5},{2,0},{3,7},{4,6},{5,1},{6,4},{7,3},{8,10},{9,13},{10,... | collective-permute-start | bytes 958472 | tf_op jit(solution)/shard_map/ppermute | solution.py:289
  85.8 2.1 %collective-permute-start.11 = (f32[1248,128]{1,0:T(8,128)S(1)}, f32[1248,128]{1,0:T(8,128)S(1)}, u32[]{:S(2)}, u32[]{:S(2)}) collective-permute-start(f32[1248,128]{1,0:T(8,128)S(1)} %pad_maximum_fusion.1), channel_id=1, source_target_pairs={{0,1},{1,0},{2,3},{3,2},{4,5},{5,4},{6,7},{7,6},{8,9},{9,8},{10,11... | collective-permute-start | bytes 1916936 | tf_op jit(solution)/shard_map/ppermute | solution.py:289

commit v5 on v4

--- a/solution.py
+++ b/solution.py
@@ -126,6 +126,7 @@
     halo_l, halo_r = ls_ref[...].astype(F32), roll(rs_ref[...].astype(F32), RIGHT)
     strip = jnp.where(lane < RIGHT, jnp.where(col < 2, halo_l, 0.0), jnp.where(col > 0, halo_r, 0.0))
     strip = jnp.where(part < (height + 4) * PITCH, strip, 0.0) + own_ref[...].astype(F32)
+    strip16 = strip.astype(BF16)
     strip_taps = taps(strip)
     lane1 = lanes_of((1, 128))
     part1 = lax.rem(lane1, RIGHT)
@@ -133,23 +134,20 @@
     mask = jnp.where(lane1 < RIGHT, mask * has_l, mask * has_r)
     mask = jnp.where((lax.rem(part1, PITCH) == 0) & (part1 < (height + 2) * PITCH), mask, 0.0)
     hid_s, grad_s = gelu_and_slope(dot(kin, strip_taps))
-    hid_s = (hid_s * mask).astype(BF16).astype(F32)
+    hid_s = (hid_s * mask).astype(BF16)
     grad_s = grad_s * mask
 
     def put(dst, r, seg, rim, at):
         lo, hi = r * width, (r + 1) * width
-        seg32 = seg.astype(F32)
-        ahead = roll(seg32, 1)
-        first = roll(rim, -at) if rim is not None else 0.0
-        first = jnp.where(lane == 0, first, ahead[:, :128])
-        dst[0:chans, lo : lo + 128] = first.astype(BF16)
-        dst[0:chans, lo + 128 : hi] = ahead[:, 128:].astype(BF16)
+        ahead = roll(seg, 1)
+        first = roll(rim, -at) if rim is not None else jnp.zeros((chans, 128), BF16)
+        dst[0:chans, lo : lo + 128] = jnp.where(lane == 0, first, ahead[:, :128])
+        dst[0:chans, lo + 128 : hi] = ahead[:, 128:]
         dst[chans : 2 * chans, lo:hi] = seg
-        back = roll(seg32, -1)
-        last = roll(rim, 127 - RIGHT - at) if rim is not None else 0.0
-        last = jnp.where(lane == 127, last, back[:, width - 128 :])
-        dst[2 * chans :, lo : hi - 128] = back[:, : width - 128].astype(BF16)
-        dst[2 * chans :, hi - 128 : hi] = last.astype(BF16)
+        back = roll(seg, -1)
+        last = roll(rim, 127 - RIGHT - at) if rim is not None else jnp.zeros((chans, 128), BF16)
+        dst[2 * chans :, lo : hi - 128] = back[:, : width - 128]
+        dst[2 * chans :, hi - 128 : hi] = jnp.where(lane == 127, last, back[:, width - 128 :])
 
     def rows3(src, r):
         return jnp.concatenate(
@@ -163,7 +161,7 @@
             seg = x2_ref[:, (r - 2) * width : (r - 1) * width]
         else:
             seg = bot_ref[:, (r - height - 2) * width : (r - height - 1) * width]
-        put(x3, r, seg, strip, r * PITCH + 1)
+        put(x3, r, seg, strip16, r * PITCH + 1)
 
     def teach(k):
         pieces[k].wait()
@@ -284,37 +282,37 @@
     return pltpu.CompilerParams(vmem_limit_bytes=mib << 20)
 
 
-def swap(v, bits):
+def swap(v, bits, other=None):
     n = lax.axis_size("row") * lax.axis_size("col")
-    return lax.ppermute(v, ("row", "col"), [(i, i ^ bits[i & 1]) for i in range(n)])
+    pick = (bits, bits if other is None else other)
+    return lax.ppermute(v, ("row", "col"), [(i, i ^ pick[i & 1]) for i in range(n)])
 
 
 def sum_all(v):
     me = lax.axis_index("row") * lax.axis_size("col") + lax.axis_index("col")
     n = lax.axis_size("row") * lax.axis_size("col")
-    bits = [1 << k for k in range(1, n.bit_length() - 1)]
-    steps = [(1, 1)]
-    for k in range(len(bits)):
-        other = k ^ 1 if k ^ 1 < len(bits) else k
-        steps.append((bits[k], bits[other]))
-    halved, rest = steps[:3], steps[3:]
-
-    def upper(pair):
-        return (me & jnp.where(me % 2 == 0, pair[0], pair[1])) != 0
-
-    for pair in halved:
-        mine = upper(pair).astype(jnp.int32)
-        half = v.shape[0] // 2
-        give = lax.dynamic_slice_in_dim(v, (1 - mine) * half, half, 0)
-        keep = lax.dynamic_slice_in_dim(v, mine * half, half, 0)
-        v = keep + swap(give, pair)
-    for pair in rest:
-        v = v + swap(v, pair)
-    for pair in halved[::-1]:
-        got = swap(v, pair)
-        top = upper(pair)
-        v = jnp.concatenate([jnp.where(top, got, v), jnp.where(top, v, got)], 0)
-    return v
+
+    def rows_of(v, parts, k):
+        size = v.shape[0] // parts
+        return lax.dynamic_slice_in_dim(v, k * size, size, 0)
+
+    core, chip = me & 1, (me >> 1) & 3
+    v = rows_of(v, 2, core) + swap(rows_of(v, 2, 1 - core), 1)
+    got = [swap(rows_of(v, 4, chip ^ k), k << 1) for k in (1, 2, 3)]
+    v = ((rows_of(v, 4, chip) + got[0]) + got[1]) + got[2]
+    rest = [1 << k for k in range(3, n.bit_length() - 1)]
+    for bits, other in zip(rest, rest[::-1]):
+        v = v + swap(v, bits, other)
+    got = [v] + [swap(v, k << 1) for k in (1, 2, 3)]
+    pieces = []
+    for q in range(4):
+        piece = got[3]
+        for k in range(3):
+            piece = jnp.where(chip ^ q == k, got[k], piece)
+        pieces.append(piece)
+    v = jnp.concatenate(pieces, 0)
+    other = swap(v, 1)
+    return jnp.concatenate([jnp.where(core == 0, v, other), jnp.where(core == 0, other, v)], 0)
 
 
 def shift(v, axis, by):

time: 89.7 us -> 83.9 us (0.935)
  waiting for transfers between devices: 42.1 us -> 35.4 us
  starting transfers between devices: 21.5 us -> 22.8 us
    ppermute x8 -> x10, waiting for transfers between devices: 33.9 us -> 27.2 us  [swap(): lax.ppermute(v, ('row', 'col'), [(i, i ^ pick[i & 1]) for i in range(n)])]
    ppermute x8 -> x10, starting transfers between devices: 12.8 us -> 14.1 us  [swap(): lax.ppermute(v, ('row', 'col'), [(i, i ^ pick[i & 1]) for i in range(n)])]
  transfers between devices with their start and end apart: 12 -> 14, of which waited for: 11 -> 12; matrix products, arithmetic and copies ran while one was open for 0% -> 0% of each run, Pallas kernels for 0% -> 0%
where the time goes in v5:
time: 83.9 us; the launch traced here: 83.7 us
  waiting for transfers between devices  35.4 us (42%)
  Pallas kernels  22.9 us (27%)
  starting transfers between devices  22.8 us (27%)
  local copies, waits for them, and re-layouts  1.28 us (2%)
    ppermute x10, waiting for transfers between devices, swap(): lax.ppermute(v, ('row', 'col'), [(i, i ^ pick[i & 1]) for i in range(n)])  27.2 us
    pallas_call x1, Pallas kernels, shards(): pl.pallas_call(functools.partial(main_kernel, inv_npix=1.0 / npix, count=...  20.4 us
    ppermute x10, starting transfers between devices, swap(): lax.ppermute(v, ('row', 'col'), [(i, i ^ pick[i & 1]) for i in range(n)])  14.1 us
    ppermute x4, starting transfers between devices, shift(): lax.ppermute(v, axis, [(i, i + by) for i in range(n) if 0 <= i + by < n])  8.72 us
    ppermute x4, waiting for transfers between devices, shift(): lax.ppermute(v, axis, [(i, i + by) for i in range(n) if 0 <= i + by < n])  8.23 us
  transfers between devices with their start and end apart: 14, of which 12 were waited for; matrix products, arithmetic and copies ran while one was open for 0% of the time, Pallas kernels for 0%

profile of v5, /device:TPU:0, one launch (start us, length us, event | category | flops | bytes accessed | tf_op | source)
XLA Modules:
  0.0 83.7 jit_solution(5932069708461514202)
XLA Ops:
  2.0 4.8 %collective-permute-start = (bf16[96,512]{1,0:T(8,128)(2,1)S(1)}, bf16[96,512]{1,0:T(8,128)(2,1)S(1)}, u32[]{:S(2)}, u32[]{:S(2)}) collective-permute-start(bf16[96,512]{1,0:T(8,128)(2,1)S(1)} %get-tuple-element.16), channel_id=1, source_target_pairs={{0,4},{4,8},{8,12},{12,16},{16,20},{20,24},{24,28},{1,5},{5,9},{9,... | collective-permute-start | bytes 294920 | tf_op jit(solution)/shard_map/ppermute | solution.py:320
  6.9 1.3 %collective-permute-start.1 = (bf16[96,512]{1,0:T(8,128)(2,1)S(1)}, bf16[96,512]{1,0:T(8,128)(2,1)S(1)}, u32[]{:S(2)}, u32[]{:S(2)}) collective-permute-start(bf16[96,512]{1,0:T(8,128)(2,1)S(1)} %get-tuple-element.17), channel_id=1, source_target_pairs={{4,0},{8,4},{12,8},{16,12},{20,16},{24,20},{28,24},{5,1},{9,5},{13... | collective-permute-start | bytes 294920 | tf_op jit(solution)/shard_map/ppermute | solution.py:320
  9.1 4.3 %collective-permute-done.1.bot_ref.refs_6_ = bf16[96,512]{1,0:T(8,128)(2,1)S(1)} collective-permute-done((bf16[96,512]{1,0:T(8,128)(2,1)S(1)}, bf16[96,512]{1,0:T(8,128)(2,1)S(1)}, u32[]{:S(2)}, u32[]{:S(2)}) %collective-permute-start.1) | collective-permute-done | bytes 98336 | tf_op jit(solution)/shard_map/ppermute | solution.py:320
  14.0 1.3 %collective-permute-start.2 = (bf16[96,128]{1,0:T(8,128)(2,1)S(1)}, bf16[96,128]{1,0:T(8,128)(2,1)S(1)}, u32[]{:S(2)}, u32[]{:S(2)}) collective-permute-start(bf16[96,128]{1,0:T(8,128)(2,1)S(1)} %get-tuple-element.19), channel_id=1, source_target_pairs={{0,1},{1,2},{2,3},{4,5},{5,6},{6,7},{8,9},{9,10},{10,11},{12,13},{... | collective-permute-start | bytes 73736 | tf_op jit(solution)/shard_map/ppermute | solution.py:320
  15.3 1.3 %collective-permute-start.3 = (bf16[96,128]{1,0:T(8,128)(2,1)S(1)}, bf16[96,128]{1,0:T(8,128)(2,1)S(1)}, u32[]{:S(2)}, u32[]{:S(2)}) collective-permute-start(bf16[96,128]{1,0:T(8,128)(2,1)S(1)} %get-tuple-element.20), channel_id=1, source_target_pairs={{1,0},{2,1},{3,2},{5,4},{6,5},{7,6},{9,8},{10,9},{11,10},{13,12},{... | collective-permute-start | bytes 73736 | tf_op jit(solution)/shard_map/ppermute | solution.py:320
  17.1 3.0 %collective-permute-done.3.refs_4_ = bf16[96,128]{1,0:T(8,128)(2,1)S(1)} collective-permute-done((bf16[96,128]{1,0:T(8,128)(2,1)S(1)}, bf16[96,128]{1,0:T(8,128)(2,1)S(1)}, u32[]{:S(2)}, u32[]{:S(2)}) %collective-permute-start.3) | collective-permute-done | bytes 24608 | tf_op jit(solution)/shard_map/ppermute | solution.py:320
  20.1 20.4 %block.1 = f32[2496,128]{1,0:T(8,128)S(1)} custom-call(s32[4]{0:T(128)S(1)} %add_convert_fusion.flags, bf16[3,96,864]{2,1,0:T(8,128)(2,1)S(1)} %get-tuple-element.14.refs_0_, bf16[96,4096]{1,0:T(8,128)(2,1)S(1)} %get-tuple-element.15.x2_ref.refs_1_, bf16[96,128]{1,0:T(8,128)(2,1)S(1)} %get-tuple-element.18.refs_2_, ...), custom_call_target="tpu_custom_call" | custom-call | tf_op jit(solution)/shard_map/block/pallas_call | solution.py:371
  40.6 2.6 %collective-permute-start.4 = (f32[1248,128]{1,0:T(8,128)S(1)}, f32[1248,128]{1,0:T(8,128)S(1)}, u32[]{:S(2)}, u32[]{:S(2)}) collective-permute-start(f32[1248,128]{1,0:T(8,128)S(1)} %constant_dynamic-slice_fusion.3), channel_id=1, source_target_pairs={{0,1},{1,0},{2,3},{3,2},{4,5},{5,4},{6,7},{7,6},{8,9},{9,8},{10,11... | collective-permute-start | bytes 1916936 | tf_op jit(solution)/shard_map/ppermute | solution.py:288
  43.2 1.7 %collective-permute-done.4 = f32[1248,128]{1,0:T(8,128)S(1)} collective-permute-done((f32[1248,128]{1,0:T(8,128)S(1)}, f32[1248,128]{1,0:T(8,128)S(1)}, u32[]{:S(2)}, u32[]{:S(2)}) %collective-permute-start.4) | collective-permute-done | bytes 639008 | tf_op jit(solution)/shard_map/ppermute | solution.py:288
  45.4 2.5 %collective-permute-start.6 = (f32[312,128]{1,0:T(8,128)S(1)}, f32[312,128]{1,0:T(8,128)S(1)}, u32[]{:S(2)}, u32[]{:S(2)}) collective-permute-start(f32[312,128]{1,0:T(8,128)S(1)} %get-tuple-element.33), channel_id=1, source_target_pairs={{0,4},{1,5},{2,6},{3,7},{4,0},{5,1},{6,2},{7,3},{8,12},{9,13},{10,... | collective-permute-start | bytes 479240 | tf_op jit(solution)/shard_map/ppermute | solution.py:288
  47.9 1.2 %collective-permute-start.7 = (f32[312,128]{1,0:T(8,128)S(1)}, f32[312,128]{1,0:T(8,128)S(1)}, u32[]{:S(2)}, u32[]{:S(2)}) collective-permute-start(f32[312,128]{1,0:T(8,128)S(1)} %get-tuple-element.32), channel_id=1, source_target_pairs={{0,6},{1,7},{2,4},{3,5},{4,2},{5,3},{6,0},{7,1},{8,14},{9,15},{10,... | collective-permute-start | bytes 479240 | tf_op jit(solution)/shard_map/ppermute | solution.py:288
  49.0 2.5 %collective-permute-done.5 = f32[312,128]{1,0:T(8,128)S(1)} collective-permute-done((f32[312,128]{1,0:T(8,128)S(1)}, f32[312,128]{1,0:T(8,128)S(1)}, u32[]{:S(2)}, u32[]{:S(2)}) %collective-permute-start.5) | collective-permute-done | bytes 159776 | tf_op jit(solution)/shard_map/ppermute | solution.py:288
  51.5 1.2 %collective-permute-done.6 = f32[312,128]{1,0:T(8,128)S(1)} collective-permute-done((f32[312,128]{1,0:T(8,128)S(1)}, f32[312,128]{1,0:T(8,128)S(1)}, u32[]{:S(2)}, u32[]{:S(2)}) %collective-permute-start.6) | collective-permute-done | bytes 159776 | tf_op jit(solution)/shard_map/ppermute | solution.py:288
  52.7 4.1 %collective-permute-done.7 = f32[312,128]{1,0:T(8,128)S(1)} collective-permute-done((f32[312,128]{1,0:T(8,128)S(1)}, f32[312,128]{1,0:T(8,128)S(1)}, u32[]{:S(2)}, u32[]{:S(2)}) %collective-permute-start.7) | collective-permute-done | bytes 159776 | tf_op jit(solution)/shard_map/ppermute | solution.py:288
  56.9 1.6 %collective-permute-start.8 = (f32[312,128]{1,0:T(8,128)S(1)}, f32[312,128]{1,0:T(8,128)S(1)}, u32[]{:S(2)}, u32[]{:S(2)}) collective-permute-start(f32[312,128]{1,0:T(8,128)S(1)} %add_add_fusion), channel_id=1, source_target_pairs={{0,8},{1,17},{2,10},{3,19},{4,12},{5,21},{6,14},{7,23},{8,0},{9,25... | collective-permute-start | bytes 479240 | tf_op jit(solution)/shard_map/ppermute | solution.py:288
  58.5 4.4 %collective-permute-done.8 = f32[312,128]{1,0:T(8,128)S(1)} collective-permute-done((f32[312,128]{1,0:T(8,128)S(1)}, f32[312,128]{1,0:T(8,128)S(1)}, u32[]{:S(2)}, u32[]{:S(2)}) %collective-permute-start.8) | collective-permute-done | bytes 159776 | tf_op jit(solution)/shard_map/ppermute | solution.py:288
  62.9 2.2 %collective-permute-start.9 = (f32[312,128]{1,0:T(8,128)S(1)}, f32[312,128]{1,0:T(8,128)S(1)}, u32[]{:S(2)}, u32[]{:S(2)}) collective-permute-start(f32[312,128]{1,0:T(8,128)S(1)} %add.50), channel_id=1, source_target_pairs={{0,16},{1,9},{2,18},{3,11},{4,20},{5,13},{6,22},{7,15},{8,24},{9,1... | collective-permute-start | bytes 479240 | tf_op jit(solution)/shard_map/ppermute | solution.py:288
  65.1 4.2 %collective-permute-done.9 = f32[312,128]{1,0:T(8,128)S(1)} collective-permute-done((f32[312,128]{1,0:T(8,128)S(1)}, f32[312,128]{1,0:T(8,128)S(1)}, u32[]{:S(2)}, u32[]{:S(2)}) %collective-permute-start.9) | collective-permute-done | bytes 159776 | tf_op jit(solution)/shard_map/ppermute | solution.py:288
  69.3 1.4 %collective-permute-start.10 = (f32[312,128]{1,0:T(8,128)S(1)}, f32[312,128]{1,0:T(8,128)S(1)}, u32[]{:S(2)}, u32[]{:S(2)}) collective-permute-start(f32[312,128]{1,0:T(8,128)S(1)} %add.51), channel_id=1, source_target_pairs={{0,4},{1,5},{2,6},{3,7},{4,0},{5,1},{6,2},{7,3},{8,12},{9,13},{10,... | collective-permute-start | bytes 479240 | tf_op jit(solution)/shard_map/ppermute | solution.py:288
  71.2 1.7 %collective-permute-start.12 = (f32[312,128]{1,0:T(8,128)S(1)}, f32[312,128]{1,0:T(8,128)S(1)}, u32[]{:S(2)}, u32[]{:S(2)}) collective-permute-start(f32[312,128]{1,0:T(8,128)S(1)} %add.51), channel_id=1, source_target_pairs={{0,6},{1,7},{2,4},{3,5},{4,2},{5,3},{6,0},{7,1},{8,14},{9,15},{10,... | collective-permute-start | bytes 479240 | tf_op jit(solution)/shard_map/ppermute | solution.py:288
  72.9 3.5 %collective-permute-done.10 = f32[312,128]{1,0:T(8,128)S(1)} collective-permute-done((f32[312,128]{1,0:T(8,128)S(1)}, f32[312,128]{1,0:T(8,128)S(1)}, u32[]{:S(2)}, u32[]{:S(2)}) %collective-permute-start.10) | collective-permute-done | bytes 159776 | tf_op jit(solution)/shard_map/ppermute | solution.py:288
  76.3 3.6 %collective-permute-done.11 = f32[312,128]{1,0:T(8,128)S(1)} collective-permute-done((f32[312,128]{1,0:T(8,128)S(1)}, f32[312,128]{1,0:T(8,128)S(1)}, u32[]{:S(2)}, u32[]{:S(2)}) %collective-permute-start.11) | collective-permute-done | bytes 159776 | tf_op jit(solution)/shard_map/ppermute | solution.py:288
  80.1 2.1 %collective-permute-done.13 = f32[1248,128]{1,0:T(8,128)S(1)} collective-permute-done((f32[1248,128]{1,0:T(8,128)S(1)}, f32[1248,128]{1,0:T(8,128)S(1)}, u32[]{:S(2)}, u32[]{:S(2)}) %collective-permute-start.13) | collective-permute-done | bytes 639008 | tf_op jit(solution)/shard_map/ppermute | solution.py:288
  82.4 1.3 %unpack.1 = (f32[864,96]{1,0:T(8,128)}, f32[864,96]{1,0:T(8,128)}, f32[96,1536]{1,0:T(8,128)}) custom-call(f32[2496,128]{1,0:T(8,128)S(1)} %pad_maximum_fusion.v_ref), custom_call_target="tpu_custom_call" | custom-call | tf_op jit(solution)/shard_map/unpack/pallas_call | solution.py:394
  (28 shorter events, 4.8 us)
Async XLA Ops:
  0.6 16.0 %copy-start = (bf16[96,1536]{1,0:T(8,128)(2,1)S(1)}, bf16[96,1536]{1,0:T(8,128)(2,1)}, u32[]{:S(2)}) copy-start(bf16[96,1536]{1,0:T(8,128)(2,1)} %refs_8_.1) | copy-start | bytes 884740
  0.6 1.2 %copy-start.1 = (bf16[96,16,256]{2,1,0:T(8,128)(2,1)S(1)}, bf16[96,16,256]{2,1,0:T(8,128)(2,1)}, u32[]{:S(2)}) copy-start(bf16[96,16,256]{2,1,0:T(8,128)(2,1)} %x_ref.1) | copy-start | bytes 2359300
  1.8 14.9 %copy-start.2 = (bf16[9,96,96]{2,1,0:T(8,128)(2,1)S(1)}, bf16[9,96,96]{2,1,0:T(8,128)(2,1)}, u32[]{:S(2)}) copy-start(bf16[9,96,96]{2,1,0:T(8,128)(2,1)} %cin_ref.1) | copy-start | bytes 497668
  1.8 14.9 %copy-start.3 = (bf16[9,96,96]{2,1,0:T(8,128)(2,1)S(1)}, bf16[9,96,96]{2,1,0:T(8,128)(2,1)}, u32[]{:S(2)}) copy-start(bf16[9,96,96]{2,1,0:T(8,128)(2,1)} %cout_ref.1) | copy-start | bytes 497668
  2.0 7.0 %collective-permute-start = (bf16[96,512]{1,0:T(8,128)(2,1)S(1)}, bf16[96,512]{1,0:T(8,128)(2,1)S(1)}, u32[]{:S(2)}, u32[]{:S(2)}) collective-permute-start(bf16[96,512]{1,0:T(8,128)(2,1)S(1)} %get-tuple-element.16), channel_id=1, source_target_pairs={{0,4},{4,8},{8,12},{12,16},{16,20},{20,24},{24,28},{1,5},{5,9},{9,... | collective-permute-start | bytes 294920 | tf_op jit(solution)/shard_map/ppermute | solution.py:320
  6.9 6.5 %collective-permute-start.1 = (bf16[96,512]{1,0:T(8,128)(2,1)S(1)}, bf16[96,512]{1,0:T(8,128)(2,1)S(1)}, u32[]{:S(2)}, u32[]{:S(2)}) collective-permute-start(bf16[96,512]{1,0:T(8,128)(2,1)S(1)} %get-tuple-element.17), channel_id=1, source_target_pairs={{4,0},{8,4},{12,8},{16,12},{20,16},{24,20},{28,24},{5,1},{9,5},{13... | collective-permute-start | bytes 294920 | tf_op jit(solution)/shard_map/ppermute | solution.py:320
  14.0 3.1 %collective-permute-start.2 = (bf16[96,128]{1,0:T(8,128)(2,1)S(1)}, bf16[96,128]{1,0:T(8,128)(2,1)S(1)}, u32[]{:S(2)}, u32[]{:S(2)}) collective-permute-start(bf16[96,128]{1,0:T(8,128)(2,1)S(1)} %get-tuple-element.19), channel_id=1, source_target_pairs={{0,1},{1,2},{2,3},{4,5},{5,6},{6,7},{8,9},{9,10},{10,11},{12,13},{... | collective-permute-start | bytes 73736 | tf_op jit(solution)/shard_map/ppermute | solution.py:320
  15.3 4.8 %collective-permute-start.3 = (bf16[96,128]{1,0:T(8,128)(2,1)S(1)}, bf16[96,128]{1,0:T(8,128)(2,1)S(1)}, u32[]{:S(2)}, u32[]{:S(2)}) collective-permute-start(bf16[96,128]{1,0:T(8,128)(2,1)S(1)} %get-tuple-element.20), channel_id=1, source_target_pairs={{1,0},{2,1},{3,2},{5,4},{6,5},{7,6},{9,8},{10,9},{11,10},{13,12},{... | collective-permute-start | bytes 73736 | tf_op jit(solution)/shard_map/ppermute | solution.py:320
  40.6 4.3 %collective-permute-start.4 = (f32[1248,128]{1,0:T(8,128)S(1)}, f32[1248,128]{1,0:T(8,128)S(1)}, u32[]{:S(2)}, u32[]{:S(2)}) collective-permute-start(f32[1248,128]{1,0:T(8,128)S(1)} %constant_dynamic-slice_fusion.3), channel_id=1, source_target_pairs={{0,1},{1,0},{2,3},{3,2},{4,5},{5,4},{6,7},{7,6},{8,9},{9,8},{10,11... | collective-permute-start | bytes 1916936 | tf_op jit(solution)/shard_map/ppermute | solution.py:288
  45.1 6.5 %collective-permute-start.5 = (f32[312,128]{1,0:T(8,128)S(1)}, f32[312,128]{1,0:T(8,128)S(1)}, u32[]{:S(2)}, u32[]{:S(2)}) collective-permute-start(f32[312,128]{1,0:T(8,128)S(1)} %get-tuple-element.31), channel_id=1, source_target_pairs={{0,2},{1,3},{2,0},{3,1},{4,6},{5,7},{6,4},{7,5},{8,10},{9,11},{10,... | collective-permute-start | bytes 479240 | tf_op jit(solution)/shard_map/ppermute | solution.py:288
  45.4 7.3 %collective-permute-start.6 = (f32[312,128]{1,0:T(8,128)S(1)}, f32[312,128]{1,0:T(8,128)S(1)}, u32[]{:S(2)}, u32[]{:S(2)}) collective-permute-start(f32[312,128]{1,0:T(8,128)S(1)} %get-tuple-element.33), channel_id=1, source_target_pairs={{0,4},{1,5},{2,6},{3,7},{4,0},{5,1},{6,2},{7,3},{8,12},{9,13},{10,... | collective-permute-start | bytes 479240 | tf_op jit(solution)/shard_map/ppermute | solution.py:288
  47.9 9.0 %collective-permute-start.7 = (f32[312,128]{1,0:T(8,128)S(1)}, f32[312,128]{1,0:T(8,128)S(1)}, u32[]{:S(2)}, u32[]{:S(2)}) collective-permute-start(f32[312,128]{1,0:T(8,128)S(1)} %get-tuple-element.32), channel_id=1, source_target_pairs={{0,6},{1,7},{2,4},{3,5},{4,2},{5,3},{6,0},{7,1},{8,14},{9,15},{10,... | collective-permute-start | bytes 479240 | tf_op jit(solution)/shard_map/ppermute | solution.py:288
  56.9 6.0 %collective-permute-start.8 = (f32[312,128]{1,0:T(8,128)S(1)}, f32[312,128]{1,0:T(8,128)S(1)}, u32[]{:S(2)}, u32[]{:S(2)}) collective-permute-start(f32[312,128]{1,0:T(8,128)S(1)} %add_add_fusion), channel_id=1, source_target_pairs={{0,8},{1,17},{2,10},{3,19},{4,12},{5,21},{6,14},{7,23},{8,0},{9,25... | collective-permute-start | bytes 479240 | tf_op jit(solution)/shard_map/ppermute | solution.py:288
  62.9 6.4 %collective-permute-start.9 = (f32[312,128]{1,0:T(8,128)S(1)}, f32[312,128]{1,0:T(8,128)S(1)}, u32[]{:S(2)}, u32[]{:S(2)}) collective-permute-start(f32[312,128]{1,0:T(8,128)S(1)} %add.50), channel_id=1, source_target_pairs={{0,16},{1,9},{2,18},{3,11},{4,20},{5,13},{6,22},{7,15},{8,24},{9,1... | collective-permute-start | bytes 479240 | tf_op jit(solution)/shard_map/ppermute | solution.py:288
  69.3 7.0 %collective-permute-start.10 = (f32[312,128]{1,0:T(8,128)S(1)}, f32[312,128]{1,0:T(8,128)S(1)}, u32[]{:S(2)}, u32[]{:S(2)}) collective-permute-start(f32[312,128]{1,0:T(8,128)S(1)} %add.51), channel_id=1, source_target_pairs={{0,4},{1,5},{2,6},{3,7},{4,0},{5,1},{6,2},{7,3},{8,12},{9,13},{10,... | collective-permute-start | bytes 479240 | tf_op jit(solution)/shard_map/ppermute | solution.py:288
  70.7 9.2 %collective-permute-start.11 = (f32[312,128]{1,0:T(8,128)S(1)}, f32[312,128]{1,0:T(8,128)S(1)}, u32[]{:S(2)}, u32[]{:S(2)}) collective-permute-start(f32[312,128]{1,0:T(8,128)S(1)} %add.51), channel_id=1, source_target_pairs={{0,2},{1,3},{2,0},{3,1},{4,6},{5,7},{6,4},{7,5},{8,10},{9,11},{10,... | collective-permute-start | bytes 479240 | tf_op jit(solution)/shard_map/ppermute | solution.py:288
  71.2 8.7 %collective-permute-start.12 = (f32[312,128]{1,0:T(8,128)S(1)}, f32[312,128]{1,0:T(8,128)S(1)}, u32[]{:S(2)}, u32[]{:S(2)}) collective-permute-start(f32[312,128]{1,0:T(8,128)S(1)} %add.51), channel_id=1, source_target_pairs={{0,6},{1,7},{2,4},{3,5},{4,2},{5,3},{6,0},{7,1},{8,14},{9,15},{10,... | collective-permute-start | bytes 479240 | tf_op jit(solution)/shard_map/ppermute | solution.py:288
  80.0 2.1 %collective-permute-start.13 = (f32[1248,128]{1,0:T(8,128)S(1)}, f32[1248,128]{1,0:T(8,128)S(1)}, u32[]{:S(2)}, u32[]{:S(2)}) collective-permute-start(f32[1248,128]{1,0:T(8,128)S(1)} %pad_maximum_fusion.1), channel_id=1, source_target_pairs={{0,1},{1,0},{2,3},{3,2},{4,5},{5,4},{6,7},{7,6},{8,9},{9,8},{10,11... | collective-permute-start | bytes 1916936 | tf_op jit(solution)/shard_map/ppermute | solution.py:288

commit v6 on v5

--- a/solution.py
+++ b/solution.py
@@ -52,29 +52,37 @@
         dn_ref[:, h * width : (h + 1) * width] = rows[height - 2 + h]
 
 
-def strip_kernel(x2_ref, top_ref, bot_ref, ml_ref, mr_ref, own_ref):
+def strip_row(left, right, own, first, last, at, lane):
+    left = jnp.where((lane >= at + 1) & (lane < at + 3), roll(first, at + 1), left)
+    right = jnp.where((lane >= at) & (lane < at + 2), roll(last, at - 126), right)
+    own = jnp.where(lane == at + 2, roll(first, at + 2), own)
+    own = jnp.where(lane == at + RIGHT, roll(last, at + RIGHT - 127), own)
+    return left, right, own
+
+
+def own_kernel(x2_ref, part_ref, *, width):
     chans = x2_ref.shape[0]
+    lane = lanes_of((chans, 128))
+    strips = (jnp.zeros((chans, 128), BF16),) * 3
+    for r in range(x2_ref.shape[1] // width):
+        first = x2_ref[:, r * width : r * width + 128]
+        last = x2_ref[:, (r + 1) * width - 128 : (r + 1) * width]
+        strips = strip_row(*strips, first, last, (r + 2) * PITCH, lane)
+    for k in range(3):
+        part_ref[k] = strips[k]
+
+
+def strip_kernel(part_ref, top_ref, bot_ref, ml_ref, mr_ref, own_ref, *, height):
     width = top_ref.shape[1] // 2
-    height = x2_ref.shape[1] // width
-    lane = lanes_of((chans, 128))
-    left = right = own = jnp.zeros((chans, 128), F32)
-    for r in range(height + 4):
-        if r < 2:
-            ref, base = top_ref, r * width
-        elif r < height + 2:
-            ref, base = x2_ref, (r - 2) * width
-        else:
-            ref, base = bot_ref, (r - height - 2) * width
-        first = ref[:, base : base + 128].astype(F32)
-        last = ref[:, base + width - 128 : base + width].astype(F32)
-        at = r * PITCH
-        left = jnp.where((lane >= at + 1) & (lane < at + 3), roll(first, at + 1), left)
-        right = jnp.where((lane >= at) & (lane < at + 2), roll(last, at - 126), right)
-        own = jnp.where(lane == at + 2, roll(first, at + 2), own)
-        own = jnp.where(lane == at + RIGHT, roll(last, at + RIGHT - 127), own)
-    ml_ref[...] = left.astype(BF16)
-    mr_ref[...] = right.astype(BF16)
-    own_ref[...] = own.astype(BF16)
+    lane = lanes_of((part_ref.shape[1], 128))
+    strips = (part_ref[0], part_ref[1], part_ref[2])
+    for r in range(2):
+        for ref, at in ((top_ref, r * PITCH), (bot_ref, (height + 2 + r) * PITCH)):
+            first = ref[:, r * width : r * width + 128]
+            last = ref[:, (r + 1) * width - 128 : (r + 1) * width]
+            strips = strip_row(*strips, first, last, at, lane)
+    for ref, v in zip((ml_ref, mr_ref, own_ref), strips):
+        ref[...] = v
 
 
 def gelu_and_slope(pre):
@@ -350,14 +358,22 @@
         compiler_params=grant(8),
         name="weights",
     )(conv_in, conv_out, projector)
+    part = pl.pallas_call(
+        functools.partial(own_kernel, width=width),
+        in_specs=[VMEM],
+        out_specs=VMEM,
+        out_shape=jax.ShapeDtypeStruct((3, chans, 128), BF16),
+        compiler_params=grant(8),
+        name="own",
+    )(x2)
     ml, mr, own = pl.pallas_call(
-        strip_kernel,
+        functools.partial(strip_kernel, height=height),
         in_specs=[VMEM] * 3,
         out_specs=[VMEM] * 3,
         out_shape=[jax.ShapeDtypeStruct((chans, 128), BF16)] * 3,
         compiler_params=grant(8),
         name="strips",
-    )(x2, top, bot)
+    )(part, top, bot)
     rs = shift(ml, "col", -1)
     ls = shift(mr, "col", 1)
     row, col = lax.axis_index("row"), lax.axis_index("col")

time: 83.9 us -> 83.5 us (level)
  transfers between devices with their start and end apart: 14 -> 14, of which waited for: 12 -> 12; matrix products, arithmetic and copies ran while one was open for 0% -> 0% of each run, Pallas kernels for 0% -> 1%
where the time goes in v6:
time: 83.5 us; the launch traced here: 83.3 us
  waiting for transfers between devices  34.9 us (42%)
  Pallas kernels  23 us (28%)
  starting transfers between devices  22.8 us (27%)
  local copies, waits for them, and re-layouts  1.28 us (2%)
    ppermute x10, waiting for transfers between devices, swap(): lax.ppermute(v, ('row', 'col'), [(i, i ^ pick[i & 1]) for i in range(n)])  27.2 us
    pallas_call x1, Pallas kernels, shards(): pl.pallas_call(functools.partial(main_kernel, inv_npix=1.0 / npix, count=...  20.4 us
    ppermute x10, starting transfers between devices, swap(): lax.ppermute(v, ('row', 'col'), [(i, i ^ pick[i & 1]) for i in range(n)])  14.1 us
    ppermute x4, starting transfers between devices, shift(): lax.ppermute(v, axis, [(i, i + by) for i in range(n) if 0 <= i + by < n])  8.72 us
    ppermute x4, waiting for transfers between devices, shift(): lax.ppermute(v, axis, [(i, i + by) for i in range(n) if 0 <= i + by < n])  7.74 us
  transfers between devices with their start and end apart: 14, of which 12 were waited for; matrix products, arithmetic and copies ran while one was open for 0% of the time, Pallas kernels for 1%

profile of v6, /device:TPU:0, one launch (start us, length us, event | category | flops | bytes accessed | tf_op | source)
XLA Modules:
  0.0 83.3 jit_solution(16975096701701421521)
XLA Ops:
  2.0 4.8 %collective-permute-start = (bf16[96,512]{1,0:T(8,128)(2,1)S(1)}, bf16[96,512]{1,0:T(8,128)(2,1)S(1)}, u32[]{:S(2)}, u32[]{:S(2)}) collective-permute-start(bf16[96,512]{1,0:T(8,128)(2,1)S(1)} %get-tuple-element.16), channel_id=1, source_target_pairs={{0,4},{4,8},{8,12},{12,16},{16,20},{20,24},{24,28},{1,5},{5,9},{9,... | collective-permute-start | bytes 294920 | tf_op jit(solution)/shard_map/ppermute | solution.py:328
  6.9 1.3 %collective-permute-start.1 = (bf16[96,512]{1,0:T(8,128)(2,1)S(1)}, bf16[96,512]{1,0:T(8,128)(2,1)S(1)}, u32[]{:S(2)}, u32[]{:S(2)}) collective-permute-start(bf16[96,512]{1,0:T(8,128)(2,1)S(1)} %get-tuple-element.17), channel_id=1, source_target_pairs={{4,0},{8,4},{12,8},{16,12},{20,16},{24,20},{28,24},{5,1},{9,5},{13... | collective-permute-start | bytes 294920 | tf_op jit(solution)/shard_map/ppermute | solution.py:328
  9.1 4.3 %collective-permute-done.1.bot_ref.refs_6_ = bf16[96,512]{1,0:T(8,128)(2,1)S(1)} collective-permute-done((bf16[96,512]{1,0:T(8,128)(2,1)S(1)}, bf16[96,512]{1,0:T(8,128)(2,1)S(1)}, u32[]{:S(2)}, u32[]{:S(2)}) %collective-permute-start.1) | collective-permute-done | bytes 98336 | tf_op jit(solution)/shard_map/ppermute | solution.py:328
  13.6 1.3 %collective-permute-start.2 = (bf16[96,128]{1,0:T(8,128)(2,1)S(1)}, bf16[96,128]{1,0:T(8,128)(2,1)S(1)}, u32[]{:S(2)}, u32[]{:S(2)}) collective-permute-start(bf16[96,128]{1,0:T(8,128)(2,1)S(1)} %get-tuple-element.19), channel_id=1, source_target_pairs={{0,1},{1,2},{2,3},{4,5},{5,6},{6,7},{8,9},{9,10},{10,11},{12,13},{... | collective-permute-start | bytes 73736 | tf_op jit(solution)/shard_map/ppermute | solution.py:328
  14.9 1.3 %collective-permute-start.3 = (bf16[96,128]{1,0:T(8,128)(2,1)S(1)}, bf16[96,128]{1,0:T(8,128)(2,1)S(1)}, u32[]{:S(2)}, u32[]{:S(2)}) collective-permute-start(bf16[96,128]{1,0:T(8,128)(2,1)S(1)} %get-tuple-element.20), channel_id=1, source_target_pairs={{1,0},{2,1},{3,2},{5,4},{6,5},{7,6},{9,8},{10,9},{11,10},{13,12},{... | collective-permute-start | bytes 73736 | tf_op jit(solution)/shard_map/ppermute | solution.py:328
  16.7 3.0 %collective-permute-done.3.refs_4_ = bf16[96,128]{1,0:T(8,128)(2,1)S(1)} collective-permute-done((bf16[96,128]{1,0:T(8,128)(2,1)S(1)}, bf16[96,128]{1,0:T(8,128)(2,1)S(1)}, u32[]{:S(2)}, u32[]{:S(2)}) %collective-permute-start.3) | collective-permute-done | bytes 24608 | tf_op jit(solution)/shard_map/ppermute | solution.py:328
  19.7 20.4 %block.1 = f32[2496,128]{1,0:T(8,128)S(1)} custom-call(s32[4]{0:T(128)S(1)} %add_convert_fusion.flags, bf16[3,96,864]{2,1,0:T(8,128)(2,1)S(1)} %get-tuple-element.14.refs_0_, bf16[96,4096]{1,0:T(8,128)(2,1)S(1)} %get-tuple-element.15.x2_ref.refs_1_, bf16[96,128]{1,0:T(8,128)(2,1)S(1)} %get-tuple-element.18.refs_2_, ...), custom_call_target="tpu_custom_call" | custom-call | tf_op jit(solution)/shard_map/block/pallas_call | solution.py:387
  40.2 2.6 %collective-permute-start.4 = (f32[1248,128]{1,0:T(8,128)S(1)}, f32[1248,128]{1,0:T(8,128)S(1)}, u32[]{:S(2)}, u32[]{:S(2)}) collective-permute-start(f32[1248,128]{1,0:T(8,128)S(1)} %constant_dynamic-slice_fusion.3), channel_id=1, source_target_pairs={{0,1},{1,0},{2,3},{3,2},{4,5},{5,4},{6,7},{7,6},{8,9},{9,8},{10,11... | collective-permute-start | bytes 1916936 | tf_op jit(solution)/shard_map/ppermute | solution.py:296
  42.8 1.7 %collective-permute-done.4 = f32[1248,128]{1,0:T(8,128)S(1)} collective-permute-done((f32[1248,128]{1,0:T(8,128)S(1)}, f32[1248,128]{1,0:T(8,128)S(1)}, u32[]{:S(2)}, u32[]{:S(2)}) %collective-permute-start.4) | collective-permute-done | bytes 639008 | tf_op jit(solution)/shard_map/ppermute | solution.py:296
  45.0 2.5 %collective-permute-start.6 = (f32[312,128]{1,0:T(8,128)S(1)}, f32[312,128]{1,0:T(8,128)S(1)}, u32[]{:S(2)}, u32[]{:S(2)}) collective-permute-start(f32[312,128]{1,0:T(8,128)S(1)} %get-tuple-element.33), channel_id=1, source_target_pairs={{0,4},{1,5},{2,6},{3,7},{4,0},{5,1},{6,2},{7,3},{8,12},{9,13},{10,... | collective-permute-start | bytes 479240 | tf_op jit(solution)/shard_map/ppermute | solution.py:296
  47.4 1.2 %collective-permute-start.7 = (f32[312,128]{1,0:T(8,128)S(1)}, f32[312,128]{1,0:T(8,128)S(1)}, u32[]{:S(2)}, u32[]{:S(2)}) collective-permute-start(f32[312,128]{1,0:T(8,128)S(1)} %get-tuple-element.32), channel_id=1, source_target_pairs={{0,6},{1,7},{2,4},{3,5},{4,2},{5,3},{6,0},{7,1},{8,14},{9,15},{10,... | collective-permute-start | bytes 479240 | tf_op jit(solution)/shard_map/ppermute | solution.py:296
  48.6 2.5 %collective-permute-done.5 = f32[312,128]{1,0:T(8,128)S(1)} collective-permute-done((f32[312,128]{1,0:T(8,128)S(1)}, f32[312,128]{1,0:T(8,128)S(1)}, u32[]{:S(2)}, u32[]{:S(2)}) %collective-permute-start.5) | collective-permute-done | bytes 159776 | tf_op jit(solution)/shard_map/ppermute | solution.py:296
  51.1 1.2 %collective-permute-done.6 = f32[312,128]{1,0:T(8,128)S(1)} collective-permute-done((f32[312,128]{1,0:T(8,128)S(1)}, f32[312,128]{1,0:T(8,128)S(1)}, u32[]{:S(2)}, u32[]{:S(2)}) %collective-permute-start.6) | collective-permute-done | bytes 159776 | tf_op jit(solution)/shard_map/ppermute | solution.py:296
  52.3 4.1 %collective-permute-done.7 = f32[312,128]{1,0:T(8,128)S(1)} collective-permute-done((f32[312,128]{1,0:T(8,128)S(1)}, f32[312,128]{1,0:T(8,128)S(1)}, u32[]{:S(2)}, u32[]{:S(2)}) %collective-permute-start.7) | collective-permute-done | bytes 159776 | tf_op jit(solution)/shard_map/ppermute | solution.py:296
  56.5 1.6 %collective-permute-start.8 = (f32[312,128]{1,0:T(8,128)S(1)}, f32[312,128]{1,0:T(8,128)S(1)}, u32[]{:S(2)}, u32[]{:S(2)}) collective-permute-start(f32[312,128]{1,0:T(8,128)S(1)} %add_add_fusion), channel_id=1, source_target_pairs={{0,8},{1,17},{2,10},{3,19},{4,12},{5,21},{6,14},{7,23},{8,0},{9,25... | collective-permute-start | bytes 479240 | tf_op jit(solution)/shard_map/ppermute | solution.py:296
  58.1 4.4 %collective-permute-done.8 = f32[312,128]{1,0:T(8,128)S(1)} collective-permute-done((f32[312,128]{1,0:T(8,128)S(1)}, f32[312,128]{1,0:T(8,128)S(1)}, u32[]{:S(2)}, u32[]{:S(2)}) %collective-permute-start.8) | collective-permute-done | bytes 159776 | tf_op jit(solution)/shard_map/ppermute | solution.py:296
  62.5 2.2 %collective-permute-start.9 = (f32[312,128]{1,0:T(8,128)S(1)}, f32[312,128]{1,0:T(8,128)S(1)}, u32[]{:S(2)}, u32[]{:S(2)}) collective-permute-start(f32[312,128]{1,0:T(8,128)S(1)} %add.50), channel_id=1, source_target_pairs={{0,16},{1,9},{2,18},{3,11},{4,20},{5,13},{6,22},{7,15},{8,24},{9,1... | collective-permute-start | bytes 479240 | tf_op jit(solution)/shard_map/ppermute | solution.py:296
  64.7 4.2 %collective-permute-done.9 = f32[312,128]{1,0:T(8,128)S(1)} collective-permute-done((f32[312,128]{1,0:T(8,128)S(1)}, f32[312,128]{1,0:T(8,128)S(1)}, u32[]{:S(2)}, u32[]{:S(2)}) %collective-permute-start.9) | collective-permute-done | bytes 159776 | tf_op jit(solution)/shard_map/ppermute | solution.py:296
  68.9 1.4 %collective-permute-start.10 = (f32[312,128]{1,0:T(8,128)S(1)}, f32[312,128]{1,0:T(8,128)S(1)}, u32[]{:S(2)}, u32[]{:S(2)}) collective-permute-start(f32[312,128]{1,0:T(8,128)S(1)} %add.51), channel_id=1, source_target_pairs={{0,4},{1,5},{2,6},{3,7},{4,0},{5,1},{6,2},{7,3},{8,12},{9,13},{10,... | collective-permute-start | bytes 479240 | tf_op jit(solution)/shard_map/ppermute | solution.py:296
  70.8 1.7 %collective-permute-start.12 = (f32[312,128]{1,0:T(8,128)S(1)}, f32[312,128]{1,0:T(8,128)S(1)}, u32[]{:S(2)}, u32[]{:S(2)}) collective-permute-start(f32[312,128]{1,0:T(8,128)S(1)} %add.51), channel_id=1, source_target_pairs={{0,6},{1,7},{2,4},{3,5},{4,2},{5,3},{6,0},{7,1},{8,14},{9,15},{10,... | collective-permute-start | bytes 479240 | tf_op jit(solution)/shard_map/ppermute | solution.py:296
  72.5 3.5 %collective-permute-done.10 = f32[312,128]{1,0:T(8,128)S(1)} collective-permute-done((f32[312,128]{1,0:T(8,128)S(1)}, f32[312,128]{1,0:T(8,128)S(1)}, u32[]{:S(2)}, u32[]{:S(2)}) %collective-permute-start.10) | collective-permute-done | bytes 159776 | tf_op jit(solution)/shard_map/ppermute | solution.py:296
  75.9 3.6 %collective-permute-done.11 = f32[312,128]{1,0:T(8,128)S(1)} collective-permute-done((f32[312,128]{1,0:T(8,128)S(1)}, f32[312,128]{1,0:T(8,128)S(1)}, u32[]{:S(2)}, u32[]{:S(2)}) %collective-permute-start.11) | collective-permute-done | bytes 159776 | tf_op jit(solution)/shard_map/ppermute | solution.py:296
  79.7 2.1 %collective-permute-done.13 = f32[1248,128]{1,0:T(8,128)S(1)} collective-permute-done((f32[1248,128]{1,0:T(8,128)S(1)}, f32[1248,128]{1,0:T(8,128)S(1)}, u32[]{:S(2)}, u32[]{:S(2)}) %collective-permute-start.13) | collective-permute-done | bytes 639008 | tf_op jit(solution)/shard_map/ppermute | solution.py:296
  82.0 1.3 %unpack.1 = (f32[864,96]{1,0:T(8,128)}, f32[864,96]{1,0:T(8,128)}, f32[96,1536]{1,0:T(8,128)}) custom-call(f32[2496,128]{1,0:T(8,128)S(1)} %pad_maximum_fusion.v_ref), custom_call_target="tpu_custom_call" | custom-call | tf_op jit(solution)/shard_map/unpack/pallas_call | solution.py:410
  (29 shorter events, 4.3 us)
Async XLA Ops:
  0.6 15.6 %copy-start = (bf16[96,1536]{1,0:T(8,128)(2,1)S(1)}, bf16[96,1536]{1,0:T(8,128)(2,1)}, u32[]{:S(2)}) copy-start(bf16[96,1536]{1,0:T(8,128)(2,1)} %refs_8_.1) | copy-start | bytes 884740
  0.6 1.2 %copy-start.1 = (bf16[96,16,256]{2,1,0:T(8,128)(2,1)S(1)}, bf16[96,16,256]{2,1,0:T(8,128)(2,1)}, u32[]{:S(2)}) copy-start(bf16[96,16,256]{2,1,0:T(8,128)(2,1)} %x_ref.1) | copy-start | bytes 2359300
  1.8 14.4 %copy-start.2 = (bf16[9,96,96]{2,1,0:T(8,128)(2,1)S(1)}, bf16[9,96,96]{2,1,0:T(8,128)(2,1)}, u32[]{:S(2)}) copy-start(bf16[9,96,96]{2,1,0:T(8,128)(2,1)} %cin_ref.1) | copy-start | bytes 497668
  1.8 14.4 %copy-start.3 = (bf16[9,96,96]{2,1,0:T(8,128)(2,1)S(1)}, bf16[9,96,96]{2,1,0:T(8,128)(2,1)}, u32[]{:S(2)}) copy-start(bf16[9,96,96]{2,1,0:T(8,128)(2,1)} %cout_ref.1) | copy-start | bytes 497668
  2.0 7.0 %collective-permute-start = (bf16[96,512]{1,0:T(8,128)(2,1)S(1)}, bf16[96,512]{1,0:T(8,128)(2,1)S(1)}, u32[]{:S(2)}, u32[]{:S(2)}) collective-permute-start(bf16[96,512]{1,0:T(8,128)(2,1)S(1)} %get-tuple-element.16), channel_id=1, source_target_pairs={{0,4},{4,8},{8,12},{12,16},{16,20},{20,24},{24,28},{1,5},{5,9},{9,... | collective-permute-start | bytes 294920 | tf_op jit(solution)/shard_map/ppermute | solution.py:328
  6.9 6.5 %collective-permute-start.1 = (bf16[96,512]{1,0:T(8,128)(2,1)S(1)}, bf16[96,512]{1,0:T(8,128)(2,1)S(1)}, u32[]{:S(2)}, u32[]{:S(2)}) collective-permute-start(bf16[96,512]{1,0:T(8,128)(2,1)S(1)} %get-tuple-element.17), channel_id=1, source_target_pairs={{4,0},{8,4},{12,8},{16,12},{20,16},{24,20},{28,24},{5,1},{9,5},{13... | collective-permute-start | bytes 294920 | tf_op jit(solution)/shard_map/ppermute | solution.py:328
  13.6 3.1 %collective-permute-start.2 = (bf16[96,128]{1,0:T(8,128)(2,1)S(1)}, bf16[96,128]{1,0:T(8,128)(2,1)S(1)}, u32[]{:S(2)}, u32[]{:S(2)}) collective-permute-start(bf16[96,128]{1,0:T(8,128)(2,1)S(1)} %get-tuple-element.19), channel_id=1, source_target_pairs={{0,1},{1,2},{2,3},{4,5},{5,6},{6,7},{8,9},{9,10},{10,11},{12,13},{... | collective-permute-start | bytes 73736 | tf_op jit(solution)/shard_map/ppermute | solution.py:328
  14.9 4.8 %collective-permute-start.3 = (bf16[96,128]{1,0:T(8,128)(2,1)S(1)}, bf16[96,128]{1,0:T(8,128)(2,1)S(1)}, u32[]{:S(2)}, u32[]{:S(2)}) collective-permute-start(bf16[96,128]{1,0:T(8,128)(2,1)S(1)} %get-tuple-element.20), channel_id=1, source_target_pairs={{1,0},{2,1},{3,2},{5,4},{6,5},{7,6},{9,8},{10,9},{11,10},{13,12},{... | collective-permute-start | bytes 73736 | tf_op jit(solution)/shard_map/ppermute | solution.py:328
  40.2 4.3 %collective-permute-start.4 = (f32[1248,128]{1,0:T(8,128)S(1)}, f32[1248,128]{1,0:T(8,128)S(1)}, u32[]{:S(2)}, u32[]{:S(2)}) collective-permute-start(f32[1248,128]{1,0:T(8,128)S(1)} %constant_dynamic-slice_fusion.3), channel_id=1, source_target_pairs={{0,1},{1,0},{2,3},{3,2},{4,5},{5,4},{6,7},{7,6},{8,9},{9,8},{10,11... | collective-permute-start | bytes 1916936 | tf_op jit(solution)/shard_map/ppermute | solution.py:296
  44.6 6.5 %collective-permute-start.5 = (f32[312,128]{1,0:T(8,128)S(1)}, f32[312,128]{1,0:T(8,128)S(1)}, u32[]{:S(2)}, u32[]{:S(2)}) collective-permute-start(f32[312,128]{1,0:T(8,128)S(1)} %get-tuple-element.31), channel_id=1, source_target_pairs={{0,2},{1,3},{2,0},{3,1},{4,6},{5,7},{6,4},{7,5},{8,10},{9,11},{10,... | collective-permute-start | bytes 479240 | tf_op jit(solution)/shard_map/ppermute | solution.py:296
  45.0 7.3 %collective-permute-start.6 = (f32[312,128]{1,0:T(8,128)S(1)}, f32[312,128]{1,0:T(8,128)S(1)}, u32[]{:S(2)}, u32[]{:S(2)}) collective-permute-start(f32[312,128]{1,0:T(8,128)S(1)} %get-tuple-element.33), channel_id=1, source_target_pairs={{0,4},{1,5},{2,6},{3,7},{4,0},{5,1},{6,2},{7,3},{8,12},{9,13},{10,... | collective-permute-start | bytes 479240 | tf_op jit(solution)/shard_map/ppermute | solution.py:296
  47.4 9.0 %collective-permute-start.7 = (f32[312,128]{1,0:T(8,128)S(1)}, f32[312,128]{1,0:T(8,128)S(1)}, u32[]{:S(2)}, u32[]{:S(2)}) collective-permute-start(f32[312,128]{1,0:T(8,128)S(1)} %get-tuple-element.32), channel_id=1, source_target_pairs={{0,6},{1,7},{2,4},{3,5},{4,2},{5,3},{6,0},{7,1},{8,14},{9,15},{10,... | collective-permute-start | bytes 479240 | tf_op jit(solution)/shard_map/ppermute | solution.py:296
  56.5 6.0 %collective-permute-start.8 = (f32[312,128]{1,0:T(8,128)S(1)}, f32[312,128]{1,0:T(8,128)S(1)}, u32[]{:S(2)}, u32[]{:S(2)}) collective-permute-start(f32[312,128]{1,0:T(8,128)S(1)} %add_add_fusion), channel_id=1, source_target_pairs={{0,8},{1,17},{2,10},{3,19},{4,12},{5,21},{6,14},{7,23},{8,0},{9,25... | collective-permute-start | bytes 479240 | tf_op jit(solution)/shard_map/ppermute | solution.py:296
  62.5 6.4 %collective-permute-start.9 = (f32[312,128]{1,0:T(8,128)S(1)}, f32[312,128]{1,0:T(8,128)S(1)}, u32[]{:S(2)}, u32[]{:S(2)}) collective-permute-start(f32[312,128]{1,0:T(8,128)S(1)} %add.50), channel_id=1, source_target_pairs={{0,16},{1,9},{2,18},{3,11},{4,20},{5,13},{6,22},{7,15},{8,24},{9,1... | collective-permute-start | bytes 479240 | tf_op jit(solution)/shard_map/ppermute | solution.py:296
  68.9 7.0 %collective-permute-start.10 = (f32[312,128]{1,0:T(8,128)S(1)}, f32[312,128]{1,0:T(8,128)S(1)}, u32[]{:S(2)}, u32[]{:S(2)}) collective-permute-start(f32[312,128]{1,0:T(8,128)S(1)} %add.51), channel_id=1, source_target_pairs={{0,4},{1,5},{2,6},{3,7},{4,0},{5,1},{6,2},{7,3},{8,12},{9,13},{10,... | collective-permute-start | bytes 479240 | tf_op jit(solution)/shard_map/ppermute | solution.py:296
  70.3 9.2 %collective-permute-start.11 = (f32[312,128]{1,0:T(8,128)S(1)}, f32[312,128]{1,0:T(8,128)S(1)}, u32[]{:S(2)}, u32[]{:S(2)}) collective-permute-start(f32[312,128]{1,0:T(8,128)S(1)} %add.51), channel_id=1, source_target_pairs={{0,2},{1,3},{2,0},{3,1},{4,6},{5,7},{6,4},{7,5},{8,10},{9,11},{10,... | collective-permute-start | bytes 479240 | tf_op jit(solution)/shard_map/ppermute | solution.py:296
  70.8 8.7 %collective-permute-start.12 = (f32[312,128]{1,0:T(8,128)S(1)}, f32[312,128]{1,0:T(8,128)S(1)}, u32[]{:S(2)}, u32[]{:S(2)}) collective-permute-start(f32[312,128]{1,0:T(8,128)S(1)} %add.51), channel_id=1, source_target_pairs={{0,6},{1,7},{2,4},{3,5},{4,2},{5,3},{6,0},{7,1},{8,14},{9,15},{10,... | collective-permute-start | bytes 479240 | tf_op jit(solution)/shard_map/ppermute | solution.py:296
  79.6 2.1 %collective-permute-start.13 = (f32[1248,128]{1,0:T(8,128)S(1)}, f32[1248,128]{1,0:T(8,128)S(1)}, u32[]{:S(2)}, u32[]{:S(2)}) collective-permute-start(f32[1248,128]{1,0:T(8,128)S(1)} %pad_maximum_fusion.1), channel_id=1, source_target_pairs={{0,1},{1,0},{2,3},{3,2},{4,5},{5,4},{6,7},{7,6},{8,9},{9,8},{10,11... | collective-permute-start | bytes 1916936 | tf_op jit(solution)/shard_map/ppermute | solution.py:296
